TPU v7x, 128 devices: a whole 4x4x4 slice. The times are simulated.
128 devices in a mesh: dp: 4 (over x_hi, core), wide: 32 (over y, x_lo, z).
Axes of the slice: x: 4 (x_hi: 2, x_lo: 2; x = x_hi * 2 + x_lo), y: 4, z: 4, core: 2. Of those that a mesh axis runs over, the one named last changes fastest.
Arguments:
- hidden: bfloat16 [16384, 768], P(('dp', 'wide')), may hold values from -6 to 6
- cotangent: bfloat16 [16384, 768], P(('dp', 'wide')), may hold values from -6 to 6
- routes: int32 [16384, 1], P(('dp', 'wide')), may hold values from 0 to 31
- seg_lengths: int32 [4, 16], P('dp'), may hold values from 1 to 2048, 4096 in all within a row
- gain_mix: float32 [768], replicated, may hold values from 0.5 to 1.5
- in_x: bfloat16 [768, 1536], P(None, 'wide'), may hold values from -0.21875 to 0.21875
- in_z: bfloat16 [768, 1536], P(None, 'wide'), may hold values from -0.21875 to 0.21875
- conv_w: float32 [4, 1536], P(None, 'wide'), may hold values from -3 to 3
- conv_b: float32 [1536], P('wide'), may hold values from -3 to 3
- x_proj: bfloat16 [1536, 80], P('wide'), may hold values from -0.15625 to 0.15625
- dt_proj: bfloat16 [48, 1536], P(None, 'wide'), may hold values from -0.875 to 0.875
- dt_bias: float32 [1536], P('wide'), may hold values from -6.2 to -2
- a_log: float32 [16, 1536], P(None, 'wide'), may hold values from -2.5 to 2.77
- skip_d: float32 [1536], P('wide'), may hold values from 0.5 to 1.5
- out_proj: bfloat16 [1536, 768], P('wide'), may hold values from -0.15625 to 0.15625
- gain_moe: float32 [768], replicated, may hold values from 0.5 to 1.5
- router: bfloat16 [768, 32], replicated, may hold values from -0.109375 to 0.109375
- w_gate: bfloat16 [32, 768, 3072], P('wide', None, 'dp'), may hold values from -0.21875 to 0.21875
- w_up: bfloat16 [32, 768, 3072], P('wide', None, 'dp'), may hold values from -0.21875 to 0.21875
- w_down: bfloat16 [32, 3072, 768], P('wide', 'dp'), may hold values from -6 to 6
Outputs:
- output: bfloat16 [16384, 768], P(('dp', 'wide'))
- grad_hidden: float32 [16384, 768], P(('dp', 'wide'))
- grad_gain_mix: float32 [768], replicated
- grad_in_x: float32 [768, 1536], P(None, 'wide')
- grad_in_z: float32 [768, 1536], P(None, 'wide')
- grad_conv_w: float32 [4, 1536], P(None, 'wide')
- grad_conv_b: float32 [1536], P('wide')
- grad_x_proj: float32 [1536, 80], P('wide')
- grad_dt_proj: float32 [48, 1536], P(None, 'wide')
- grad_dt_bias: float32 [1536], P('wide')
- grad_a_log: float32 [16, 1536], P(None, 'wide')
- grad_skip_d: float32 [1536], P('wide')
- grad_out_proj: float32 [1536, 768], P('wide')
- grad_gain_moe: float32 [768], replicated
- grad_router: float32 [768, 32], replicated
- grad_w_gate: float32 [32, 768, 3072], P('wide', None, 'dp')
- grad_w_up: float32 [32, 768, 3072], P('wide', None, 'dp')
- grad_w_down: float32 [32, 3072, 768], P('wide', 'dp')
Inputs may be any that keep to these rules, and one draw needn't show every extreme that they name: `seg_lengths`: each row lists in order the lengths of its segments, which fill its 4096 positions; the last entry is the padding at the row's end; the largest entry of every row is 2048.
All inputs are finite; a program needn't handle non-finite values.
Results may differ from a plain program's by a relative error of at most 0.028.
Values may be sent and summed in bfloat16 or wider, within the bound.
No kernel may reach another device: no remote copies, remote signals or barrier semaphores. Data moves between devices by JAX's collectives and lax.ppermute only.
A program may use at most 128 MiB of HBM per device.

v0:
```python
from functools import partial

import jax
import jax.numpy as jnp
from jax import lax
from jax.experimental import pallas as pl
from jax.experimental.pallas import tpu as pltpu
from jax.sharding import PartitionSpec as P

f32 = jnp.float32
bf16 = jnp.bfloat16
KC = 4
SUB = 8
CAP = 5
STOP = 1e6
LOG2E = 1.4426950408889634
LN2 = 0.6931471805599453
epsilon = 1e-05
VMEM_LIMIT = 56 * 1024 * 1024


def dot_nn(left, right):
    return lax.dot_general(left, right, (((1,), (0,)), ((), ())), preferred_element_type=f32)


def dot_nt(left, right):
    return lax.dot_general(left, right, (((1,), (1,)), ((), ())), preferred_element_type=f32)


def dot_tn(left, right):
    return lax.dot_general(left, right, (((0,), (0,)), ((), ())), preferred_element_type=f32)


class Moves:
    def __init__(self):
        self.arriving = {}
        self.leaving = {}
        self.started = []

    def need(self, *refs):
        for ref in refs:
            copy = self.arriving.pop(id(ref), None)
            if copy is not None:
                copy.wait()

    def done(self, *refs):
        for ref in refs:
            copy = self.leaving.pop(id(ref), None)
            if copy is not None:
                copy.start()
                self.started.append(copy)


def call(
    kernel, out_shapes, scratch, args, smem=0, late=(), early=(), lanes=None, limit=VMEM_LIMIT
):
    lanes = lanes or {}
    vmem = pl.BlockSpec(memory_space=pltpu.VMEM)
    hbm = pl.BlockSpec(memory_space=pl.ANY)
    specs = [pl.BlockSpec(memory_space=pltpu.SMEM)] * smem
    specs += [hbm if i in late else vmem for i in range(smem, len(args))]
    buffers = []
    for i in late:
        dims = (args[i].shape[0], lanes[i].size) if i in lanes else args[i].shape
        buffers.append(pltpu.VMEM(dims, args[i].dtype))
    buffers += [pltpu.VMEM(out_shapes[i].shape, out_shapes[i].dtype) for i in early]
    moving = len(buffers)
    extra = buffers + [pltpu.SemaphoreType.DMA((moving,))] if moving else []

    def staged(*refs):
        refs = list(refs)
        own = refs[len(refs) - moving - 1 : -1]
        semaphores = refs[-1]
        refs = refs[: len(refs) - moving - 1]
        moves = Moves()
        for k, i in enumerate(late):
            source = refs[i].at[:, lanes[i]] if i in lanes else refs[i]
            copy = pltpu.make_async_copy(source, own[k], semaphores.at[k])
            copy.start()
            refs[i] = own[k]
            moves.arriving[id(own[k])] = copy
        for k, i in enumerate(early, len(late)):
            at = len(args) + i
            moves.leaving[id(own[k])] = pltpu.make_async_copy(own[k], refs[at], semaphores.at[k])
            refs[at] = own[k]
        kernel(moves, *refs)
        moves.need(*own)
        moves.done(*own)
        for copy in moves.started:
            copy.wait()

    return pl.pallas_call(
        staged if moving else kernel,
        out_shape=out_shapes,
        in_specs=specs,
        out_specs=[hbm if i in early else vmem for i in range(len(out_shapes))],
        scratch_shapes=list(scratch) + extra,
        compiler_params=pltpu.CompilerParams(vmem_limit_bytes=limit),
    )(*args)


def shape(dims, dtype=f32):
    return jax.ShapeDtypeStruct(dims, dtype)


def group_of(di):
    return 256 if di % 256 == 0 else 128


def sublane_iota(width):
    return lax.broadcasted_iota(jnp.int32, (SUB, width), 0)


def from_before(block, first):
    row = sublane_iota(block.shape[1])
    return jnp.where(row == 0, jnp.broadcast_to(first, block.shape), pltpu.roll(block, 1, 0))


def from_after(block, last):
    row = sublane_iota(block.shape[1])
    return jnp.where(
        row == SUB - 1, jnp.broadcast_to(last, block.shape), pltpu.roll(block, SUB - 1, 0)
    )


def spread_columns(small, first, count, out):
    steps = small.shape[0] // SUB
    for j in range(steps):
        block = small[j * SUB : (j + 1) * SUB, :]
        for n in range(count):
            out[j * count + n] = jnp.broadcast_to(block[:, first + n : first + n + 1], (SUB, 128))


def prefix_states(decay, state):
    row = sublane_iota(state.shape[1])
    for shift in (1, 2, 4):
        inside = row >= shift
        state = state + decay * jnp.where(inside, pltpu.roll(state, shift, 0), 0.0)
        decay = decay * jnp.where(inside, pltpu.roll(decay, shift, 0), 1.0)
    return state


def suffix_states(decay, state):
    row = sublane_iota(state.shape[1])
    for shift in (1, 2, 4):
        inside = row < SUB - shift
        state = state + decay * jnp.where(inside, pltpu.roll(state, SUB - shift, 0), 0.0)
        decay = decay * jnp.where(inside, pltpu.roll(decay, SUB - shift, 0), 1.0)
    return state


def prefix_sum(values):
    row = sublane_iota(values.shape[1])
    for shift in (1, 2, 4):
        values = values + jnp.where(row >= shift, pltpu.roll(values, shift, 0), 0.0)
    return values


def suffix_sum(values):
    row = sublane_iota(values.shape[1])
    for shift in (1, 2, 4):
        values = values + jnp.where(row < SUB - shift, pltpu.roll(values, SUB - shift, 0), 0.0)
    return values


def one_hot(dims, offset):
    row = lax.broadcasted_iota(jnp.int32, dims, 0)
    column = lax.broadcasted_iota(jnp.int32, dims, 1)
    return (row + offset == column).astype(bf16)


def pack_gate_kernel(core, in_z, out_proj, gate_o):
    half = in_z.shape[1] // 2
    start = pl.multiple_of(core[0] * half, 128)
    gate_o[:, :half] = in_z[:, pl.ds(start, half)]
    gate_o[:, half:] = out_proj[:, pl.ds(start, half)]


def pack_kernel(
    core, in_x, x_proj, dt_proj, conv_w, conv_b, dt_bias, skip_d, a_log, out, *, places
):
    width, model = in_x.shape
    half = model // 2
    here = core[0]
    mine = in_x[:, pl.ds(pl.multiple_of(here * half, 128), half)]
    narrow = x_proj.shape[1]
    steps = dot_nn(x_proj[...], one_hot((narrow, 128), 0)) + dot_tn(
        dt_proj[...], one_hot((dt_proj.shape[0], 128), 128 - dt_proj.shape[0])
    )
    values = jnp.concatenate(
        [
            conv_w[...],
            conv_b[...].reshape(1, width),
            dt_bias[...].reshape(1, width),
            skip_d[...].reshape(1, width),
            jnp.zeros((1, width), f32),
            a_log[...],
        ],
        axis=0,
    )
    top = values.astype(bf16)
    left = values - top.astype(f32)
    mid = left.astype(bf16)
    low = (left - mid.astype(f32)).astype(bf16)
    count = values.shape[0]
    extra = dot_tn(top, one_hot((count, 128), 0))
    extra = extra + dot_tn(mid, one_hot((count, 128), count))
    extra = extra + dot_tn(low, one_hot((count, 128), 2 * count))
    rest = jnp.where(here == 0, steps, extra).astype(bf16)
    for place in range(places):
        out[place * width : (place + 1) * width, :half] = mine
        out[place * width : (place + 1) * width, half:] = rest


def prepare_kernel(
    base, lengths, hidden, cot, route, gain, nrm_o, tail_o, hid_o, cot_o, route_o, aux_o
):
    rows = hidden.shape[0]
    steps_in = rows // SUB
    row = lax.broadcasted_iota(jnp.int32, (rows, rows), 0)
    column = lax.broadcasted_iota(jnp.int32, (rows, rows), 1)
    in_order = (row % SUB) * steps_in + row // SUB == column
    order = in_order.astype(bf16)
    hid = dot_nn(order, hidden[...])
    hid_o[...] = hid.astype(bf16)
    cot_o[...] = dot_nn(order, cot[...]).astype(bf16)
    ours = jnp.where(in_order, jnp.broadcast_to(route[...], (rows, rows)), 0)
    route_o[...] = jnp.sum(ours, axis=1, keepdims=True)
    scale = lax.rsqrt(jnp.mean(hid * hid, axis=1, keepdims=True) + epsilon)
    normed = (hid * scale * gain[...].reshape(1, -1)).astype(bf16)
    nrm_o[...] = normed
    tail_row = lax.broadcasted_iota(jnp.int32, (16, rows), 0)
    tail_column = lax.broadcasted_iota(jnp.int32, (16, rows), 1)
    picked = (tail_column == rows - 1 - (KC - 2 - tail_row) * SUB) & (tail_row < KC - 1)
    tail = dot_nn(picked.astype(bf16), normed)
    tail_row = tail_row - SUB
    picked = (tail_column == rows - 1 - (KC - 2 - tail_row) * SUB) & (tail_row < KC - 1)
    picked = picked & (tail_row >= 0)
    tail_o[...] = (tail + dot_nn(picked.astype(bf16), hid.astype(bf16))).astype(bf16)

    def layout(position, lane):
        back = position - (lane + 1)
        segment = jnp.zeros_like(position)
        segment_back = jnp.zeros_like(position)
        reset = position == 0
        end = jnp.int32(0)
        for j in range(lengths.shape[1] - 1):
            end = end + lengths[0, j]
            segment = segment + (position >= end).astype(jnp.int32)
            segment_back = segment_back + (back >= end).astype(jnp.int32)
            reset = reset | (position == end)
        same = (back >= 0) & (segment == segment_back)
        live = position < end
        picked = jnp.where(lane == KC - 1, live.astype(f32), reset.astype(f32))
        return jnp.where(lane < KC - 1, same.astype(f32), picked)

    at = lax.broadcasted_iota(jnp.int32, (rows, 128), 0)
    lane = lax.broadcasted_iota(jnp.int32, (rows, 128), 1)
    aux_o[...] = layout(base[0] + (at % SUB) * steps_in + at // SUB, lane)


def front_kernel(
    moves, core, nrm_in, halo_in, wm, wo, aux, ext_o, pre_o, steps_o, sig_o, small_o, x_o, tpre_o, tsuf_o,
    state_o, par_o, xd_o, sd_s, q_s, bw_s, nrm_s, sum_s, *, rank, count
):
    rows, di = pre_o.shape
    half = wo.shape[1] - 128
    steps_in = rows // SUB
    gs = group_of(di)
    low = core[0] == 0
    nrm_s[0, :rows] = jnp.where(low, nrm_in[:, :half], nrm_in[:, half:])
    nrm_s[1, :rows] = jnp.where(low, nrm_in[:, half:], nrm_in[:, :half])
    nrm_s[0, rows:] = jnp.where(low, halo_in[:, :half], halo_in[:, half:])
    nrm_s[1, rows:] = jnp.where(low, halo_in[:, half:], halo_in[:, :half])
    small_o[...] = jnp.zeros_like(small_o)
    moves.need(wm, wo)
    par = par_o
    total_rows = par_o.shape[0]

    def unpack(g, _):
        lanes = pl.ds(pl.multiple_of(g * 128, 128), 128)
        mine = wm[lanes, half:]
        other = wo[lanes, half:]
        xd_o[lanes, :] = jnp.where(low, mine, other)
        turned = jnp.where(low, other, mine).astype(f32).T
        par_o[:, lanes] = (
            turned[:total_rows, :]
            + turned[total_rows : 2 * total_rows, :]
            + turned[2 * total_rows : 3 * total_rows, :]
        )
        return 0

    lax.fori_loop(0, di // 128, unpack, 0)

    def project(g, _):
        lanes = pl.ds(pl.multiple_of(g * gs, gs), gs)
        inner = dot_nt(nrm_s[0], wm[lanes, :half]) + dot_nt(nrm_s[1], wo[lanes, :half])
        for back in range(1, KC):
            block = inner[rows - back * SUB : rows - (back - 1) * SUB, :]
            halo = inner[rows + KC - 1 - back : rows + KC - back, :]
            ext_o[(KC - 1 - back) * SUB : (KC - back) * SUB, lanes] = from_before(block, halo)
        ext_o[(KC - 1) * SUB :, lanes] = inner[:rows, :]
        total = par[KC : KC + 1, lanes] + par[KC - 1 : KC, lanes] * inner[:rows, :]
        for back in range(1, KC):
            shifted = ext_o[(KC - 1 - back) * SUB : (KC - 1 - back) * SUB + rows, lanes]
            total = total + par[KC - 1 - back : KC - back, lanes] * shifted * aux[:, back - 1 : back]
        pre_o[:, lanes] = total
        act = total * jax.nn.sigmoid(total)
        q_s[:, lanes] = act
        small_o[...] += dot_nn(act.astype(bf16), xd_o[lanes, :])
        return 0

    lax.fori_loop(0, di // gs, project, 0)
    moves.done(ext_o, pre_o, par_o, xd_o)
    small = small_o[...]
    lane = lax.broadcasted_iota(jnp.int32, small.shape, 1)
    step_low = jnp.where(lane >= 128 - rank, pltpu.roll(small, 128 - rank, 1), 0.0).astype(bf16)
    spread_columns(small, rank, count, bw_s)

    def stepping(g, _):
        lanes = pl.ds(pl.multiple_of(g * gs, gs), gs)
        step_pre = dot_nt(step_low, xd_o[lanes, :]) + par[KC + 1 : KC + 2, lanes]
        small_exp = jnp.exp(-jnp.abs(step_pre))
        steps = jnp.maximum(step_pre, 0.0) + jnp.log1p(small_exp)
        steps_o[:, lanes] = steps
        sig_o[:, lanes] = jax.nn.sigmoid(step_pre)
        q_s[:, lanes] = q_s[:, lanes] * steps
        sd_s[:, lanes] = jnp.where(aux[:, 4:5] > 0.5, STOP, steps)
        return 0

    lax.fori_loop(0, di // gs, stepping, 0)
    moves.done(steps_o, sig_o, sd_s, q_s)

    def chunk(g, _):
        lanes = pl.ds(pl.multiple_of(g * 128, 128), 128)
        rates = [
            jnp.broadcast_to(-LOG2E * jnp.exp(par[8 + n : 9 + n, lanes]), (SUB, 128))
            for n in range(count)
        ]

        def step(j, carry):
            states, total = carry
            at = pl.ds(pl.multiple_of(j * SUB, SUB), SUB)
            sd = sd_s[at, lanes]
            q = q_s[at, lanes]
            states = tuple(
                jnp.exp2(sd * rates[n]) * states[n] + q * bw_s[j * count + n] for n in range(count)
            )
            return (states, total + sd)

        zero = jnp.zeros((SUB, 128), f32)
        states, total = lax.fori_loop(0, steps_in, step, ((zero,) * count, zero), unroll=8)
        row = sublane_iota(128)
        ahead = prefix_sum(total)
        behind = suffix_sum(total)
        tpre_o[:, lanes] = jnp.where(row == 0, 0.0, pltpu.roll(ahead, 1, 0))
        tsuf_o[:, lanes] = jnp.where(row == SUB - 1, 0.0, pltpu.roll(behind, SUB - 1, 0))
        last = []
        for n in range(count):
            joined = prefix_states(jnp.exp2(rates[n] * total), states[n])
            x_o[n, :, lanes] = jnp.where(row == 0, 0.0, pltpu.roll(joined, 1, 0))
            last.append(joined[SUB - 1 : SUB, :])
        sum_s[pl.ds(g, 1), :] = ahead[SUB - 1 : SUB, :]
        to_copies(state_o, jnp.concatenate(last, axis=0).astype(bf16), lanes)
        return 0

    sum_s[...] = jnp.zeros_like(sum_s)
    lax.fori_loop(0, di // 128, chunk, 0)
    sums = sum_s[...]
    top = sums.astype(bf16)
    left = (sums - top.astype(f32)).astype(bf16)
    to_copies(state_o, top, slice(di, di + 128))
    to_copies(state_o, left, slice(di + 128, di + 256))


def to_copies(out, values, lanes):
    count = values.shape[0]
    for place in range(out.shape[0] // count):
        out[place * count : (place + 1) * count, lanes] = values


def negative_rates(par, out):
    out[...] = -LOG2E * jnp.exp(par[8:, :])


def group_kernel(arrived, out, state_s, sum_s, *, di, count, reverse):
    members = arrived.shape[0] // count
    rest = arrived.shape[1] - di - 256
    copies = out.shape[0] // count
    state_s[...] = jnp.zeros_like(state_s)
    total = jnp.zeros((count, 128), f32)
    for place in range(members - 1, -1, -1) if reverse else range(members):
        block = slice(place * count, (place + 1) * count)
        sums = arrived[block, di : di + 128].astype(f32)
        sums = sums + arrived[block, di + 128 : di + 256].astype(f32)
        total = total + sums
        carry_step(sums, arrived[block, :di], sum_s, state_s)
    joined = state_s[...].astype(bf16)
    top = total.astype(bf16)
    left = (total - top.astype(f32)).astype(bf16)
    for copy in range(copies):
        block = slice(copy * count, (copy + 1) * count)
        out[block, :di] = joined
        out[block, di : di + 128] = top
        out[block, di + 128 : di + 256] = left
    if rest:
        extra = jnp.zeros((count, rest), f32)
        for place in range(members):
            extra = extra + arrived[place * count : (place + 1) * count, di + 256 :].astype(f32)
        gap = jnp.zeros((count - 2, rest), f32)
        for copy in range(copies):
            rows = jnp.concatenate([extra[2 * copy : 2 * copy + 2, :], gap], axis=0)
            out[copy * count : (copy + 1) * count, di + 256 :] = rows.astype(bf16)


def forward_group_kernel(arrived, par, out, state_s, rate_s, *, di, count):
    negative_rates(par, rate_s)
    group_kernel(arrived, out, state_s, rate_s, di=di, count=count, reverse=False)


def backward_group_kernel(arrived, par, out, state_s, rate_s, *, di, count):
    negative_rates(par, rate_s)
    group_kernel(arrived, out, state_s, rate_s, di=di, count=count, reverse=True)


def step_sums(arrived, block, di):
    return arrived[block, di : di + 128].astype(f32) + arrived[block, di + 128 : di + 256].astype(
        f32
    )


def carry_step(decay_sums, arrived, rate_s, state_s):
    for g in range(state_s.shape[1] // 128):
        lanes = slice(g * 128, (g + 1) * 128)
        decay = jnp.exp2(rate_s[:, lanes] * decay_sums[g : g + 1, :])
        state_s[:, lanes] = decay * state_s[:, lanes] + arrived[:, lanes].astype(f32)


def gate_kernel(moves, core, nrm, zm, zo, gate_z_o, nrm_s):
    rows, di = gate_z_o.shape
    half = zm.shape[1]
    gs = group_of(di)
    low = core[0] == 0
    nrm_s[0] = jnp.where(low, nrm[:, :half], nrm[:, half:])
    nrm_s[1] = jnp.where(low, nrm[:, half:], nrm[:, :half])
    moves.need(zm, zo)

    def project(g, _):
        lanes = pl.ds(pl.multiple_of(g * gs, gs), gs)
        gate_z_o[:, lanes] = dot_nt(nrm_s[0], zm[lanes, :]) + dot_nt(nrm_s[1], zo[lanes, :])
        return 0

    lax.fori_loop(0, di // gs, project, 0)


def middle_kernel(
    moves, core, place, om, oo, par, aux, pre, sd, q, x_in, small, arrived, near, tpre, hid, cot,
    route, gain, router, gate_z, scan_o, send_o, middle_o, ntwo_o, chance_o, meta_o, hot_o,
    entry_o, bw_s, cw_s, rate_s, *, rank, count, experts, stride, capacity, shift
):
    rows, di = pre.shape
    half = om.shape[1]
    steps_in = rows // SUB
    gs = group_of(di)
    low = core[0] == 0
    spread_columns(small[...], rank, count, bw_s)
    spread_columns(small[...], rank + count, count, cw_s)
    negative_rates(par, rate_s)
    moves.need(arrived, near)
    entry_o[...] = jnp.zeros_like(entry_o)
    members = near.shape[0] // count

    def before_here(there, _):
        block = pl.ds(pl.multiple_of(there * count, count), count)
        carry_step(step_sums(arrived, block, di), arrived[block, :di], rate_s, entry_o)
        return 0

    def just_before(there, _):
        block = pl.ds(pl.multiple_of(there * count, count), count)
        carry_step(step_sums(near, block, di), near[block, :di], rate_s, entry_o)
        return 0

    lax.fori_loop(0, place[0] // members, before_here, 0)
    lax.fori_loop(0, place[0] % members, just_before, 0)
    moves.done(entry_o)
    moves.need(x_in, sd, q)

    def scan(g, _):
        lanes = pl.ds(pl.multiple_of(g * 128, 128), 128)
        rates = [jnp.broadcast_to(rate_s[n : n + 1, lanes], (SUB, 128)) for n in range(count)]
        before = tpre[:, lanes]
        first = tuple(
            x_in[n, :, lanes] + jnp.exp2(rates[n] * before) * entry_o[n : n + 1, lanes]
            for n in range(count)
        )
        def step(j, states):
            at = pl.ds(pl.multiple_of(j * SUB, SUB), SUB)
            sd_here = sd[at, lanes]
            q_here = q[at, lanes]
            total = jnp.zeros((SUB, 128), f32)
            fresh = []
            for n in range(count):
                state = jnp.exp2(sd_here * rates[n]) * states[n] + q_here * bw_s[j * count + n]
                total = total + state * cw_s[j * count + n]
                fresh.append(state)
            scan_o[at, lanes] = total
            return tuple(fresh)

        lax.fori_loop(0, steps_in, step, first, unroll=8)
        return 0

    lax.fori_loop(0, di // 128, scan, 0)

    def gating(g, carry):
        mine, other = carry
        lanes = pl.ds(pl.multiple_of(g * gs, gs), gs)
        z = gate_z[:, lanes]
        pre_here = pre[:, lanes]
        scanned = scan_o[:, lanes] + par[KC + 2 : KC + 3, lanes] * (
            pre_here * jax.nn.sigmoid(pre_here)
        )
        scan_o[:, lanes] = scanned
        gated = (scanned * (z * jax.nn.sigmoid(z)) * aux[:, 3:4]).astype(bf16)
        return (mine + dot_nn(gated, om[lanes, :]), other + dot_nn(gated, oo[lanes, :]))

    zero = jnp.zeros((rows, half), f32)
    moves.need(pre, gate_z, om, oo)
    mine, other = lax.fori_loop(0, di // gs, gating, (zero, zero))
    moves.done(scan_o)
    mixed = jnp.concatenate([jnp.where(low, mine, other), jnp.where(low, other, mine)], axis=1)
    middle = hid[...].astype(f32) + mixed
    middle_o[...] = middle
    scale = lax.rsqrt(jnp.mean(middle * middle, axis=1, keepdims=True) + epsilon)
    ntwo = (middle * scale * gain[...].reshape(1, -1)).astype(bf16)
    ntwo_o[...] = ntwo
    logits = dot_nt(ntwo, router[...])
    top = jnp.max(logits, axis=1, keepdims=True)
    raised = jnp.exp(logits - top)
    chances = raised / jnp.sum(raised, axis=1, keepdims=True)
    chance_o[...] = chances
    lane = lax.broadcasted_iota(jnp.int32, (rows, experts), 1)
    chosen = route[...] == lane
    chosen_f = chosen.astype(f32)
    gate = jnp.sum(chances * chosen_f, axis=1, keepdims=True)
    taken = chosen_f * aux[:, 3:4]
    here = lax.broadcasted_iota(jnp.int32, (rows, rows), 0)
    there = lax.broadcasted_iota(jnp.int32, (rows, rows), 1)
    own_id = (here & (SUB - 1)) * steps_in + (here >> shift)
    other_id = (there & (SUB - 1)) * steps_in + (there >> shift)
    earlier = (other_id < own_id).astype(bf16)
    ranks = jnp.sum(dot_nn(earlier, taken.astype(bf16)) * chosen_f, axis=1, keepdims=True)
    kept = aux[:, 3:4] * (ranks < capacity).astype(f32)
    weight = gate * kept
    up = (cot[...].astype(f32) * weight).astype(bf16)
    values = jnp.concatenate([ntwo, up], axis=0)
    rank_low = ranks.astype(jnp.int32)
    slot = jnp.concatenate([rank_low, rank_low + capacity], axis=0)
    block = route[...] * stride
    block = jnp.concatenate([block, block], axis=0)
    kept_on = jnp.concatenate([kept, kept], axis=0) > 0.5
    place = lax.broadcasted_iota(jnp.int32, (2 * rows, experts * stride), 1)
    wide_hot = ((block + slot == place) & kept_on).astype(bf16)
    at_last = (block + 2 * capacity + slot // 2 == place) & kept_on
    even_hot = (at_last & (slot % 2 == 0)).astype(bf16)
    odd_hot = (at_last & (slot % 2 == 1)).astype(bf16)
    hot_o[0] = wide_hot
    hot_o[1] = even_hot
    hot_o[2] = odd_hot
    moves.done(hot_o, middle_o, ntwo_o)
    third = ntwo.shape[1] // 3
    narrow = values[:, 2 * third :]
    last = jnp.concatenate([dot_tn(even_hot, narrow), dot_tn(odd_hot, narrow)], axis=1)
    packed = (dot_tn(wide_hot, values[:, : 2 * third]) + last).astype(bf16)
    send_o[: experts * stride, :] = packed
    send_o[experts * stride :, :] = packed
    lane8 = lax.broadcasted_iota(jnp.int32, (rows, 8), 1)
    meta_o[...] = jnp.where(
        lane8 == 0, gate, jnp.where(lane8 == 1, kept, jnp.where(lane8 == 2, scale, 0.0))
    )


def back_kernel(
    moves, core, back, om, oo, par, aux, sd, small, gate_z, hot, middle, meta, chances, route, cot, gain,
    router, ntwo, combined_o, mixlow_o, mgrad_o, ggrad_o, sg_o, gain_o, y_o, state_o, cw_s, mix_s,
    rate_s, sum_s, *, rank, count, experts
):
    rows, di = sd.shape
    half = om.shape[1]
    steps_in = rows // SUB
    gs = group_of(di)
    negative_rates(par, rate_s)
    slots = back.shape[0] // 2
    third = back.shape[1] // 2
    rows_back = (back[:slots, :].astype(f32) + back[slots:, :].astype(f32)).astype(bf16)
    last = dot_nn(hot[1], rows_back[:, :third]) + dot_nn(hot[2], rows_back[:, third:])
    both = jnp.concatenate([dot_nn(hot[0], rows_back), last], axis=1)
    combined = both[:rows, :]
    dispatch = both[rows:, :]
    combined_o[...] = combined
    gate = meta[:, 0:1]
    kept = meta[:, 1:2]
    scale = meta[:, 2:3]
    mid = middle[...]
    up = cot[...].astype(f32)
    gate_total = kept * jnp.sum(up * combined, axis=1, keepdims=True)
    lane = lax.broadcasted_iota(jnp.int32, (rows, experts), 1)
    chosen_f = (route[...] == lane).astype(f32)
    logit_grad = (gate * (chosen_f - chances[...]) * gate_total).astype(bf16)
    router_rows = dot_tn(logit_grad, ntwo[...])
    members = state_o.shape[0] // count
    for member in range(members):
        rows_here = []
        for group in range(experts // members):
            row = router_rows[group * members + member : group * members + member + 1, :]
            rows_here += [row[:, :half], row[:, half:]]
        block = slice(member * count, (member + 1) * count)
        state_o[block, di + 256 :] = jnp.concatenate(rows_here, axis=0).astype(bf16)
    ngrad = dot_nn(logit_grad, router[...]) + dispatch
    gain_o[...] = jnp.sum(ngrad * mid * scale, axis=0, keepdims=True)
    scaled = gain[...].reshape(1, -1) * ngrad
    cube = scale * scale * scale
    mgrad = up + scale * scaled - mid * cube * jnp.mean(mid * scaled, axis=1, keepdims=True)
    mgrad_o[...] = mgrad
    low = core[0] == 0
    mixlow = mgrad.astype(bf16)
    mixlow_o[...] = mixlow
    mix_s[0] = jnp.where(low, mixlow[:, :half], mixlow[:, half:])
    mix_s[1] = jnp.where(low, mixlow[:, half:], mixlow[:, :half])
    moves.done(mixlow_o, mgrad_o, combined_o)
    moves.need(om, oo, gate_z)

    def gating(g, _):
        lanes = pl.ds(pl.multiple_of(g * gs, gs), gs)
        ggrad = dot_nt(mix_s[0], om[lanes, :]) + dot_nt(mix_s[1], oo[lanes, :])
        ggrad = ggrad * aux[:, 3:4]
        ggrad_o[:, lanes] = ggrad
        z = gate_z[:, lanes]
        sg_o[:, lanes] = ggrad * (z * jax.nn.sigmoid(z))
        return 0

    lax.fori_loop(0, di // gs, gating, 0)
    moves.done(ggrad_o, sg_o)
    spread_columns(small[...], rank + count, count, cw_s)
    moves.need(sd)

    def chunk(g, _):
        lanes = pl.ds(pl.multiple_of(g * 128, 128), 128)
        rates = [jnp.broadcast_to(rate_s[n : n + 1, lanes], (SUB, 128)) for n in range(count)]

        def step(i, carry):
            grads, total = carry
            j = steps_in - 1 - i
            at = pl.ds(pl.multiple_of(j * SUB, SUB), SUB)
            sd_here = sd[at, lanes]
            sgrad = sg_o[at, lanes]
            grads = tuple(
                jnp.exp2(sd_here * rates[n]) * (grads[n] + sgrad * cw_s[j * count + n])
                for n in range(count)
            )
            return (grads, total + sd_here)

        zero = jnp.zeros((SUB, 128), f32)
        grads, total = lax.fori_loop(0, steps_in, step, ((zero,) * count, zero), unroll=8)
        row = sublane_iota(128)
        last = []
        for n in range(count):
            joined = suffix_states(jnp.exp2(rates[n] * total), grads[n])
            y_o[n, :, lanes] = jnp.where(row == SUB - 1, 0.0, pltpu.roll(joined, SUB - 1, 0))
            last.append(joined[0:1, :])
        sum_s[pl.ds(g, 1), :] = jnp.sum(total, axis=0, keepdims=True)
        to_copies(state_o, jnp.concatenate(last, axis=0).astype(bf16), lanes)
        return 0

    sum_s[...] = jnp.zeros_like(sum_s)
    lax.fori_loop(0, di // 128, chunk, 0)
    total = sum_s[...]
    top = total.astype(bf16)
    to_copies(state_o, top, slice(di, di + 128))
    to_copies(state_o, (total - top.astype(f32)).astype(bf16), slice(di + 128, di + 256))


def slot_rows(stride, capacity, blocks):
    dims = (2 * capacity * blocks, stride * blocks)
    row = lax.broadcasted_iota(jnp.int32, dims, 0)
    column = lax.broadcasted_iota(jnp.int32, dims, 1)
    half = capacity * blocks
    slot = row % capacity + row // half * capacity
    start = row % half // capacity * stride
    wide = (start + slot == column).astype(bf16)
    at_last = start + 2 * capacity + slot // 2 == column
    even = (at_last & (slot % 2 == 0)).astype(bf16)
    odd = (at_last & (slot % 2 == 1)).astype(bf16)
    return wide, even, odd


def unpack(packed, hots):
    wide, even, odd = hots
    third = packed.shape[1] // 2
    last = dot_nn(even, packed[:, :third]) + dot_nn(odd, packed[:, third:])
    return jnp.concatenate([dot_nn(wide, packed), last], axis=1).astype(bf16)


def pack(rows, hots):
    wide, even, odd = hots
    third = rows.shape[1] // 3
    narrow = rows[:, 2 * third :]
    last = jnp.concatenate([dot_tn(even, narrow), dot_tn(odd, narrow)], axis=1)
    return dot_tn(wide, rows[:, : 2 * third]) + last


def expert_kernel(
    moves, mine, other, w_gate, w_up, w_down, in_o, grad_o, act_o, gate_o, up_o, ours_o, theirs_o,
    *, stride, capacity
):
    blocks = 16
    hots = slot_rows(stride, capacity, blocks)
    size = capacity * blocks
    groups = mine.shape[0] // (stride * blocks)
    for part, arrived in enumerate((mine, other)):
        for group in range(groups):
            rows = unpack(arrived[group * stride * blocks : (group + 1) * stride * blocks, :], hots)
            at = (part * groups + group) * size
            in_o[at : at + size, :] = rows[:size, :]
            grad_o[at : at + size, :] = rows[size:, :]
    moves.need(w_gate)
    gate_in = dot_nn(in_o[...], w_gate[...])
    moves.need(w_up)
    up_in = dot_nn(in_o[...], w_up[...])
    moves.done(in_o)
    sig = jax.nn.sigmoid(gate_in)
    silu = gate_in * sig
    act = (silu * up_in).astype(bf16)
    act_o[...] = act
    moves.need(w_down)
    outputs = dot_nn(act, w_down[...])
    act_grad = dot_nt(grad_o[...], w_down[...])
    moves.done(grad_o, act_o)
    gate_grad = (act_grad * up_in * sig * (1.0 + gate_in * (1.0 - sig))).astype(bf16)
    up_grad = (act_grad * silu).astype(bf16)
    gate_o[...] = gate_grad
    up_o[...] = up_grad
    moves.done(gate_o, up_o)
    total = dot_nt(gate_grad, w_gate[...]) + dot_nt(up_grad, w_up[...])
    for part, out in ((1, theirs_o), (0, ours_o)):
        for group in range(groups):
            at = (part * groups + group) * size
            rows = jnp.concatenate([outputs[at : at + size, :], total[at : at + size, :]], axis=0)
            packed = pack(rows.astype(bf16), hots)
            out[group * stride * blocks : (group + 1) * stride * blocks, :] = packed.astype(out.dtype)
        moves.done(out)


def aside_kernel(
    moves, core, side, zm, zo, aux, pre, gate_z, scanned, ggrad, combined, middle, meta,
    out_o, comb_o, skip_o, ngrad_o, *, width, span
):
    rows, di = pre.shape
    half = zm.shape[1]
    gs = group_of(di)
    pieces = width // 16
    result = (middle[...] + meta[:, 0:1] * meta[:, 1:2] * combined[...]).astype(bf16)
    out_o[...] = dot_tn(token_order(rows), result).astype(bf16)
    def gating(g, carry):
        mine, other = carry
        lanes = pl.ds(pl.multiple_of(g * gs, gs), gs)
        grad = ggrad[:, lanes]
        z = gate_z[:, lanes]
        sig = jax.nn.sigmoid(z)
        here = scanned[:, lanes]
        zgrad = grad * here * sig * (1.0 + z * (1.0 - sig))
        z_low = zgrad.astype(bf16)
        z_turned = zgrad.T.astype(bf16)
        gated_turned = (here * (z * sig) * aux[:, 3:4]).T.astype(bf16)
        for i in range(gs // 16):
            piece = g * (gs // 16) + i
            to = pl.multiple_of(piece // pieces * span + piece % pieces * 16, 16)
            comb_o[pl.ds(to, 16), :] = z_turned[i * 16 : (i + 1) * 16, :]
            owner = piece // pieces
            holder = owner // 2 * 2 + side[0]
            to = holder * span + (1 + owner % 2) * width + piece % pieces * 16
            comb_o[pl.ds(pl.multiple_of(to, 16), 16), :] = gated_turned[i * 16 : (i + 1) * 16, :]
        pre_here = pre[:, lanes]
        act = pre_here * jax.nn.sigmoid(pre_here)
        skip_o[:, lanes] = jnp.sum(grad * (z * sig) * act, axis=0, keepdims=True)
        return (mine + dot_nn(z_low, zm[lanes, :]), other + dot_nn(z_low, zo[lanes, :]))

    moves.need(zm, zo)
    zero = jnp.zeros((rows, half), f32)
    mine, other = lax.fori_loop(0, di // gs, gating, (zero, zero))
    ngrad_o[0] = mine
    ngrad_o[1] = other


def scan_kernel(
    moves, place, xd, par, sd, q, pre, steps, sig_step, small, x_in, tpre, entry, y_in, tsuf, arrived, near,
    sgrad, cgrad_o, xd_o, spar_o, router_o, bw_s, cw_s, bacc_s, cacc_s, st_s, dk_s, sgr_s, asc_s, plow_s,
    rate_s, after_s, *, rank, count
):
    rows, di = pre.shape
    negative_rates(par, rate_s)
    after_s[...] = jnp.zeros_like(after_s)
    groups = arrived.shape[0] // count
    members = near.shape[0] // count
    spread_columns(small[...], rank, count, bw_s)
    spread_columns(small[...], rank + count, count, cw_s)
    bacc_s[...] = jnp.zeros_like(bacc_s)
    cacc_s[...] = jnp.zeros_like(cacc_s)
    spar_o[...] = jnp.zeros_like(spar_o)
    moves.need(arrived, near)

    def after_here(i, _):
        block = pl.ds(pl.multiple_of((groups - 1 - i) * count, count), count)
        carry_step(step_sums(arrived, block, di), arrived[block, :di], rate_s, after_s)
        return 0

    def just_after(i, _):
        block = pl.ds(pl.multiple_of((members - 1 - i) * count, count), count)
        carry_step(step_sums(near, block, di), near[block, :di], rate_s, after_s)
        return 0

    lax.fori_loop(0, groups - 1 - place[0] // members, after_here, 0)
    lax.fori_loop(0, members - 1 - place[0] % members, just_after, 0)
    router_sum = jnp.zeros(router_o.shape, f32)
    for there in range(groups):
        router_sum += arrived[there * count : (there + 1) * count, di + 256 :].astype(f32)
    router_o[...] = router_sum
    steps_in = rows // SUB
    gs = group_of(di)
    moves.need(x_in, sd, q, sgrad, y_in)

    def scan(g, _):
        lanes = pl.ds(pl.multiple_of(g * 128, 128), 128)
        rates = [
            jnp.broadcast_to(rate_s[n : n + 1, lanes], (SUB, 128)) for n in range(count)
        ]
        before = tpre[:, lanes]
        behind = tsuf[:, lanes]
        first = tuple(
            x_in[n, :, lanes] + jnp.exp2(rates[n] * before) * entry[n : n + 1, lanes]
            for n in range(count)
        )

        def forward(j, states):
            at = pl.ds(pl.multiple_of(j * SUB, SUB), SUB)
            sd_here = sd[at, lanes]
            q_here = q[at, lanes]
            fresh = []
            for n in range(count):
                decay = jnp.exp2(sd_here * rates[n])
                dk_s[j * count + n] = decay
                st_s[j * count + n] = states[n]
                fresh.append(decay * states[n] + q_here * bw_s[j * count + n])
            return tuple(fresh)

        last = lax.fori_loop(0, steps_in, forward, first, unroll=8)
        for n in range(count):
            st_s[steps_in * count + n] = last[n]
        zero = jnp.zeros((SUB, 128), f32)
        arriving = tuple(
            y_in[n, :, lanes] + jnp.exp2(rates[n] * behind) * after_s[n : n + 1, lanes]
            for n in range(count)
        )

        def backward(i, carry):
            grads, rate_grads = carry
            j = steps_in - 1 - i
            at = pl.ds(pl.multiple_of(j * SUB, SUB), SUB)
            sd_here = sd[at, lanes]
            q_here = q[at, lanes]
            sg = sgrad[at, lanes]
            onto = zero
            along = zero
            fresh = []
            fresh_rates = []
            for n in range(count):
                k = j * count + n
                lam = grads[n] + sg * cw_s[k]
                cacc_s[k] += sg * st_s[k + count]
                bacc_s[k] += lam * q_here
                onto = onto + lam * bw_s[k]
                carried = lam * dk_s[k]
                logs = carried * st_s[k]
                along = along + logs * rates[n]
                fresh.append(carried)
                fresh_rates.append(rate_grads[n] + logs * sd_here)
            sgr_s[at, lanes] = along
            asc_s[at, lanes] = onto
            return (tuple(fresh), tuple(fresh_rates))

        _, rate_grads = lax.fori_loop(0, steps_in, backward, (arriving, (zero,) * count), unroll=2)
        for n in range(count):
            spar_o[8 + n : 9 + n, lanes] = LN2 * jnp.sum(
                rate_grads[n] * rates[n], axis=0, keepdims=True
            )
        return 0

    lax.fori_loop(0, di // 128, scan, 0)

    moves.need(pre, sig_step, xd, steps)
    lane8 = lax.broadcasted_iota(jnp.int32, (SUB, 128), 1)
    blocks = []
    for j in range(steps_in):
        block = jnp.zeros((SUB, 128), f32)
        for n in range(count):
            k = j * count + n
            block = jnp.where(
                lane8 == rank + n, jnp.sum(bacc_s[k], axis=1, keepdims=True), block
            )
            block = jnp.where(
                lane8 == rank + count + n, jnp.sum(cacc_s[k], axis=1, keepdims=True), block
            )
        blocks.append(block)
    coef_grad = jnp.concatenate(blocks, axis=0)
    lane = lax.broadcasted_iota(jnp.int32, (rows, 128), 1)
    step_low = jnp.where(
        lane >= 128 - rank, pltpu.roll(small[...], 128 - rank, 1), 0.0
    ).astype(bf16)

    def steps_back(g, total):
        lanes = pl.ds(pl.multiple_of(g * gs, gs), gs)
        pre_here = pre[:, lanes]
        act = pre_here * jax.nn.sigmoid(pre_here)
        pre_grad = (LN2 * sgr_s[:, lanes] + act * asc_s[:, lanes]) * sig_step[:, lanes]
        spar_o[KC + 1 : KC + 2, lanes] = jnp.sum(pre_grad, axis=0, keepdims=True)
        pre_low = pre_grad.astype(bf16)
        plow_s[:, lanes] = pre_low
        return total + dot_nn(pre_low, xd[lanes, :])

    rank_grad = lax.fori_loop(0, di // gs, steps_back, jnp.zeros((rows, 128), f32))
    small_low = jnp.where(lane < rank, pltpu.roll(rank_grad, rank, 1), coef_grad).astype(bf16)

    def act_back(g, _):
        lanes = pl.ds(pl.multiple_of(g * gs, gs), gs)
        pre_here = pre[:, lanes]
        sig = jax.nn.sigmoid(pre_here)
        act_low = (pre_here * sig).astype(bf16)
        total = (
            sgrad[:, lanes] * par[KC + 2 : KC + 3, lanes]
            + steps[:, lanes] * asc_s[:, lanes]
            + dot_nt(small_low, xd[lanes, :])
        )
        cgrad_o[:, lanes] = total * sig * (1.0 + pre_here * (1.0 - sig))
        xd_o[lanes, :] = (dot_tn(act_low, small_low) + dot_tn(plow_s[:, lanes], step_low)).astype(bf16)
        return 0

    lax.fori_loop(0, di // gs, act_back, 0)


def last_kernel(
    moves, core, cgrad, halo, aux, ext, par, wm, wo, ngrad_z, spar, skip, xd, hid, gain_two,
    router_sum, pay_o, ngrad_o, extra_o, low_s, far_s, *, width
):
    rows, di = cgrad.shape
    gs = 128
    moves.need(ext)
    ahead_lane = spar.shape[0] + 4 * (hid.shape[1] // width)
    moves.need(xd)

    def conv(g, _):
        lanes = pl.ds(pl.multiple_of(g * gs, gs), gs)
        cg = cgrad[:, lanes]
        grad = par[KC - 1 : KC, lanes] * cg
        parts = [jnp.sum(cg * ext[(KC - 1) * SUB :, lanes], axis=0, keepdims=True)]
        zero = jnp.zeros((1, gs), f32)
        behind = [zero] * (KC - 1)
        for ahead in range(1, KC):
            tap = par[KC - 1 - ahead : KC - ahead, lanes]
            masked = cg * aux[:, ahead - 1 : ahead]
            shifted = ext[(KC - 1 - ahead) * SUB : (KC - 1 - ahead) * SUB + rows, lanes]
            parts.append(jnp.sum(masked * shifted, axis=0, keepdims=True))
            pieces = [masked[ahead * SUB :, :]]
            for i in range(ahead):
                pieces.append(from_after(masked[i * SUB : (i + 1) * SUB, :], zero))
                k = KC - 1 - ahead + i
                behind[k] = behind[k] + tap * masked[i * SUB : i * SUB + 1, :]
            grad = grad + tap * jnp.concatenate(pieces, axis=0)
        low_s[:, lanes] = grad.astype(bf16)
        pay_o[lanes, 0:128] = grad.T.astype(bf16)
        pay_o[lanes, 128:256] = xd[lanes, :]
        extra = jnp.concatenate(behind + [jnp.zeros((SUB - KC + 1, gs), f32)], axis=0)
        far_s[:SUB, lanes] = extra.astype(bf16)
        own = jnp.concatenate(
            parts[::-1]
            + [jnp.sum(cg, axis=0, keepdims=True), spar[KC + 1 : KC + 2, lanes], skip[:, lanes]]
            + [zero, spar[8:, lanes], jnp.zeros((ahead_lane - spar.shape[0], gs), f32), extra]
            + [jnp.zeros((128 - ahead_lane - SUB, gs), f32)],
            axis=0,
        )
        pay_o[lanes, 256:384] = own.T.astype(bf16)
        return 0

    lax.fori_loop(0, di // gs, conv, 0)
    far_s[SUB:, :] = jnp.zeros_like(far_s[SUB:, :])
    moves.need(wm, wo, ngrad_z, hid)
    low = core[0] == 0

    def onto_inputs(values):
        return dot_nn(values, wm[...]), dot_nn(values, wo[...])

    def joined(mine, other):
        return jnp.concatenate([jnp.where(low, mine, other), jnp.where(low, other, mine)], axis=1)

    mine, other = onto_inputs(low_s[...])
    ngrad = joined(mine + ngrad_z[0], other + ngrad_z[1])
    ngrad_o[...] = ngrad
    far = joined(*onto_inputs(far_s[...]))[:SUB, :]
    extra_o[...] = far
    first = hid[...].astype(f32)
    scale = lax.rsqrt(jnp.mean(first * first, axis=1, keepdims=True) + epsilon)
    gains = jnp.sum(ngrad * first * scale, axis=0, keepdims=True)
    first = halo[SUB:, :].astype(f32)
    scale = lax.rsqrt(jnp.mean(first * first, axis=1, keepdims=True) + epsilon)
    gains = gains + jnp.sum(far * first * scale, axis=0, keepdims=True)
    model = first.shape[1]
    each = model // width
    row = lax.broadcasted_iota(jnp.int32, (width, model), 0)
    column = lax.broadcasted_iota(jnp.int32, (width, model), 1)
    here = column // each == row
    extra = jnp.zeros((width, 128), f32)
    router_row = jnp.concatenate([router_sum[0:1, :], router_sum[1:2, :]], axis=1)
    router_top = router_row.astype(bf16).astype(f32)
    rows_sent = (gains, gain_two[...], router_top, router_row - router_top)
    for k, values in enumerate(rows_sent):
        spread = jnp.where(here, values, 0.0).astype(bf16)
        at = lax.broadcasted_iota(jnp.int32, (model, 128), 0)
        to = lax.broadcasted_iota(jnp.int32, (model, 128), 1)
        placed = (at % each + spar.shape[0] + k * each == to).astype(bf16)
        extra = extra + dot_nn(spread, placed)
    extra = extra.astype(bf16)
    for place in range(di // width):
        pay_o[place * width : (place + 1) * width, 256:384] += extra


def tail_kernel(
    moves, place, core, xd, par, sd, q, pre, steps, sig_step, small, x_in, tpre, entry, y_in, tsuf,
    arrived, near, sgrad, halo, aux, ext, wm, wo, ngrad_z, skip, hid, gain_two,
    pay_o, ngrad_o, extra_o, low_s, far_s, cgrad_s, xd_s, spar_s, router_s, *scratch,
    rank, count, width
):
    scan_kernel(
        moves, place, xd, par, sd, q, pre, steps, sig_step, small, x_in, tpre, entry, y_in, tsuf,
        arrived, near, sgrad, cgrad_s, xd_s, spar_s, router_s, *scratch, rank=rank, count=count
    )
    last_kernel(
        moves, core, cgrad_s, halo, aux, ext, par, wm, wo, ngrad_z, spar_s, skip, xd_s, hid,
        gain_two, router_s, pay_o, ngrad_o, extra_o, low_s, far_s, width=width
    )


def hidden_kernel(ngrad_in, beyond, hid, mgrad, gain, first_o):
    first = hid[...].astype(f32)
    rows = first.shape[0]
    ngrad = ngrad_in[...]
    row = lax.broadcasted_iota(jnp.int32, first.shape, 0)
    for i in range(KC - 1):
        at = rows - 1 - (KC - 2 - i) * SUB
        ngrad = ngrad + jnp.where(row == at, beyond[i : i + 1, :], 0.0)
    scale = lax.rsqrt(jnp.mean(first * first, axis=1, keepdims=True) + epsilon)
    scaled = gain[...].reshape(1, -1) * ngrad
    cube = scale * scale * scale
    grad = (
        mgrad[...] + scale * scaled - first * cube * jnp.mean(first * scaled, axis=1, keepdims=True)
    )
    order = token_order(rows)
    top = grad.astype(bf16)
    left = grad - top.astype(f32)
    mid = left.astype(bf16)
    low_part = (left - mid.astype(f32)).astype(bf16)
    first_o[...] = dot_tn(order, top) + dot_tn(order, mid) + dot_tn(order, low_part)


def ready_kernel(
    moves, side, comb, nrm_all, mix_half, z_o, mine_o, theirs_o, z_s, gated_s
):
    places = comb.shape[0]
    width = z_o.shape[0]
    for place in range(places):
        z_s[:, place * 128 : (place + 1) * 128] = comb[place, :width, :]
    for k in range(places // 2):
        place = 2 * k + side[0]
        gated_s[:, k * 128 : (k + 1) * 128] = comb[place, width : 3 * width, :]
    moves.need(mix_half)
    grads = dot_nn(gated_s[...], mix_half[...]).astype(bf16)
    first = side[0] == 0
    mine_o[...] = jnp.where(first, grads[:width, :], grads[width:, :])
    theirs_o[...] = jnp.where(first, grads[width:, :], grads[:width, :])
    moves.need(nrm_all)
    z_o[...] = dot_nn(z_s[...], nrm_all[...]).astype(bf16)


def grads_kernel(got, nrm_all, out_o, left_s, *, base):
    places, width, _ = got.shape
    model = nrm_all.shape[1]
    each = model // width
    rest = jnp.zeros((width, 256), f32)
    routers = [jnp.zeros((width, 128), f32) for _ in range(places * each // 128)]
    lane = lax.broadcasted_iota(jnp.int32, (width, 128), 1)
    row = lax.broadcasted_iota(jnp.int32, (128, 128), 0)
    column = lax.broadcasted_iota(jnp.int32, (128, 128), 1)
    after = row - (base + 2 * each)
    late = column == 127 - (KC - 2 - after) * SUB
    placed = (late & (after >= 0) & (after < KC - 1)).astype(bf16)
    for place in range(places):
        at = gathered_place(place)
        inner = got[at, :, :128]
        if place + 1 < places:
            beyond = dot_nn(got[gathered_place(place + 1), :, 256:384], placed)
            inner = (inner.astype(f32) + beyond).astype(bf16)
        left_s[:, at * 128 : (at + 1) * 128] = inner
        there = got[at, :, 128:].astype(f32)
        rest = rest + there
        k = place * each // 128
        inside = place * each % 128
        mine = (lane >= inside) & (lane < inside + each)
        for part in range(2):
            turn = (inside - base - part * each) % 128
            routers[k] = routers[k] + jnp.where(mine, pltpu.roll(there[:, 128:], turn, 1), 0.0)
    out_o[width:, :256] = rest.astype(bf16)
    out_o[width:, 256:] = jnp.concatenate(routers, axis=1).astype(bf16)
    out_o[:width, :model] = dot_nn(left_s[...], nrm_all[...]).astype(bf16)


def token_order(rows):
    steps_in = rows // SUB
    row = lax.broadcasted_iota(jnp.int32, (rows, rows), 0)
    column = lax.broadcasted_iota(jnp.int32, (rows, rows), 1)
    return ((row % SUB) * steps_in + row // SUB == column).astype(bf16)


def final_kernel(
    ours, theirs, ours_two, theirs_two, x_o, z_o, out_o, conv_o, bias_o, xp_o, dt_o, db_o, al_o, skip_o, router_o, one_o,
    two_o, mine_s, other_s, *, rank, count, experts
):
    width = out_o.shape[0]
    model = router_o.shape[1]
    each = model // width
    x_o[...] = ours[:width, :model].astype(f32) + theirs[:width, :model].astype(f32)
    z_o[...] = ours_two[:width, :].astype(f32) + theirs_two[:width, :].astype(f32)
    out_o[...] = ours_two[width:, :].astype(f32) + theirs_two[width:, :].astype(f32)
    rest = slice(width, 2 * width)
    xd = ours[rest, :128].astype(f32) + theirs[rest, :128].astype(f32)
    xp_o[...] = xd[:, : rank + 2 * count]
    gap = jnp.zeros((128 - width, 128), f32)
    turned = jnp.concatenate([xd, gap], axis=0).T
    dt_o[...] = turned[128 - rank :, :width]
    vectors = jnp.zeros((128, 128), f32)
    for part, held in ((ours, mine_s), (theirs, other_s)):
        block = jnp.concatenate([part[rest, 128:256].astype(f32), gap], axis=0).T
        vectors = vectors + block
        for k in range(experts * each // 128):
            lanes = slice(256 + k * 128, 384 + k * 128)
            piece = jnp.concatenate([part[rest, lanes].astype(f32), gap], axis=0)
            held[k * 128 : (k + 1) * 128, :] = piece.T
        held[experts * each :, :] = jnp.zeros_like(held[experts * each :, :])
        held[experts * each : (experts + 2) * each, :] = block[8 + count : 8 + count + 2 * each, :]
    conv_o[...] = vectors[:KC, :width]
    bias_o[...] = vectors[KC : KC + 1, :width].reshape(width)
    db_o[...] = vectors[KC + 1 : KC + 2, :width].reshape(width)
    skip_o[...] = vectors[KC + 2 : KC + 3, :width].reshape(width)
    al_o[...] = vectors[8 : 8 + count, :width]
    row = lax.broadcasted_iota(jnp.int32, (128, model), 0)
    column = lax.broadcasted_iota(jnp.int32, (128, model), 1)
    total = jnp.zeros((experts + 8, model), f32)
    for at in range(each):
        to = (row * each + at == column).astype(bf16)
        picked = pl.ds(at, experts + 8, stride=each)
        total = total + dot_nn(mine_s[picked, :].astype(bf16), to)
        total = total + dot_nn(other_s[picked, :].astype(bf16), to)
    router_o[...] = total[:experts, :]
    one_o[...] = total[experts : experts + 1, :].reshape(model)
    two_o[...] = total[experts + 1 : experts + 2, :].reshape(model)


def token_order(rows):
    steps_in = rows // SUB
    row = lax.broadcasted_iota(jnp.int32, (rows, rows), 0)
    column = lax.broadcasted_iota(jnp.int32, (rows, rows), 1)
    return ((row % SUB) * steps_in + row // SUB == column).astype(bf16)


def exchange(values):
    return lax.all_to_all(values, "wide", split_axis=0, concat_axis=0, tiled=True)


def exchange_near(values, members):
    groups = [[u * members + z for z in range(members)] for u in range(32 // members)]
    blocks = values.reshape(members, -1, values.shape[1])
    return lax.all_to_all(
        blocks, "wide", split_axis=0, concat_axis=0, tiled=True, axis_index_groups=groups
    ).reshape(values.shape)


def exchange_far(values, members):
    groups = [[u * members + z for u in range(32 // members)] for z in range(members)]
    blocks = values.reshape(32 // members, -1, values.shape[1])
    return lax.all_to_all(
        blocks, "wide", split_axis=0, concat_axis=0, tiled=True, axis_index_groups=groups
    ).reshape(values.shape)


def gathered_place(place):
    return (place // 8 * 4 + place % 4) * 2 + place // 4 % 2


def exchange_channels(values):
    order = sorted(range(32), key=gathered_place)
    return lax.all_to_all(
        values, "wide", split_axis=0, concat_axis=0, tiled=True, axis_index_groups=[order]
    )


def other_chip(values):
    return lax.ppermute(values, "wide", [(i, i ^ 4) for i in range(32)])


def pair_up(values, partner, place):
    first = (place // 4) % 2 == 0
    return jnp.concatenate(
        [jnp.where(first, values, partner), jnp.where(first, partner, values)], axis=0
    )


def gather_pairs(both):
    groups = [[(y * 2 + x) * 4 + z for y in range(4) for z in range(4)] for x in range(2)]
    return lax.all_gather(both, "wide", axis=0, tiled=True, axis_index_groups=groups)


def exchange_sides(values):
    groups = [
        [(side * 2 + core) * 32 + place for side in range(2) for place in range(32)]
        for core in range(2)
    ]
    return lax.all_to_all(
        values, ("dp", "wide"), split_axis=0, concat_axis=0, tiled=True, axis_index_groups=groups
    )


def other_core(values):
    return lax.ppermute(values, "dp", [(0, 1), (1, 0), (2, 3), (3, 2)])


def other_side(values):
    return lax.ppermute(values, "dp", [(0, 2), (2, 0), (1, 3), (3, 1)])


def body(
    hidden, cotangent, routes, seg_lengths, gain_mix, in_x, in_z, conv_w, conv_b, x_proj, dt_proj,
    dt_bias, a_log, skip_d, out_proj, gain_moe, router, w_gate, w_up, w_down,
):
    rows, model = hidden.shape
    places = lax.axis_size("wide")
    place = lax.axis_index("wide")
    core = (lax.axis_index("dp") % 2).astype(jnp.int32).reshape(1)
    place_arr = place.astype(jnp.int32).reshape(1)
    width = in_x.shape[1]
    di = width * places
    count = a_log.shape[0]
    rank = dt_proj.shape[0]
    experts = router.shape[1]
    capacity = max(CAP * rows // (4 * places), 2)
    stride = -(-2 * capacity // 16) * 16
    half = model // 2
    steps_in = rows // SUB
    shift = SUB.bit_length() - 1
    span = 3 * width
    members = 4
    side = (place // 4 % 2).astype(jnp.int32).reshape(1)

    gate_share = call(
        pack_gate_kernel, [shape((width, model), bf16)], [], (core, in_z.T, out_proj), smem=1
    )[0]
    gate_share, x_proj = lax.optimization_barrier((gate_share, x_proj))
    pay_one = call(
        partial(pack_kernel, places=places),
        [shape((di, half + 128), bf16)],
        [],
        (core, in_x.T, x_proj, dt_proj, conv_w, conv_b, dt_bias, skip_d, a_log),
        smem=1,
    )[0]
    pay_one, hidden, cotangent, routes, seg_lengths = lax.optimization_barrier(
        (pay_one, hidden, cotangent, routes, seg_lengths)
    )
    gate_partner = other_chip(gate_share)
    pay_one, gate_partner = lax.optimization_barrier((pay_one, gate_partner))
    wm = exchange_channels(pay_one.reshape(places, width, half + 128)).reshape(di, half + 128)
    zm = gather_pairs(pair_up(gate_share, gate_partner, place))
    nrm, tail, hid, cot, route, aux = call(
        prepare_kernel,
        [
            shape((rows, model), bf16),
            shape((16, model), bf16),
            shape((rows, model), bf16),
            shape((rows, model), bf16),
            shape((rows, 1), jnp.int32),
            shape((rows, 128)),
        ],
        [],
        (place_arr * rows, seg_lengths, hidden, cotangent, routes.T, gain_mix),
        smem=2,
    )
    halo = lax.ppermute(tail, "wide", [(i, i + 1) for i in range(places - 1)])
    nrm_partner = other_chip(nrm)
    wm, halo = lax.optimization_barrier((wm, halo))
    wo = other_core(wm)
    ext, pre, steps, sig_step, small, x_in, tpre, tsuf, states, par, xd_weight, sd, q = call(
        partial(front_kernel, rank=rank, count=count),
        [
            shape((rows + (KC - 1) * SUB, di)),
            shape((rows, di)),
            shape((rows, di)),
            shape((rows, di)),
            shape((rows, 128)),
            shape((count, SUB, di)),
            shape((SUB, di)),
            shape((SUB, di)),
            shape((members * count, di + 256), bf16),
            shape((8 + count, di)),
            shape((di, 128), bf16),
            shape((rows, di)),
            shape((rows, di)),
        ],
        [
            pltpu.VMEM((steps_in * count, SUB, 128), f32),
            pltpu.VMEM((2, rows + 16, half), bf16),
            pltpu.VMEM((16, 128), f32),
        ],
        (core, nrm, halo, wm, wo, aux),
        smem=1,
        late=(3, 4),
        early=(0, 1, 2, 3, 9, 10, 11, 12),
    )

    near = exchange_near(states, members)
    zm, nrm_partner, near = lax.optimization_barrier((zm, nrm_partner, near))
    zo = other_core(zm)
    z_lanes = pl.ds(0, half)
    out_lanes = pl.ds(half, half)
    gate_z = call(
        gate_kernel,
        [shape((rows, di))],
        [pltpu.VMEM((2, rows, half), bf16)],
        (core, nrm, zm, zo),
        smem=1,
        late=(2, 3),
        lanes={2: z_lanes, 3: z_lanes},
    )[0]
    states = call(
        partial(forward_group_kernel, di=di, count=count),
        [shape((places // members * count, di + 256), bf16)],
        [pltpu.VMEM((count, di), f32)] * 2,
        (near, par),
        limit=12 * 1024 * 1024,
    )[0]
    states = exchange_far(states, members)

    nrm_pair = pair_up(nrm, nrm_partner, place)
    states, gate_z, nrm_pair = lax.optimization_barrier((states, gate_z, nrm_pair))
    normed_all = gather_pairs(nrm_pair)
    scanned, send, middle, ntwo, chances, meta, hot, entry = call(
        partial(
            middle_kernel,
            rank=rank,
            count=count,
            experts=experts,
            stride=stride,
            capacity=capacity,
            shift=shift,
        ),
        [
            shape((rows, di)),
            shape((2 * experts * stride, 2 * model // 3), bf16),
            shape((rows, model)),
            shape((rows, model), bf16),
            shape((rows, experts)),
            shape((rows, 8)),
            shape((3, 2 * rows, experts * stride), bf16),
            shape((count, di)),
        ],
        [
            pltpu.VMEM((steps_in * count, SUB, 128), f32),
            pltpu.VMEM((steps_in * count, SUB, 128), f32),
            pltpu.VMEM((count, di), f32),
        ],
        (
            core, place_arr, zm, zo, par, aux, pre, sd, q, x_in, small, states, near, tpre, hid, cot,
            route, gain_moe, router.T, gate_z,
        ),
        smem=2,
        late=(11, 12, 9, 7, 8, 6, 19, 2, 3),
        early=(7, 0, 6, 2, 3),
        lanes={2: out_lanes, 3: out_lanes},
    )
    arrived = exchange_sides(send.reshape(2 * experts, stride, -1)).reshape(send.shape)
    slots = 2 * places * capacity
    theirs_in = other_core(arrived)
    expert_in, grad_rows, hidden_act, gate_grad, up_grad, ours, theirs = call(
        partial(expert_kernel, stride=stride, capacity=capacity),
        [shape((2 * slots, model), bf16)] * 2
        + [shape((2 * slots, w_gate.shape[2]), bf16)] * 3
        + [shape(send.shape, bf16)] * 2,
        [],
        (arrived, theirs_in, w_gate[0], w_up[0], w_down[0]),
        late=(2, 3, 4),
        early=(0, 1, 2, 3, 4, 5, 6),
    )
    back = (ours.astype(f32) + other_core(theirs).astype(f32)).astype(bf16)
    back = exchange_sides(back.reshape(2 * experts, stride, -1)).reshape(send.shape)
    grad_w_down = dot_tn(hidden_act, grad_rows)[None]
    grad_w_gate = dot_tn(expert_in, gate_grad)[None]
    grad_w_up = dot_tn(expert_in, up_grad)[None]
    back, grad_w_down, grad_w_gate, grad_w_up = lax.optimization_barrier(
        (back, grad_w_down, grad_w_gate, grad_w_up)
    )

    combined, mixlow, mgrad, ggrad, sgrad, gain_two, y_in, adjoints = call(
        partial(back_kernel, rank=rank, count=count, experts=experts),
        [
            shape((rows, model)),
            shape((rows, model), bf16),
            shape((rows, model)),
            shape((rows, di)),
            shape((rows, di)),
            shape((1, model)),
            shape((count, SUB, di)),
            shape((members * count, di + 256 + half), bf16),
        ],
        [
            pltpu.VMEM((steps_in * count, SUB, 128), f32),
            pltpu.VMEM((2, rows, half), bf16),
            pltpu.VMEM((count, di), f32),
            pltpu.VMEM((16, 128), f32),
        ],
        (
            core, back, zm, zo, par, aux, sd, small, gate_z, hot, middle, meta, chances, route,
            cot, gain_moe, router.T, ntwo,
        ),
        smem=1,
        late=(2, 3, 8, 6),
        early=(1, 2, 0, 3, 4),
        lanes={2: out_lanes, 3: out_lanes},
    )
    near_back = exchange_near(adjoints, members)
    adjoints = call(
        partial(backward_group_kernel, di=di, count=count),
        [shape((places // members * count, di + 256 + half), bf16)],
        [pltpu.VMEM((count, di), f32)] * 2,
        (near_back, par),
        limit=12 * 1024 * 1024,
    )[0]
    adjoints = exchange_far(adjoints, members)
    out, comb, skip_part, ngrad_z = call(
        partial(aside_kernel, width=width, span=span),
        [
            shape((rows, model), bf16),
            shape((places * span, 128), bf16),
            shape((1, di)),
            shape((2, rows, half)),
        ],
        [],
        (
            core, side, zm, zo, aux, pre, gate_z, scanned, ggrad, combined, middle, meta,
        ),
        smem=2,
        late=(2, 3),
        lanes={2: z_lanes, 3: z_lanes},
    )
    adjoints, comb = lax.optimization_barrier((adjoints, comb))
    mixlow, normed_all = lax.optimization_barrier((mixlow, normed_all))
    mix_half = gather_pairs(mixlow)
    comb_got = exchange_channels(comb.reshape(places, span, 128))

    pay, ngrad, beyond = call(
        partial(tail_kernel, rank=rank, count=count, width=width),
        [shape((di, 384), bf16), shape((rows, model)), shape((SUB, model))],
        [
            pltpu.VMEM((rows, di), bf16),
            pltpu.VMEM((16, di), bf16),
            pltpu.VMEM((rows, di), f32),
            pltpu.VMEM((di, 128), bf16),
            pltpu.VMEM((8 + count, di), f32),
            pltpu.VMEM((count, half), f32),
        ]
        + [pltpu.VMEM((steps_in * count, SUB, 128), f32)] * 4
        + [pltpu.VMEM(((steps_in + 1) * count, SUB, 128), f32)]
        + [pltpu.VMEM((steps_in * count, SUB, 128), f32)]
        + [pltpu.VMEM((rows, di), f32)] * 2
        + [pltpu.VMEM((rows, di), bf16)]
        + [pltpu.VMEM((count, di), f32)] * 2,
        (
            place_arr, core, xd_weight, par, sd, q, pre, steps, sig_step, small, x_in, tpre, entry,
            y_in, tsuf, adjoints, near_back, sgrad, halo, aux, ext, wm, wo, ngrad_z, skip_part, hid,
            gain_two,
        ),
        smem=2,
        late=(15, 16, 10, 4, 5, 17, 13, 6, 8, 2, 7, 20, 21, 22, 23, 25),
        lanes={21: z_lanes, 22: z_lanes},
    )
    got_pay = exchange_channels(pay.reshape(places, width, 384))
    beyond = lax.ppermute(beyond, "wide", [(i + 1, i) for i in range(places - 1)])
    z_ready, out_ready, out_theirs = call(
        ready_kernel,
        [shape((width, model), bf16)] * 3,
        [
            pltpu.VMEM((width, places * rows), bf16),
            pltpu.VMEM((2 * width, places // 2 * rows), bf16),
        ],
        (side, comb_got, normed_all, mix_half),
        smem=1,
        late=(3,),
        limit=24 * 1024 * 1024,
    )
    out_other = other_chip(out_theirs)
    got_pay, out_other, beyond = lax.optimization_barrier((got_pay, out_other, beyond))
    first_grad = call(
        hidden_kernel, [shape((rows, model))], [], (ngrad, beyond, hid, mgrad, gain_mix), limit=12 * 1024 * 1024
    )[0]
    out_ready = (out_ready.astype(f32) + out_other.astype(f32)).astype(bf16)
    ready = jnp.concatenate([z_ready, out_ready], axis=0)
    ready = (ready.astype(f32) + other_core(ready).astype(f32)).astype(bf16)
    ready_side = other_side(ready)
    per_place = model // width
    mats = call(
        partial(grads_kernel, base=8 + count + 2 * per_place),
        [shape((2 * width, 256 + places * per_place), bf16)],
        [pltpu.VMEM((width, places * rows), bf16)],
        (got_pay, normed_all),
        limit=24 * 1024 * 1024,
    )[0]
    mats = (mats.astype(f32) + other_core(mats).astype(f32)).astype(bf16)
    grad_x, grad_z, grad_out, grad_conv, grad_bias, grad_xp, grad_dt, grad_db, grad_al, grad_sk, grad_router, gain_one, gain_two = call(
        partial(final_kernel, rank=rank, count=count, experts=experts),
        [
            shape((width, model)),
            shape((width, model)),
            shape((width, model)),
            shape((KC, width)),
            shape((width,)),
            shape((width, rank + 2 * count)),
            shape((rank, width)),
            shape((width,)),
            shape((count, width)),
            shape((width,)),
            shape((experts, model)),
            shape((model,)),
            shape((model,)),
        ],
        [pltpu.VMEM(((experts + 8) * per_place, 128), f32)] * 2,
        (mats, other_side(mats), ready, ready_side),
        limit=12 * 1024 * 1024,
    )
    return (
        out,
        first_grad,
        gain_one,
        grad_x.T,
        grad_z.T,
        grad_conv,
        grad_bias,
        grad_xp,
        grad_dt,
        grad_db,
        grad_al,
        grad_sk,
        grad_out,
        gain_two,
        grad_router.T,
        grad_w_gate,
        grad_w_up,
        grad_w_down,
    )


def solution(mesh):
    rows = P(("dp", "wide"), None)
    expert_columns = P("wide", None, "dp")
    expert_rows = P("wide", "dp", None)
    placed = (
        rows, rows, rows, P("dp", None), P(), P(None, "wide"), P(None, "wide"), P(None, "wide"),
        P("wide"), P("wide", None), P(None, "wide"), P("wide"), P(None, "wide"), P("wide"),
        P("wide", None), P(), P(), expert_columns, expert_columns, expert_rows,
    )
    given = (
        rows, rows, P(), P(None, "wide"), P(None, "wide"), P(None, "wide"), P("wide"),
        P("wide", None), P(None, "wide"), P("wide"), P(None, "wide"), P("wide"), P("wide", None),
        P(), P(), expert_columns, expert_columns, expert_rows,
    )
    return jax.shard_map(body, mesh=mesh, in_specs=placed, out_specs=given, check_vma=False)
```

profile of v0, /device:TPU:1, one launch (start us, length us, event | category | flops | bytes accessed | tf_op | source)
XLA Modules:
  0.0 289.9 jit_solution(8765853007057702062)
XLA Ops:
  7.2 1.6 shard_map.331
  8.8 2.0 collective-permute-start
  10.8 2.4 shard_map.332
  14.9 8.8 %all-to-all-start = ((bf16[32,48,512]{2,1,0:T(8,128)(2,1)}), bf16[32,48,512]{2,1,0:T(8,128)(2,1)S(1)}, u32[]{:S(2)}, u32[]{:S(2)}) async-start(bf16[32,48,512]{2,1,0:T(8,128)(2,1)} %bitcast.48), calls=%async_computation | async-start | bytes 3145728 | tf_op jit(solution)/shard_map/all_to_all | solution.py:1207
  23.7 2.4 shard_map.333
  26.1 3.1 %collective-permute-start.2 = (bf16[16,768]{1,0:T(8,128)(2,1)}, bf16[16,768]{1,0:T(8,128)(2,1)S(1)}, u32[]{:S(2)}, u32[]{:S(2)}) collective-permute-start(bf16[16,768]{1,0:T(8,128)(2,1)} %get-tuple-element.121), channel_id=1, source_target_pairs={{0,1},{1,2},{2,3},{3,4},{4,5},{5,6},{6,7},{7,8},{8,9},{9,10},{10,1... | collective-permute-start | bytes 73736 | tf_op jit(solution)/shard_map/ppermute | solution.py:1301
  29.2 12.3 %collective-permute-done.2.refs_2_.refs_18_ = bf16[16,768]{1,0:T(8,128)(2,1)S(1)} collective-permute-done((bf16[16,768]{1,0:T(8,128)(2,1)}, bf16[16,768]{1,0:T(8,128)(2,1)S(1)}, u32[]{:S(2)}, u32[]{:S(2)}) %collective-permute-start.2) | collective-permute-done | bytes 24608 | tf_op jit(solution)/shard_map/ppermute | solution.py:1301
  41.5 4.0 %all-to-all-done = bf16[32,48,512]{2,1,0:T(8,128)(2,1)S(1)} async-done(((bf16[32,48,512]{2,1,0:T(8,128)(2,1)}), bf16[32,48,512]{2,1,0:T(8,128)(2,1)S(1)}, u32[]{:S(2)}, u32[]{:S(2)}) %all-to-all-start) | async-done | bytes 1572896 | tf_op jit(solution)/shard_map/all_to_all | solution.py:1207
  45.6 3.1 %collective-permute-start.3 = (bf16[1536,512]{1,0:T(8,128)(2,1)S(1)}, bf16[1536,512]{1,0:T(8,128)(2,1)S(1)}, u32[]{:S(2)}, u32[]{:S(2)}) collective-permute-start(bf16[1536,512]{1,0:T(8,128)(2,1)S(1)} %bitcast.45), channel_id=1, source_target_pairs={{0,32},{32,0},{64,96},{96,64},{1,33},{33,1},{65,97},{97,65},{2,34}... | collective-permute-start | bytes 4718600 | tf_op jit(solution)/shard_map/ppermute | solution.py:1239
  48.7 1.8 collective-permute-start.1
  52.9 13.4 %shard_map.334 = (f32[152,1536]{1,0:T(8,128)}, f32[128,1536]{1,0:T(8,128)}, f32[128,1536]{1,0:T(8,128)}, f32[128,1536]{1,0:T(8,128)}, f32[128,128]{1,0:T(8,128)}...) custom-call(s32[1]{0:T(128)} %bitcast.core.refs_0_.refs_1_, ...), custom_call_target="tpu_custom_call" | custom-call | tf_op jit(solution)/shard_map/pallas_call | solution.py:92
  66.3 3.4 %all-to-all-start.1 = ((bf16[4,16,1792]{2,1,0:T(8,128)(2,1)}), bf16[4,16,1792]{2,1,0:T(8,128)(2,1)S(1)}, u32[]{:S(2)}, u32[]{:S(2)}) async-start(bf16[4,16,1792]{2,1,0:T(8,128)(2,1)} %bitcast.61), calls=%async_computation.1 | async-start | bytes 458752 | tf_op jit(solution)/shard_map/all_to_all | solution.py:1188
  69.7 5.9 %all-to-all-done.1 = bf16[4,16,1792]{2,1,0:T(8,128)(2,1)S(1)} async-done(((bf16[4,16,1792]{2,1,0:T(8,128)(2,1)}), bf16[4,16,1792]{2,1,0:T(8,128)(2,1)S(1)}, u32[]{:S(2)}, u32[]{:S(2)}) %all-to-all-start.1) | async-done | bytes 229408 | tf_op jit(solution)/shard_map/all_to_all | solution.py:1188
  78.8 4.2 %all-to-all-start.2 = ((bf16[8,16,1792]{2,1,0:T(8,128)(2,1)}), bf16[8,16,1792]{2,1,0:T(8,128)(2,1)S(1)}, u32[]{:S(2)}, u32[]{:S(2)}) async-start(bf16[8,16,1792]{2,1,0:T(8,128)(2,1)} %bitcast.10), calls=%async_computation.2 | async-start | bytes 917504 | tf_op jit(solution)/shard_map/all_to_all | solution.py:1196
  83.9 1.4 copy-done.11
  85.3 5.1 %shard_map.336.refs_19_.refs_8_.refs_6_ = f32[128,1536]{1,0:T(8,128)} custom-call(s32[1]{0:T(128)} %bitcast.core.refs_0_.refs_1_, bf16[128,768]{1,0:T(8,128)(2,1)} %get-tuple-element.119.refs_1_, bf16[1536,768]{1,0:T(8,128)(2,1)} %all-gather.4.cloned.1.call-done.refs_2_, bf16[1536,768]{1,0:T(8,128)(2,1)} %copy-done.11), custom_call_target="tpu_custom_call" | custom-call | tf_op jit(solution)/shard_map/pallas_call | solution.py:92
  90.4 1.4 all-to-all-done.2
  92.6 11.4 %shard_map.337 = (f32[128,1536]{1,0:T(8,128)}, bf16[1024,512]{1,0:T(8,128)(2,1)}, f32[128,768]{1,0:T(8,128)}, bf16[128,768]{1,0:T(8,128)(2,1)}, f32[128,32]{1,0:...) custom-call(s32[1]{0:T(128)} %bitcast.core.refs_0_.refs_1_, ...), custom_call_target="tpu_custom_call" | custom-call | tf_op jit(solution)/shard_map/pallas_call | solution.py:92
  104.0 24.2 %all_to_all.45 = bf16[64,16,512]{2,1,0:T(8,128)(2,1)S(1)} all-to-all(bf16[64,16,512]{2,1,0:T(8,128)(2,1)} %bitcast.59), channel_id=1, replica_groups={{0,1,2,3,4,5,6,7,8,9,10,11,12,13,14,15,16,17,18,19,20,21,22,23,24,25,26..., dimensions={0} | all-to-all | bytes 2097152 | tf_op jit(solution)/shard_map/all_to_all | solution.py:1233
  128.2 2.5 collective-permute-start.5
  130.7 2.3 collective-permute-done.5.refs_1_
  133.9 11.9 %shard_map.338 = (bf16[640,768]{1,0:T(8,128)(2,1)}, bf16[640,768]{1,0:T(8,128)(2,1)}, bf16[640,768]{1,0:T(8,128)(2,1)}, bf16[640,768]{1,0:T(8,128)(2,1)}, bf16[6...) custom-call(bf16[1024,512]{1,0:T(8,128)(2,1)} %bitcast.51, bf16[1024,512]{1,0:T(8,128)(2,1)} %copy-done.19, ...), custom_call_target="tpu_custom_call" | custom-call | tf_op jit(solution)/shard_map/pallas_call | solution.py:92
  146.3 2.5 collective-permute-done.6
  148.9 2.7 add_convert_fusion
  151.5 4.9 %all-to-all-start.4 = ((bf16[64,16,512]{2,1,0:T(8,128)(2,1)}), bf16[64,16,512]{2,1,0:T(8,128)(2,1)S(1)}, u32[]{:S(2)}, u32[]{:S(2)}) async-start(bf16[64,16,512]{2,1,0:T(8,128)(2,1)} %bitcast.18), calls=%async_computation.4 | async-start | bytes 2097152 | tf_op jit(solution)/shard_map/all_to_all | solution.py:1233
  156.7 2.5 convolution_bitcast_fusion.1
  159.3 2.5 convolution_bitcast_fusion
  161.8 2.5 convolution_bitcast_fusion.2
  164.3 9.9 %all-to-all-done.4 = bf16[64,16,512]{2,1,0:T(8,128)(2,1)S(1)} async-done(((bf16[64,16,512]{2,1,0:T(8,128)(2,1)}), bf16[64,16,512]{2,1,0:T(8,128)(2,1)S(1)}, u32[]{:S(2)}, u32[]{:S(2)}) %all-to-all-start.4) | async-done | bytes 1048608 | tf_op jit(solution)/shard_map/all_to_all | solution.py:1233
  175.3 10.0 %shard_map.339 = (f32[128,768]{1,0:T(8,128)}, bf16[128,768]{1,0:T(8,128)(2,1)}, f32[128,768]{1,0:T(8,128)}, f32[128,1536]{1,0:T(8,128)}, f32[128,1536]{1,0:T(8,1...) custom-call(s32[1]{0:T(128)} %bitcast.core.refs_0_.refs_1_, bf16[1024,512]{1,0:T(8,128)(2,1)} %bitcast.49, ...), custom_call_target="tpu_custom_call" | custom-call | tf_op jit(solution)/shard_map/pallas_call | solution.py:92
  185.3 9.0 %all_to_all.46 = bf16[4,16,2176]{2,1,0:T(8,128)(2,1)S(1)} all-to-all(bf16[4,16,2176]{2,1,0:T(8,128)(2,1)} %bitcast.60), channel_id=1, replica_groups={{0,1,2,3},{4,5,6,7},{8,9,10,11},{12,13,14,15},{16,17,18,19},{20,21,22,2..., dimensions={0} | all-to-all | bytes 557056 | tf_op jit(solution)/shard_map/all_to_all | solution.py:1188
  195.3 3.5 %all-to-all-start.6 = ((bf16[8,16,2176]{2,1,0:T(8,128)(2,1)}), bf16[8,16,2176]{2,1,0:T(8,128)(2,1)S(1)}, u32[]{:S(2)}, u32[]{:S(2)}) async-start(bf16[8,16,2176]{2,1,0:T(8,128)(2,1)} %bitcast.25), calls=%async_computation.6 | async-start | bytes 1114112 | tf_op jit(solution)/shard_map/all_to_all | solution.py:1196
  198.8 7.2 %shard_map.340 = (bf16[128,768]{1,0:T(8,128)(2,1)}, bf16[4608,128]{1,0:T(8,128)(2,1)}, f32[1,1536]{1,0:T(1,128)}, f32[2,128,384]{2,1,0:T(8,128)}) custom-call(s32[1]{0:T(128)} %bitcast.core.refs_0_.refs_1_, s32[1]{0:T(128)} %bitcast.1.refs_1_.refs_0_, bf16[1536,768]{1,0:T(8,128)(2,1)} %all-gather.4.cloned.1.call-done.refs_2_, bf16[1536,768]{1,0:T(8,128)(2,1)} %copy-done.11, ...), custom_call_target="tpu_custom_call" | custom-call | tf_op jit(solution)/shard_map/pallas_call | solution.py:92
  206.7 7.2 %all-to-all-start.8 = ((bf16[32,144,128]{2,1,0:T(8,128)(2,1)}), bf16[32,144,128]{2,1,0:T(8,128)(2,1)S(1)}, u32[]{:S(2)}, u32[]{:S(2)}) async-start(bf16[32,144,128]{2,1,0:T(8,128)(2,1)} %bitcast.55), calls=%async_computation.8 | async-start | bytes 2359296 | tf_op jit(solution)/shard_map/all_to_all | solution.py:1207
  214.0 22.9 %shard_map.342 = (bf16[1536,384]{1,0:T(8,128)(2,1)}, f32[128,768]{1,0:T(8,128)}, f32[8,768]{1,0:T(8,128)}) custom-call(s32[1]{0:T(128)} %bitcast.4.refs_1_.refs_0_, s32[1]{0:T(128)} %bitcast.core.refs_0_.refs_1_, bf16[1536,128]{1,0:T(8,128)(2,1)} %get-tuple-element.159.refs_2_, f32[24,1536]{1,0:T(8,128)} %get-tuple-element.129.par.refs_4_.refs_3_, ...), custom_call_target="tpu_custom_call" | custom-call | tf_op jit(solution)/shard_map/pallas_call | solution.py:92
  237.0 7.7 %all-to-all-start.7 = ((bf16[32,48,384]{2,1,0:T(8,128)(2,1)}), bf16[32,48,384]{2,1,0:T(8,128)(2,1)S(1)}, u32[]{:S(2)}, u32[]{:S(2)}) async-start(bf16[32,48,384]{2,1,0:T(8,128)(2,1)} %bitcast.54), calls=%async_computation.7 | async-start | bytes 2359296 | tf_op jit(solution)/shard_map/all_to_all | solution.py:1207
  245.2 2.8 copy-done
  248.0 1.9 copy-done.4
  249.9 2.0 shard_map.343
  252.8 1.5 collective-permute-start.8
  254.3 5.2 %collective-permute-done.8.beyond = f32[8,768]{1,0:T(8,128)S(1)} collective-permute-done((f32[8,768]{1,0:T(8,128)S(1)}, f32[8,768]{1,0:T(8,128)S(1)}, u32[]{:S(2)}, u32[]{:S(2)}) %collective-permute-start.8) | collective-permute-done | bytes 24608 | tf_op jit(solution)/shard_map/ppermute | solution.py:1499
  259.5 2.2 all-to-all-done.7.got
  261.7 2.8 copy-done.1
  265.9 4.1 %collective-permute-start.9 = (bf16[96,768]{1,0:T(8,128)(2,1)S(1)}, bf16[96,768]{1,0:T(8,128)(2,1)S(1)}, u32[]{:S(2)}, u32[]{:S(2)}) collective-permute-start(bf16[96,768]{1,0:T(8,128)(2,1)S(1)} %shard_map.345), channel_id=1, source_target_pairs={{0,32},{32,0},{64,96},{96,64},{1,33},{33,1},{65,97},{97,65},{2,34}... | collective-permute-start | bytes 442376 | tf_op jit(solution)/shard_map/ppermute | solution.py:1239
  271.0 2.8 collective-permute-start.10
  275.5 2.1 collective-permute-done.10.theirs
  277.6 3.2 %collective-permute-done.12.theirs_two = bf16[96,768]{1,0:T(8,128)(2,1)S(1)} collective-permute-done((bf16[96,768]{1,0:T(8,128)(2,1)S(1)}, bf16[96,768]{1,0:T(8,128)(2,1)S(1)}, u32[]{:S(2)}, u32[]{:S(2)}) %collective-permute-start.12) | collective-permute-done | bytes 147488 | tf_op jit(solution)/shard_map/ppermute | solution.py:1243
  280.8 2.6 shard_map.346
  (85 shorter events, 18.7 us)
Async XLA Ops:
  7.2 68.4 %all-gather.4.cloned.1.call-start = ((), (), s32[]{:S(2)}) async-start(), calls=%async_computation.9 | async-start | bytes 2506752 | tf_op jit(solution)/shard_map/all_gather | solution.py:1225
  8.8 4.5 %collective-permute-start = (bf16[48,768]{1,0:T(8,128)(2,1)}, bf16[48,768]{1,0:T(8,128)(2,1)S(1)}, u32[]{:S(2)}, u32[]{:S(2)}) collective-permute-start(bf16[48,768]{1,0:T(8,128)(2,1)} %shard_map.331), channel_id=1, source_target_pairs={{0,4},{1,5},{2,6},{3,7},{4,0},{5,1},{6,2},{7,3},{8,12},{9,13},{10,... | collective-permute-start | bytes 221192 | tf_op jit(solution)/shard_map/ppermute | solution.py:1213
  14.9 30.7 %all-to-all-start = ((bf16[32,48,512]{2,1,0:T(8,128)(2,1)}), bf16[32,48,512]{2,1,0:T(8,128)(2,1)S(1)}, u32[]{:S(2)}, u32[]{:S(2)}) async-start(bf16[32,48,512]{2,1,0:T(8,128)(2,1)} %bitcast.48), calls=%async_computation | async-start | bytes 3145728 | tf_op jit(solution)/shard_map/all_to_all | solution.py:1207
  26.1 15.5 %collective-permute-start.2 = (bf16[16,768]{1,0:T(8,128)(2,1)}, bf16[16,768]{1,0:T(8,128)(2,1)S(1)}, u32[]{:S(2)}, u32[]{:S(2)}) collective-permute-start(bf16[16,768]{1,0:T(8,128)(2,1)} %get-tuple-element.121), channel_id=1, source_target_pairs={{0,1},{1,2},{2,3},{3,4},{4,5},{5,6},{6,7},{7,8},{8,9},{9,10},{10,1... | collective-permute-start | bytes 73736 | tf_op jit(solution)/shard_map/ppermute | solution.py:1301
  41.5 10.2 %copy-start.20 = (bf16[16,768]{1,0:T(8,128)(2,1)}, bf16[16,768]{1,0:T(8,128)(2,1)S(1)}, u32[]{:S(2)}) copy-start(bf16[16,768]{1,0:T(8,128)(2,1)S(1)} %collective-permute-done.2.refs_2_.refs_18_) | copy-start | bytes 73732
  45.6 6.1 %copy-start.12 = (bf16[32,48,512]{2,1,0:T(8,128)(2,1)}, bf16[32,48,512]{2,1,0:T(8,128)(2,1)S(1)}, u32[]{:S(2)}) copy-start(bf16[32,48,512]{2,1,0:T(8,128)(2,1)S(1)} %all-to-all-done) | copy-start | bytes 4718596
  45.6 6.1 %collective-permute-start.3 = (bf16[1536,512]{1,0:T(8,128)(2,1)S(1)}, bf16[1536,512]{1,0:T(8,128)(2,1)S(1)}, u32[]{:S(2)}, u32[]{:S(2)}) collective-permute-start(bf16[1536,512]{1,0:T(8,128)(2,1)S(1)} %bitcast.45), channel_id=1, source_target_pairs={{0,32},{32,0},{64,96},{96,64},{1,33},{33,1},{65,97},{97,65},{2,34}... | collective-permute-start | bytes 4718600 | tf_op jit(solution)/shard_map/ppermute | solution.py:1239
  48.7 21.0 %collective-permute-start.1 = (bf16[128,768]{1,0:T(8,128)(2,1)}, bf16[128,768]{1,0:T(8,128)(2,1)S(1)}, u32[]{:S(2)}, u32[]{:S(2)}) collective-permute-start(bf16[128,768]{1,0:T(8,128)(2,1)} %get-tuple-element.119.refs_1_), channel_id=1, source_target_pairs={{0,4},{1,5},{2,6},{3,7},{4,0},{5,1},{6,2},{7,3},{8,12},{9,13},{10,... | collective-permute-start | bytes 589832 | tf_op jit(solution)/shard_map/ppermute | solution.py:1213
  51.7 1.2 copy-start.13
  52.9 30.2 %copy-start.18 = (bf16[128,768]{1,0:T(8,128)(2,1)S(1)}, bf16[128,768]{1,0:T(8,128)(2,1)}, u32[]{:S(2)}) copy-start(bf16[128,768]{1,0:T(8,128)(2,1)} %get-tuple-element.119.refs_1_) | copy-start | bytes 589828
  66.3 9.3 %all-to-all-start.1 = ((bf16[4,16,1792]{2,1,0:T(8,128)(2,1)}), bf16[4,16,1792]{2,1,0:T(8,128)(2,1)S(1)}, u32[]{:S(2)}, u32[]{:S(2)}) async-start(bf16[4,16,1792]{2,1,0:T(8,128)(2,1)} %bitcast.61), calls=%async_computation.1 | async-start | bytes 458752 | tf_op jit(solution)/shard_map/all_to_all | solution.py:1188
  75.6 14.8 %copy-start.6 = (bf16[4,16,1792]{2,1,0:T(8,128)(2,1)}, bf16[4,16,1792]{2,1,0:T(8,128)(2,1)S(1)}, u32[]{:S(2)}) copy-start(bf16[4,16,1792]{2,1,0:T(8,128)(2,1)S(1)} %all-to-all-done.1) | copy-start | bytes 688132
  75.6 8.2 %collective-permute-start.4 = (bf16[1536,768]{1,0:T(8,128)(2,1)}, bf16[1536,768]{1,0:T(8,128)(2,1)S(1)}, u32[]{:S(2)}, u32[]{:S(2)}) collective-permute-start(bf16[1536,768]{1,0:T(8,128)(2,1)} %all-gather.4.cloned.1.call-done.refs_2_), channel_id=1, source_target_pairs={{0,32},{32,0},{64,96},{96,64},{1,33},{33,1},{65,97},{97,65},{2,34}... | collective-permute-start | bytes 7077896 | tf_op jit(solution)/shard_map/ppermute | solution.py:1239
  78.8 13.0 %all-to-all-start.2 = ((bf16[8,16,1792]{2,1,0:T(8,128)(2,1)}), bf16[8,16,1792]{2,1,0:T(8,128)(2,1)S(1)}, u32[]{:S(2)}, u32[]{:S(2)}) async-start(bf16[8,16,1792]{2,1,0:T(8,128)(2,1)} %bitcast.10), calls=%async_computation.2 | async-start | bytes 917504 | tf_op jit(solution)/shard_map/all_to_all | solution.py:1196
  83.0 102.3 %all-gather.6.cloned.1.call-start = ((), (), s32[]{:S(2)}) async-start(), calls=%async_computation.10 | async-start | bytes 6684672 | tf_op jit(solution)/shard_map/all_gather | solution.py:1225
  83.9 1.4 copy-start.11
  128.2 4.8 %copy-start.15 = (bf16[64,16,512]{2,1,0:T(8,128)(2,1)}, bf16[64,16,512]{2,1,0:T(8,128)(2,1)S(1)}, u32[]{:S(2)}) copy-start(bf16[64,16,512]{2,1,0:T(8,128)(2,1)S(1)} %all_to_all.45) | copy-start | bytes 3145732
  128.2 4.8 %collective-permute-start.5 = (bf16[1024,512]{1,0:T(8,128)(2,1)S(1)}, bf16[1024,512]{1,0:T(8,128)(2,1)S(1)}, u32[]{:S(2)}, u32[]{:S(2)}) collective-permute-start(bf16[1024,512]{1,0:T(8,128)(2,1)S(1)} %bitcast.50), channel_id=1, source_target_pairs={{0,32},{32,0},{64,96},{96,64},{1,33},{33,1},{65,97},{97,65},{2,34}... | collective-permute-start | bytes 3145736 | tf_op jit(solution)/shard_map/ppermute | solution.py:1239
  133.0 1.0 copy-start.19
  145.9 3.0 %collective-permute-start.6 = (bf16[1024,512]{1,0:T(8,128)(2,1)}, bf16[1024,512]{1,0:T(8,128)(2,1)S(1)}, u32[]{:S(2)}, u32[]{:S(2)}) collective-permute-start(bf16[1024,512]{1,0:T(8,128)(2,1)} %get-tuple-element.144), channel_id=1, source_target_pairs={{0,32},{32,0},{64,96},{96,64},{1,33},{33,1},{65,97},{97,65},{2,34}... | collective-permute-start | bytes 3145736 | tf_op jit(solution)/shard_map/ppermute | solution.py:1239
  148.8 7.9 %copy-start.23 = (bf16[640,768]{1,0:T(8,128)(2,1)S(1)}, bf16[640,768]{1,0:T(8,128)(2,1)}, u32[]{:S(2)}) copy-start(bf16[640,768]{1,0:T(8,128)(2,1)} %get-tuple-element.147) | copy-start | bytes 2949124
  148.8 7.9 %copy-start.25 = (bf16[640,768]{1,0:T(8,128)(2,1)S(1)}, bf16[640,768]{1,0:T(8,128)(2,1)}, u32[]{:S(2)}) copy-start(bf16[640,768]{1,0:T(8,128)(2,1)} %get-tuple-element.148) | copy-start | bytes 2949124
  151.5 22.7 %all-to-all-start.4 = ((bf16[64,16,512]{2,1,0:T(8,128)(2,1)}), bf16[64,16,512]{2,1,0:T(8,128)(2,1)S(1)}, u32[]{:S(2)}, u32[]{:S(2)}) async-start(bf16[64,16,512]{2,1,0:T(8,128)(2,1)} %bitcast.18), calls=%async_computation.4 | async-start | bytes 2097152 | tf_op jit(solution)/shard_map/all_to_all | solution.py:1233
  156.4 88.8 %all-gather.8.cloned.1.call-start = ((), (), s32[]{:S(2)}) async-start(), calls=%async_computation.11 | async-start | bytes 3342336 | tf_op jit(solution)/shard_map/all_gather | solution.py:1225
  156.7 2.5 copy-start.24
  159.3 2.5 copy-start.21
  159.3 2.5 copy-start.22
  174.2 1.0 copy-start.14
  175.2 19.1 %copy-start.3 = (f32[24,1536]{1,0:T(8,128)S(1)}, f32[24,1536]{1,0:T(8,128)}, u32[]{:S(2)}) copy-start(f32[24,1536]{1,0:T(8,128)} %get-tuple-element.129.par.refs_4_.refs_3_) | copy-start | bytes 442372
  194.3 11.7 %copy-start.5 = (bf16[4,16,2176]{2,1,0:T(8,128)(2,1)}, bf16[4,16,2176]{2,1,0:T(8,128)(2,1)S(1)}, u32[]{:S(2)}) copy-start(bf16[4,16,2176]{2,1,0:T(8,128)(2,1)S(1)} %all_to_all.46) | copy-start | bytes 835588
  195.3 11.5 %all-to-all-start.6 = ((bf16[8,16,2176]{2,1,0:T(8,128)(2,1)}), bf16[8,16,2176]{2,1,0:T(8,128)(2,1)S(1)}, u32[]{:S(2)}, u32[]{:S(2)}) async-start(bf16[8,16,2176]{2,1,0:T(8,128)(2,1)} %bitcast.25), calls=%async_computation.6 | async-start | bytes 1114112 | tf_op jit(solution)/shard_map/all_to_all | solution.py:1196
  206.7 7.3 %copy-start.16 = (bf16[8,16,2176]{2,1,0:T(8,128)(2,1)}, bf16[8,16,2176]{2,1,0:T(8,128)(2,1)S(1)}, u32[]{:S(2)}) copy-start(bf16[8,16,2176]{2,1,0:T(8,128)(2,1)S(1)} %all-to-all-done.6) | copy-start | bytes 1671172
  206.7 30.2 %all-to-all-start.8 = ((bf16[32,144,128]{2,1,0:T(8,128)(2,1)}), bf16[32,144,128]{2,1,0:T(8,128)(2,1)S(1)}, u32[]{:S(2)}, u32[]{:S(2)}) async-start(bf16[32,144,128]{2,1,0:T(8,128)(2,1)} %bitcast.55), calls=%async_computation.8 | async-start | bytes 2359296 | tf_op jit(solution)/shard_map/all_to_all | solution.py:1207
  237.0 24.8 %all-to-all-start.7 = ((bf16[32,48,384]{2,1,0:T(8,128)(2,1)}), bf16[32,48,384]{2,1,0:T(8,128)(2,1)S(1)}, u32[]{:S(2)}, u32[]{:S(2)}) async-start(bf16[32,48,384]{2,1,0:T(8,128)(2,1)} %bitcast.54), calls=%async_computation.7 | async-start | bytes 2359296 | tf_op jit(solution)/shard_map/all_to_all | solution.py:1207
  245.2 2.8 copy-start
  248.0 1.9 copy-start.4
  249.9 2.9 %copy-start.26 = (f32[8,768]{1,0:T(8,128)S(1)}, f32[8,768]{1,0:T(8,128)}, u32[]{:S(2)}) copy-start(f32[8,768]{1,0:T(8,128)} %get-tuple-element.181) | copy-start | bytes 73732
  251.9 9.8 %collective-permute-start.7 = (bf16[48,768]{1,0:T(8,128)(2,1)S(1)}, bf16[48,768]{1,0:T(8,128)(2,1)S(1)}, u32[]{:S(2)}, u32[]{:S(2)}) collective-permute-start(bf16[48,768]{1,0:T(8,128)(2,1)S(1)} %get-tuple-element.180), channel_id=1, source_target_pairs={{0,4},{1,5},{2,6},{3,7},{4,0},{5,1},{6,2},{7,3},{8,12},{9,13},{10,... | collective-permute-start | bytes 221192 | tf_op jit(solution)/shard_map/ppermute | solution.py:1213
  252.8 6.7 %collective-permute-start.8 = (f32[8,768]{1,0:T(8,128)S(1)}, f32[8,768]{1,0:T(8,128)S(1)}, u32[]{:S(2)}, u32[]{:S(2)}) collective-permute-start(f32[8,768]{1,0:T(8,128)S(1)} %copy-done.26), channel_id=1, source_target_pairs={{1,0},{2,1},{3,2},{4,3},{5,4},{6,5},{7,6},{8,7},{9,8},{10,9},{11,1... | collective-permute-start | bytes 73736 | tf_op jit(solution)/shard_map/ppermute | solution.py:1499
  261.7 2.8 copy-start.1
  264.5 9.7 %copy-start.7 = (bf16[128,768]{1,0:T(8,128)(2,1)S(1)}, bf16[128,768]{1,0:T(8,128)(2,1)}, u32[]{:S(2)}) copy-start(bf16[128,768]{1,0:T(8,128)(2,1)} %get-tuple-element.138.refs_14_.refs_25_.hid) | copy-start | bytes 589828
  264.5 9.7 %copy-start.8 = (f32[128,768]{1,0:T(8,128)S(1)}, f32[128,768]{1,0:T(8,128)}, u32[]{:S(2)}) copy-start(f32[128,768]{1,0:T(8,128)} %get-tuple-element.183.mgrad) | copy-start | bytes 1179652
  264.5 9.7 %copy-start.9 = (f32[128,768]{1,0:T(8,128)S(1)}, f32[128,768]{1,0:T(8,128)}, u32[]{:S(2)}) copy-start(f32[128,768]{1,0:T(8,128)} %get-tuple-element.173.ngrad_in) | copy-start | bytes 1179652
  264.5 9.7 %copy-start.10 = (f32[768]{0:T(1024)S(1)}, f32[768]{0:T(1024)}, u32[]{:S(2)}) copy-start(f32[768]{0:T(1024)} %gain.3) | copy-start | bytes 9220
  265.9 5.1 %collective-permute-start.9 = (bf16[96,768]{1,0:T(8,128)(2,1)S(1)}, bf16[96,768]{1,0:T(8,128)(2,1)S(1)}, u32[]{:S(2)}, u32[]{:S(2)}) collective-permute-start(bf16[96,768]{1,0:T(8,128)(2,1)S(1)} %shard_map.345), channel_id=1, source_target_pairs={{0,32},{32,0},{64,96},{96,64},{1,33},{33,1},{65,97},{97,65},{2,34}... | collective-permute-start | bytes 442376 | tf_op jit(solution)/shard_map/ppermute | solution.py:1239
  270.0 3.8 %collective-permute-start.11 = (bf16[96,768]{1,0:T(8,128)(2,1)S(1)}, bf16[96,768]{1,0:T(8,128)(2,1)S(1)}, u32[]{:S(2)}, u32[]{:S(2)}) collective-permute-start(bf16[96,768]{1,0:T(8,128)(2,1)S(1)} %pad_maximum_fusion.2), channel_id=1, source_target_pairs={{0,32},{32,0},{64,96},{96,64},{1,33},{33,1},{65,97},{97,65},{2,34}... | collective-permute-start | bytes 442376 | tf_op jit(solution)/shard_map/ppermute | solution.py:1239
  271.0 6.7 %collective-permute-start.10 = (bf16[96,768]{1,0:T(8,128)(2,1)S(1)}, bf16[96,768]{1,0:T(8,128)(2,1)S(1)}, u32[]{:S(2)}, u32[]{:S(2)}) collective-permute-start(bf16[96,768]{1,0:T(8,128)(2,1)S(1)} %add_convert_fusion.2.ours), channel_id=1, source_target_pairs={{0,64},{64,0},{32,96},{96,32},{1,65},{65,1},{33,97},{97,33},{2,66}... | collective-permute-start | bytes 442376 | tf_op jit(solution)/shard_map/ppermute | solution.py:1243
  273.8 7.0 %collective-permute-start.12 = (bf16[96,768]{1,0:T(8,128)(2,1)S(1)}, bf16[96,768]{1,0:T(8,128)(2,1)S(1)}, u32[]{:S(2)}, u32[]{:S(2)}) collective-permute-start(bf16[96,768]{1,0:T(8,128)(2,1)S(1)} %add_convert_fusion.1.ours_two), channel_id=1, source_target_pairs={{0,64},{64,0},{32,96},{96,32},{1,65},{65,1},{33,97},{97,33},{2,66}... | collective-permute-start | bytes 442376 | tf_op jit(solution)/shard_map/ppermute | solution.py:1243
  (2 other events, 1.7 us)
Sparse Core Ops, SparseCore 0:
  15.0 58.6 all-gather.3
  92.0 70.3 all-gather.5
  185.4 59.7 all-gather.7
where the time goes:
time: 291 us; the launch traced here: 290 us
  Pallas kernels  97.3 us (33%)
  starting transfers between devices  64.3 us (22%)
  waiting for transfers between devices  54.5 us (19%)
  blocking collectives  33.3 us (11%)
  between operations  14.1 us (5%)
  local copies, waits for them, and re-layouts  13.8 us (5%)
  matrix products  7.57 us (3%)
  other arithmetic  5.2 us (2%)
    pallas_call x16, Pallas kernels, call(): pl.pallas_call(staged if moving else kernel, out_shape=out_shapes, in_spe...  97.3 us
    all_to_all x1, blocking collectives, exchange_sides(): lax.all_to_all(values, ('dp', 'wide'), split_axis=0, concat_axis=0, tiled...  24.2 us
    all_to_all x3, starting transfers between devices, exchange_channels(): lax.all_to_all(values, 'wide', split_axis=0, concat_axis=0, tiled=True, a...  23.8 us
    unnamed x54, local copies, waits for them, and re-layouts  13.8 us
    ppermute x1, waiting for transfers between devices, body(): halo = lax.ppermute(tail, 'wide', [(i, i + 1) for i in range(places - 1)])  12.3 us
    ppermute x6, starting transfers between devices, other_core(): return lax.ppermute(values, 'dp', [(0, 1), (1, 0), (2, 3), (3, 2)])  11.6 us
    all_to_all x1, waiting for transfers between devices, exchange_sides(): lax.all_to_all(values, ('dp', 'wide'), split_axis=0, concat_axis=0, tiled...  9.89 us
    all_to_all x1, blocking collectives, exchange_near(): lax.all_to_all(blocks, 'wide', split_axis=0, concat_axis=0, tiled=True, a...  9.05 us
  transfers between devices with their start and end apart: 23, of which 15 were waited for; matrix products, arithmetic and copies ran while one was open for 4% of the time, Pallas kernels for 32%

commit v1 on v0

--- a/solution.py
+++ b/solution.py
@@ -709,45 +709,48 @@
 
 
 def expert_kernel(
-    moves, mine, other, w_gate, w_up, w_down, in_o, grad_o, act_o, gate_o, up_o, ours_o, theirs_o,
+    moves, arrived, w_gate, w_up, w_down, w_gate_two, w_up_two, w_down_two, kept_o, sent_o, back_o,
     *, stride, capacity
 ):
     blocks = 16
     hots = slot_rows(stride, capacity, blocks)
     size = capacity * blocks
-    groups = mine.shape[0] // (stride * blocks)
-    for part, arrived in enumerate((mine, other)):
-        for group in range(groups):
-            rows = unpack(arrived[group * stride * blocks : (group + 1) * stride * blocks, :], hots)
-            at = (part * groups + group) * size
-            in_o[at : at + size, :] = rows[:size, :]
-            grad_o[at : at + size, :] = rows[size:, :]
-    moves.need(w_gate)
-    gate_in = dot_nn(in_o[...], w_gate[...])
-    moves.need(w_up)
-    up_in = dot_nn(in_o[...], w_up[...])
-    moves.done(in_o)
-    sig = jax.nn.sigmoid(gate_in)
-    silu = gate_in * sig
-    act = (silu * up_in).astype(bf16)
-    act_o[...] = act
-    moves.need(w_down)
-    outputs = dot_nn(act, w_down[...])
-    act_grad = dot_nt(grad_o[...], w_down[...])
-    moves.done(grad_o, act_o)
-    gate_grad = (act_grad * up_in * sig * (1.0 + gate_in * (1.0 - sig))).astype(bf16)
-    up_grad = (act_grad * silu).astype(bf16)
-    gate_o[...] = gate_grad
-    up_o[...] = up_grad
-    moves.done(gate_o, up_o)
-    total = dot_nt(gate_grad, w_gate[...]) + dot_nt(up_grad, w_up[...])
-    for part, out in ((1, theirs_o), (0, ours_o)):
-        for group in range(groups):
-            at = (part * groups + group) * size
-            rows = jnp.concatenate([outputs[at : at + size, :], total[at : at + size, :]], axis=0)
-            packed = pack(rows.astype(bf16), hots)
-            out[group * stride * blocks : (group + 1) * stride * blocks, :] = packed.astype(out.dtype)
+    groups = arrived.shape[0] // (stride * blocks)
+    slots = kept_o.shape[0] // 5
+    for group in range(groups):
+        rows = unpack(arrived[group * stride * blocks : (group + 1) * stride * blocks, :], hots)
+        at = group * size
+        kept_o[at : at + size, :] = rows[:size, :]
+        kept_o[slots + at : slots + at + size, :] = rows[size:, :]
+    sent_o[: 2 * slots, :] = kept_o[: 2 * slots, :]
+    inputs = kept_o[:slots, :]
+    grads = kept_o[slots : 2 * slots, :]
+    outputs = 0.0
+    total = 0.0
+    weights = ((sent_o, w_gate_two, w_up_two, w_down_two), (kept_o, w_gate, w_up, w_down))
+    for out, gate_weight, up_weight, down_weight in weights[::-1]:
+        moves.need(gate_weight)
+        gate_in = dot_nn(inputs, gate_weight[...])
+        moves.need(up_weight)
+        up_in = dot_nn(inputs, up_weight[...])
+        sig = jax.nn.sigmoid(gate_in)
+        silu = gate_in * sig
+        act = (silu * up_in).astype(bf16)
+        out[2 * slots : 3 * slots, :] = act
+        moves.need(down_weight)
+        outputs = outputs + dot_nn(act, down_weight[...])
+        act_grad = dot_nt(grads, down_weight[...])
+        gate_grad = (act_grad * up_in * sig * (1.0 + gate_in * (1.0 - sig))).astype(bf16)
+        up_grad = (act_grad * silu).astype(bf16)
+        out[3 * slots : 4 * slots, :] = gate_grad
+        out[4 * slots :, :] = up_grad
         moves.done(out)
+        total = total + dot_nt(gate_grad, gate_weight[...]) + dot_nt(up_grad, up_weight[...])
+    for group in range(groups):
+        at = group * size
+        rows = jnp.concatenate([outputs[at : at + size, :], total[at : at + size, :]], axis=0)
+        packed = pack(rows.astype(bf16), hots).astype(bf16)
+        back_o[group * stride * blocks : (group + 1) * stride * blocks, :] = packed
 
 
 def aside_kernel(
@@ -1277,6 +1280,7 @@
         (core, in_x.T, x_proj, dt_proj, conv_w, conv_b, dt_bias, skip_d, a_log),
         smem=1,
     )[0]
+    w_gate_two, w_up_two, w_down_two = (other_core(w[0]) for w in (w_gate, w_up, w_down))
     pay_one, hidden, cotangent, routes, seg_lengths = lax.optimization_barrier(
         (pay_one, hidden, cotangent, routes, seg_lengths)
     )
@@ -1392,22 +1396,27 @@
     )
     arrived = exchange_sides(send.reshape(2 * experts, stride, -1)).reshape(send.shape)
     slots = 2 * places * capacity
-    theirs_in = other_core(arrived)
-    expert_in, grad_rows, hidden_act, gate_grad, up_grad, ours, theirs = call(
+    kept, sent, back = call(
         partial(expert_kernel, stride=stride, capacity=capacity),
-        [shape((2 * slots, model), bf16)] * 2
-        + [shape((2 * slots, w_gate.shape[2]), bf16)] * 3
-        + [shape(send.shape, bf16)] * 2,
+        [shape((5 * slots, model), bf16)] * 2 + [shape(send.shape, bf16)],
         [],
-        (arrived, theirs_in, w_gate[0], w_up[0], w_down[0]),
-        late=(2, 3, 4),
-        early=(0, 1, 2, 3, 4, 5, 6),
-    )
-    back = (ours.astype(f32) + other_core(theirs).astype(f32)).astype(bf16)
+        (arrived, w_gate[0], w_up[0], w_down[0], w_gate_two, w_up_two, w_down_two),
+        late=(1, 2, 3, 4, 5, 6),
+        early=(0, 1, 2),
+    )
     back = exchange_sides(back.reshape(2 * experts, stride, -1)).reshape(send.shape)
-    grad_w_down = dot_tn(hidden_act, grad_rows)[None]
-    grad_w_gate = dot_tn(expert_in, gate_grad)[None]
-    grad_w_up = dot_tn(expert_in, up_grad)[None]
+    given = other_core(sent)
+
+    def both_cores(left, right):
+        total = 0.0
+        for part in (kept, given):
+            rows_left = part[left * slots : (left + 1) * slots]
+            total = total + dot_tn(rows_left, part[right * slots : (right + 1) * slots])
+        return total[None]
+
+    grad_w_down = both_cores(2, 1)
+    grad_w_gate = both_cores(0, 3)
+    grad_w_up = both_cores(0, 4)
     back, grad_w_down, grad_w_gate, grad_w_up = lax.optimization_barrier(
         (back, grad_w_down, grad_w_gate, grad_w_up)
     )

time: 291 us -> 285 us (0.979)
  blocking collectives: 33.3 us -> 9.05 us
  waiting for transfers between devices: 54.5 us -> 62.8 us
  starting transfers between devices: 64.3 us -> 72.3 us
  matrix products: 7.57 us -> 12.8 us
    all_to_all x1 -> x0, blocking collectives: 24.2 us -> none  [exchange_sides(): lax.all_to_all(values, ('dp', 'wide'), split_axis=0, concat_axis=0, tiled...]
    all_to_all x1 -> x2, waiting for transfers between devices: 9.89 us -> 23 us  [exchange_sides(): lax.all_to_all(values, ('dp', 'wide'), split_axis=0, concat_axis=0, tiled...]
    all_to_all x1 -> x2, starting transfers between devices: 4.87 us -> 10.9 us  [exchange_sides(): lax.all_to_all(values, ('dp', 'wide'), split_axis=0, concat_axis=0, tiled...]
    dot_general x3 -> x6, matrix products: 7.57 us -> 12.8 us  [dot_tn(): lax.dot_general(left, right, (((0,), (0,)), ((), ())), preferred_element_...]
    ppermute x6 -> x8, waiting for transfers between devices: 6.89 us -> 2.11 us  [other_core(): return lax.ppermute(values, 'dp', [(0, 1), (1, 0), (2, 3), (3, 2)])]
    unnamed x54 -> x48, local copies, waits for them, and re-layouts: 13.8 us -> 13 us
    ppermute x6 -> x8, starting transfers between devices: 11.6 us -> 12.4 us  [other_core(): return lax.ppermute(values, 'dp', [(0, 1), (1, 0), (2, 3), (3, 2)])]
  transfers between devices with their start and end apart: 23 -> 26, of which waited for: 15 -> 13; matrix products, arithmetic and copies ran while one was open for 4% -> 5% of each run, Pallas kernels for 32% -> 32%
where the time goes in v1:
time: 285 us; the launch traced here: 284 us
  Pallas kernels  97.2 us (34%)
  starting transfers between devices  72.3 us (25%)
  waiting for transfers between devices  62.8 us (22%)
  between operations  14.1 us (5%)
  local copies, waits for them, and re-layouts  13 us (5%)
  matrix products  12.8 us (4%)
  blocking collectives  9.05 us (3%)
    pallas_call x16, Pallas kernels, call(): pl.pallas_call(staged if moving else kernel, out_shape=out_shapes, in_spe...  97.2 us
    all_to_all x3, starting transfers between devices, exchange_channels(): lax.all_to_all(values, 'wide', split_axis=0, concat_axis=0, tiled=True, a...  24.3 us
    all_to_all x2, waiting for transfers between devices, exchange_sides(): lax.all_to_all(values, ('dp', 'wide'), split_axis=0, concat_axis=0, tiled...  23 us
    unnamed x48, local copies, waits for them, and re-layouts  13 us
    dot_general x6, matrix products, dot_tn(): lax.dot_general(left, right, (((0,), (0,)), ((), ())), preferred_element_...  12.8 us
    ppermute x8, starting transfers between devices, other_core(): return lax.ppermute(values, 'dp', [(0, 1), (1, 0), (2, 3), (3, 2)])  12.4 us
    ppermute x1, waiting for transfers between devices, body(): halo = lax.ppermute(tail, 'wide', [(i, i + 1) for i in range(places - 1)])  12.3 us
    all_to_all x2, starting transfers between devices, exchange_sides(): lax.all_to_all(values, ('dp', 'wide'), split_axis=0, concat_axis=0, tiled...  10.9 us
  transfers between devices with their start and end apart: 26, of which 13 were waited for; matrix products, arithmetic and copies ran while one was open for 5% of the time, Pallas kernels for 32%

profile of v1, /device:TPU:1, one launch (start us, length us, event | category | flops | bytes accessed | tf_op | source)
XLA Modules:
  0.0 283.7 jit_solution(2388832263884734788)
XLA Ops:
  7.2 1.6 shard_map.331
  8.8 2.0 collective-permute-start
  10.8 2.4 shard_map.332
  14.9 8.8 %all-to-all-start = ((bf16[32,48,512]{2,1,0:T(8,128)(2,1)}), bf16[32,48,512]{2,1,0:T(8,128)(2,1)S(1)}, u32[]{:S(2)}, u32[]{:S(2)}) async-start(bf16[32,48,512]{2,1,0:T(8,128)(2,1)} %bitcast.42), calls=%async_computation | async-start | bytes 3145728 | tf_op jit(solution)/shard_map/all_to_all | solution.py:1210
  23.7 2.4 shard_map.333
  26.1 3.1 %collective-permute-start.2 = (bf16[16,768]{1,0:T(8,128)(2,1)}, bf16[16,768]{1,0:T(8,128)(2,1)S(1)}, u32[]{:S(2)}, u32[]{:S(2)}) collective-permute-start(bf16[16,768]{1,0:T(8,128)(2,1)} %get-tuple-element.117), channel_id=1, source_target_pairs={{0,1},{1,2},{2,3},{3,4},{4,5},{5,6},{6,7},{7,8},{8,9},{9,10},{10,1... | collective-permute-start | bytes 73736 | tf_op jit(solution)/shard_map/ppermute | solution.py:1305
  29.2 12.3 %collective-permute-done.2.refs_2_.refs_18_ = bf16[16,768]{1,0:T(8,128)(2,1)S(1)} collective-permute-done((bf16[16,768]{1,0:T(8,128)(2,1)}, bf16[16,768]{1,0:T(8,128)(2,1)S(1)}, u32[]{:S(2)}, u32[]{:S(2)}) %collective-permute-start.2) | collective-permute-done | bytes 24608 | tf_op jit(solution)/shard_map/ppermute | solution.py:1305
  41.5 4.0 %all-to-all-done = bf16[32,48,512]{2,1,0:T(8,128)(2,1)S(1)} async-done(((bf16[32,48,512]{2,1,0:T(8,128)(2,1)}), bf16[32,48,512]{2,1,0:T(8,128)(2,1)S(1)}, u32[]{:S(2)}, u32[]{:S(2)}) %all-to-all-start) | async-done | bytes 1572896 | tf_op jit(solution)/shard_map/all_to_all | solution.py:1210
  45.6 3.1 %collective-permute-start.3 = (bf16[1536,512]{1,0:T(8,128)(2,1)S(1)}, bf16[1536,512]{1,0:T(8,128)(2,1)S(1)}, u32[]{:S(2)}, u32[]{:S(2)}) collective-permute-start(bf16[1536,512]{1,0:T(8,128)(2,1)S(1)} %bitcast.39), channel_id=1, source_target_pairs={{0,32},{32,0},{64,96},{96,64},{1,33},{33,1},{65,97},{97,65},{2,34}... | collective-permute-start | bytes 4718600 | tf_op jit(solution)/shard_map/ppermute | solution.py:1242
  48.7 1.8 collective-permute-start.1
  52.9 13.4 %shard_map.334 = (f32[152,1536]{1,0:T(8,128)}, f32[128,1536]{1,0:T(8,128)}, f32[128,1536]{1,0:T(8,128)}, f32[128,1536]{1,0:T(8,128)}, f32[128,128]{1,0:T(8,128)}...) custom-call(s32[1]{0:T(128)} %bitcast.core.refs_0_.refs_1_, ...), custom_call_target="tpu_custom_call" | custom-call | tf_op jit(solution)/shard_map/pallas_call | solution.py:92
  66.3 3.4 %all-to-all-start.1 = ((bf16[4,16,1792]{2,1,0:T(8,128)(2,1)}), bf16[4,16,1792]{2,1,0:T(8,128)(2,1)S(1)}, u32[]{:S(2)}, u32[]{:S(2)}) async-start(bf16[4,16,1792]{2,1,0:T(8,128)(2,1)} %bitcast.58), calls=%async_computation.1 | async-start | bytes 458752 | tf_op jit(solution)/shard_map/all_to_all | solution.py:1191
  69.7 5.9 %all-to-all-done.1 = bf16[4,16,1792]{2,1,0:T(8,128)(2,1)S(1)} async-done(((bf16[4,16,1792]{2,1,0:T(8,128)(2,1)}), bf16[4,16,1792]{2,1,0:T(8,128)(2,1)S(1)}, u32[]{:S(2)}, u32[]{:S(2)}) %all-to-all-start.1) | async-done | bytes 229408 | tf_op jit(solution)/shard_map/all_to_all | solution.py:1191
  78.8 4.2 %all-to-all-start.2 = ((bf16[8,16,1792]{2,1,0:T(8,128)(2,1)}), bf16[8,16,1792]{2,1,0:T(8,128)(2,1)S(1)}, u32[]{:S(2)}, u32[]{:S(2)}) async-start(bf16[8,16,1792]{2,1,0:T(8,128)(2,1)} %bitcast.10), calls=%async_computation.2 | async-start | bytes 917504 | tf_op jit(solution)/shard_map/all_to_all | solution.py:1199
  85.3 5.1 %shard_map.336.refs_19_.refs_8_.refs_6_ = f32[128,1536]{1,0:T(8,128)} custom-call(s32[1]{0:T(128)} %bitcast.core.refs_0_.refs_1_, bf16[128,768]{1,0:T(8,128)(2,1)} %get-tuple-element.115.refs_1_, bf16[1536,768]{1,0:T(8,128)(2,1)} %all-gather.4.cloned.1.call-done.refs_2_, bf16[1536,768]{1,0:T(8,128)(2,1)} %copy-done.11), custom_call_target="tpu_custom_call" | custom-call | tf_op jit(solution)/shard_map/pallas_call | solution.py:92
  90.4 1.5 all-to-all-done.2
  91.9 1.6 collective-permute-start.5
  94.0 11.4 %shard_map.337 = (f32[128,1536]{1,0:T(8,128)}, bf16[1024,512]{1,0:T(8,128)(2,1)}, f32[128,768]{1,0:T(8,128)}, bf16[128,768]{1,0:T(8,128)(2,1)}, f32[128,32]{1,0:...) custom-call(s32[1]{0:T(128)} %bitcast.core.refs_0_.refs_1_, ...), custom_call_target="tpu_custom_call" | custom-call | tf_op jit(solution)/shard_map/pallas_call | solution.py:92
  105.3 6.3 %all-to-all-start.3 = ((bf16[64,16,512]{2,1,0:T(8,128)(2,1)}), bf16[64,16,512]{2,1,0:T(8,128)(2,1)S(1)}, u32[]{:S(2)}, u32[]{:S(2)}) async-start(bf16[64,16,512]{2,1,0:T(8,128)(2,1)} %bitcast.56), calls=%async_computation.3 | async-start | bytes 2097152 | tf_op jit(solution)/shard_map/all_to_all | solution.py:1236
  111.7 17.8 %all-to-all-done.3 = bf16[64,16,512]{2,1,0:T(8,128)(2,1)S(1)} async-done(((bf16[64,16,512]{2,1,0:T(8,128)(2,1)}), bf16[64,16,512]{2,1,0:T(8,128)(2,1)S(1)}, u32[]{:S(2)}, u32[]{:S(2)}) %all-to-all-start.3) | async-done | bytes 1048608 | tf_op jit(solution)/shard_map/all_to_all | solution.py:1236
  130.4 11.6 %shard_map.338 = (bf16[1600,768]{1,0:T(8,128)(2,1)}, bf16[1600,768]{1,0:T(8,128)(2,1)}, bf16[1024,512]{1,0:T(8,128)(2,1)}) custom-call(bf16[1024,512]{1,0:T(8,128)(2,1)} %bitcast.44, bf16[768,768]{1,0:T(8,128)(2,1)} %bitcast.50, bf16[768,768]{1,0:T(8,128)(2,1)} %bitcast.52, bf16[768,768]{1,0:T(8,128)(2,1)} %bitcast.54, bf16[768,768]{1,0:T(8,128)(2,1)} %copy-done.20, ...), custom_call_target="tpu_custom_call" | custom-call | tf_op jit(solution)/shard_map/pallas_call | solution.py:92
  142.1 1.8 collective-permute-start.8
  143.8 4.7 %all-to-all-start.4 = ((bf16[64,16,512]{2,1,0:T(8,128)(2,1)}), bf16[64,16,512]{2,1,0:T(8,128)(2,1)S(1)}, u32[]{:S(2)}, u32[]{:S(2)}) async-start(bf16[64,16,512]{2,1,0:T(8,128)(2,1)} %bitcast.55), calls=%async_computation.4 | async-start | bytes 2097152 | tf_op jit(solution)/shard_map/all_to_all | solution.py:1236
  148.8 2.0 fusion.4
  150.8 2.1 fusion.2
  153.0 2.2 add_bitcast_fusion.2
  155.2 2.2 add_bitcast_fusion.1
  157.4 2.0 fusion
  159.4 2.2 add_bitcast_fusion
  161.6 5.2 %all-to-all-done.4 = bf16[64,16,512]{2,1,0:T(8,128)(2,1)S(1)} async-done(((bf16[64,16,512]{2,1,0:T(8,128)(2,1)}), bf16[64,16,512]{2,1,0:T(8,128)(2,1)S(1)}, u32[]{:S(2)}, u32[]{:S(2)}) %all-to-all-start.4) | async-done | bytes 1048608 | tf_op jit(solution)/shard_map/all_to_all | solution.py:1236
  167.8 10.0 %shard_map.339 = (f32[128,768]{1,0:T(8,128)}, bf16[128,768]{1,0:T(8,128)(2,1)}, f32[128,768]{1,0:T(8,128)}, f32[128,1536]{1,0:T(8,128)}, f32[128,1536]{1,0:T(8,1...) custom-call(s32[1]{0:T(128)} %bitcast.core.refs_0_.refs_1_, bf16[1024,512]{1,0:T(8,128)(2,1)} %bitcast.43, ...), custom_call_target="tpu_custom_call" | custom-call | tf_op jit(solution)/shard_map/pallas_call | solution.py:92
  177.9 9.0 %all_to_all.45 = bf16[4,16,2176]{2,1,0:T(8,128)(2,1)S(1)} all-to-all(bf16[4,16,2176]{2,1,0:T(8,128)(2,1)} %bitcast.57), channel_id=1, replica_groups={{0,1,2,3},{4,5,6,7},{8,9,10,11},{12,13,14,15},{16,17,18,19},{20,21,22,2..., dimensions={0} | all-to-all | bytes 557056 | tf_op jit(solution)/shard_map/all_to_all | solution.py:1191
  187.9 3.7 %all-to-all-start.6 = ((bf16[8,16,2176]{2,1,0:T(8,128)(2,1)}), bf16[8,16,2176]{2,1,0:T(8,128)(2,1)S(1)}, u32[]{:S(2)}, u32[]{:S(2)}) async-start(bf16[8,16,2176]{2,1,0:T(8,128)(2,1)} %bitcast.25), calls=%async_computation.6 | async-start | bytes 1114112 | tf_op jit(solution)/shard_map/all_to_all | solution.py:1199
  191.6 7.2 %shard_map.340 = (bf16[128,768]{1,0:T(8,128)(2,1)}, bf16[4608,128]{1,0:T(8,128)(2,1)}, f32[1,1536]{1,0:T(1,128)}, f32[2,128,384]{2,1,0:T(8,128)}) custom-call(s32[1]{0:T(128)} %bitcast.core.refs_0_.refs_1_, s32[1]{0:T(128)} %bitcast.1.refs_1_.refs_0_, bf16[1536,768]{1,0:T(8,128)(2,1)} %all-gather.4.cloned.1.call-done.refs_2_, bf16[1536,768]{1,0:T(8,128)(2,1)} %copy-done.11, ...), custom_call_target="tpu_custom_call" | custom-call | tf_op jit(solution)/shard_map/pallas_call | solution.py:92
  200.0 7.6 %all-to-all-start.8 = ((bf16[32,144,128]{2,1,0:T(8,128)(2,1)}), bf16[32,144,128]{2,1,0:T(8,128)(2,1)S(1)}, u32[]{:S(2)}, u32[]{:S(2)}) async-start(bf16[32,144,128]{2,1,0:T(8,128)(2,1)} %bitcast.48), calls=%async_computation.8 | async-start | bytes 2359296 | tf_op jit(solution)/shard_map/all_to_all | solution.py:1210
  207.7 23.2 %shard_map.342 = (bf16[1536,384]{1,0:T(8,128)(2,1)}, f32[128,768]{1,0:T(8,128)}, f32[8,768]{1,0:T(8,128)}) custom-call(s32[1]{0:T(128)} %bitcast.4.refs_1_.refs_0_, s32[1]{0:T(128)} %bitcast.core.refs_0_.refs_1_, bf16[1536,128]{1,0:T(8,128)(2,1)} %get-tuple-element.151.refs_2_, f32[24,1536]{1,0:T(8,128)} %get-tuple-element.125.par.refs_4_.refs_3_, ...), custom_call_target="tpu_custom_call" | custom-call | tf_op jit(solution)/shard_map/pallas_call | solution.py:92
  230.9 7.9 %all-to-all-start.7 = ((bf16[32,48,384]{2,1,0:T(8,128)(2,1)}), bf16[32,48,384]{2,1,0:T(8,128)(2,1)S(1)}, u32[]{:S(2)}, u32[]{:S(2)}) async-start(bf16[32,48,384]{2,1,0:T(8,128)(2,1)} %bitcast.47), calls=%async_computation.7 | async-start | bytes 2359296 | tf_op jit(solution)/shard_map/all_to_all | solution.py:1210
  238.8 2.8 copy-done
  241.6 1.9 copy-done.4
  243.5 2.0 shard_map.343
  247.9 5.2 %collective-permute-done.10.beyond = f32[8,768]{1,0:T(8,128)S(1)} collective-permute-done((f32[8,768]{1,0:T(8,128)S(1)}, f32[8,768]{1,0:T(8,128)S(1)}, u32[]{:S(2)}, u32[]{:S(2)}) %collective-permute-start.10) | collective-permute-done | bytes 24608 | tf_op jit(solution)/shard_map/ppermute | solution.py:1508
  253.1 2.6 all-to-all-done.7.got
  255.7 2.8 copy-done.1
  259.8 3.9 %collective-permute-start.11 = (bf16[96,768]{1,0:T(8,128)(2,1)S(1)}, bf16[96,768]{1,0:T(8,128)(2,1)S(1)}, u32[]{:S(2)}, u32[]{:S(2)}) collective-permute-start(bf16[96,768]{1,0:T(8,128)(2,1)S(1)} %shard_map.345), channel_id=1, source_target_pairs={{0,32},{32,0},{64,96},{96,64},{1,33},{33,1},{65,97},{97,65},{2,34}... | collective-permute-start | bytes 442376 | tf_op jit(solution)/shard_map/ppermute | solution.py:1242
  264.8 3.3 %collective-permute-start.12 = (bf16[96,768]{1,0:T(8,128)(2,1)S(1)}, bf16[96,768]{1,0:T(8,128)(2,1)S(1)}, u32[]{:S(2)}, u32[]{:S(2)}) collective-permute-start(bf16[96,768]{1,0:T(8,128)(2,1)S(1)} %add_convert_fusion.1.ours), channel_id=1, source_target_pairs={{0,64},{64,0},{32,96},{96,32},{1,65},{65,1},{33,97},{97,33},{2,66}... | collective-permute-start | bytes 442376 | tf_op jit(solution)/shard_map/ppermute | solution.py:1246
  269.9 2.2 collective-permute-done.12.theirs
  272.0 2.6 collective-permute-done.14.theirs_two
  274.6 2.6 shard_map.346
  (86 shorter events, 21.0 us)
Async XLA Ops:
  7.2 68.4 %all-gather.4.cloned.1.call-start = ((), (), s32[]{:S(2)}) async-start(), calls=%async_computation.9 | async-start | bytes 2506752 | tf_op jit(solution)/shard_map/all_gather | solution.py:1228
  8.8 4.5 %collective-permute-start = (bf16[48,768]{1,0:T(8,128)(2,1)}, bf16[48,768]{1,0:T(8,128)(2,1)S(1)}, u32[]{:S(2)}, u32[]{:S(2)}) collective-permute-start(bf16[48,768]{1,0:T(8,128)(2,1)} %shard_map.331), channel_id=1, source_target_pairs={{0,4},{1,5},{2,6},{3,7},{4,0},{5,1},{6,2},{7,3},{8,12},{9,13},{10,... | collective-permute-start | bytes 221192 | tf_op jit(solution)/shard_map/ppermute | solution.py:1216
  14.9 30.7 %all-to-all-start = ((bf16[32,48,512]{2,1,0:T(8,128)(2,1)}), bf16[32,48,512]{2,1,0:T(8,128)(2,1)S(1)}, u32[]{:S(2)}, u32[]{:S(2)}) async-start(bf16[32,48,512]{2,1,0:T(8,128)(2,1)} %bitcast.42), calls=%async_computation | async-start | bytes 3145728 | tf_op jit(solution)/shard_map/all_to_all | solution.py:1210
  26.1 15.5 %collective-permute-start.2 = (bf16[16,768]{1,0:T(8,128)(2,1)}, bf16[16,768]{1,0:T(8,128)(2,1)S(1)}, u32[]{:S(2)}, u32[]{:S(2)}) collective-permute-start(bf16[16,768]{1,0:T(8,128)(2,1)} %get-tuple-element.117), channel_id=1, source_target_pairs={{0,1},{1,2},{2,3},{3,4},{4,5},{5,6},{6,7},{7,8},{8,9},{9,10},{10,1... | collective-permute-start | bytes 73736 | tf_op jit(solution)/shard_map/ppermute | solution.py:1305
  41.5 10.2 %copy-start.22 = (bf16[16,768]{1,0:T(8,128)(2,1)}, bf16[16,768]{1,0:T(8,128)(2,1)S(1)}, u32[]{:S(2)}) copy-start(bf16[16,768]{1,0:T(8,128)(2,1)S(1)} %collective-permute-done.2.refs_2_.refs_18_) | copy-start | bytes 73732
  45.6 6.1 %copy-start.12 = (bf16[32,48,512]{2,1,0:T(8,128)(2,1)}, bf16[32,48,512]{2,1,0:T(8,128)(2,1)S(1)}, u32[]{:S(2)}) copy-start(bf16[32,48,512]{2,1,0:T(8,128)(2,1)S(1)} %all-to-all-done) | copy-start | bytes 4718596
  45.6 6.1 %collective-permute-start.3 = (bf16[1536,512]{1,0:T(8,128)(2,1)S(1)}, bf16[1536,512]{1,0:T(8,128)(2,1)S(1)}, u32[]{:S(2)}, u32[]{:S(2)}) collective-permute-start(bf16[1536,512]{1,0:T(8,128)(2,1)S(1)} %bitcast.39), channel_id=1, source_target_pairs={{0,32},{32,0},{64,96},{96,64},{1,33},{33,1},{65,97},{97,65},{2,34}... | collective-permute-start | bytes 4718600 | tf_op jit(solution)/shard_map/ppermute | solution.py:1242
  48.7 21.0 %collective-permute-start.1 = (bf16[128,768]{1,0:T(8,128)(2,1)}, bf16[128,768]{1,0:T(8,128)(2,1)S(1)}, u32[]{:S(2)}, u32[]{:S(2)}) collective-permute-start(bf16[128,768]{1,0:T(8,128)(2,1)} %get-tuple-element.115.refs_1_), channel_id=1, source_target_pairs={{0,4},{1,5},{2,6},{3,7},{4,0},{5,1},{6,2},{7,3},{8,12},{9,13},{10,... | collective-permute-start | bytes 589832 | tf_op jit(solution)/shard_map/ppermute | solution.py:1216
  51.7 1.2 copy-start.13
  52.9 30.2 %copy-start.19 = (bf16[128,768]{1,0:T(8,128)(2,1)S(1)}, bf16[128,768]{1,0:T(8,128)(2,1)}, u32[]{:S(2)}) copy-start(bf16[128,768]{1,0:T(8,128)(2,1)} %get-tuple-element.115.refs_1_) | copy-start | bytes 589828
  66.3 9.3 %all-to-all-start.1 = ((bf16[4,16,1792]{2,1,0:T(8,128)(2,1)}), bf16[4,16,1792]{2,1,0:T(8,128)(2,1)S(1)}, u32[]{:S(2)}, u32[]{:S(2)}) async-start(bf16[4,16,1792]{2,1,0:T(8,128)(2,1)} %bitcast.58), calls=%async_computation.1 | async-start | bytes 458752 | tf_op jit(solution)/shard_map/all_to_all | solution.py:1191
  75.6 14.8 %copy-start.6 = (bf16[4,16,1792]{2,1,0:T(8,128)(2,1)}, bf16[4,16,1792]{2,1,0:T(8,128)(2,1)S(1)}, u32[]{:S(2)}) copy-start(bf16[4,16,1792]{2,1,0:T(8,128)(2,1)S(1)} %all-to-all-done.1) | copy-start | bytes 688132
  75.6 8.3 %collective-permute-start.4 = (bf16[1536,768]{1,0:T(8,128)(2,1)}, bf16[1536,768]{1,0:T(8,128)(2,1)S(1)}, u32[]{:S(2)}, u32[]{:S(2)}) collective-permute-start(bf16[1536,768]{1,0:T(8,128)(2,1)} %all-gather.4.cloned.1.call-done.refs_2_), channel_id=1, source_target_pairs={{0,32},{32,0},{64,96},{96,64},{1,33},{33,1},{65,97},{97,65},{2,34}... | collective-permute-start | bytes 7077896 | tf_op jit(solution)/shard_map/ppermute | solution.py:1242
  78.8 13.0 %all-to-all-start.2 = ((bf16[8,16,1792]{2,1,0:T(8,128)(2,1)}), bf16[8,16,1792]{2,1,0:T(8,128)(2,1)S(1)}, u32[]{:S(2)}, u32[]{:S(2)}) async-start(bf16[8,16,1792]{2,1,0:T(8,128)(2,1)} %bitcast.10), calls=%async_computation.2 | async-start | bytes 917504 | tf_op jit(solution)/shard_map/all_to_all | solution.py:1199
  83.0 94.9 %all-gather.6.cloned.1.call-start = ((), (), s32[]{:S(2)}) async-start(), calls=%async_computation.10 | async-start | bytes 6684672 | tf_op jit(solution)/shard_map/all_gather | solution.py:1228
  83.9 1.4 copy-start.11
  91.9 2.1 copy-start.18
  91.9 19.7 %collective-permute-start.5 = (bf16[768,768]{1,0:T(8,128)(2,1)}, bf16[768,768]{1,0:T(8,128)(2,1)S(1)}, u32[]{:S(2)}, u32[]{:S(2)}) collective-permute-start(bf16[768,768]{1,0:T(8,128)(2,1)} %bitcast.49), channel_id=1, source_target_pairs={{0,32},{32,0},{64,96},{96,64},{1,33},{33,1},{65,97},{97,65},{2,34}... | collective-permute-start | bytes 3538952 | tf_op jit(solution)/shard_map/ppermute | solution.py:1242
  93.4 18.2 %collective-permute-start.6 = (bf16[768,768]{1,0:T(8,128)(2,1)}, bf16[768,768]{1,0:T(8,128)(2,1)S(1)}, u32[]{:S(2)}, u32[]{:S(2)}) collective-permute-start(bf16[768,768]{1,0:T(8,128)(2,1)} %bitcast.51), channel_id=1, source_target_pairs={{0,32},{32,0},{64,96},{96,64},{1,33},{33,1},{65,97},{97,65},{2,34}... | collective-permute-start | bytes 3538952 | tf_op jit(solution)/shard_map/ppermute | solution.py:1242
  93.5 18.1 %collective-permute-start.7 = (bf16[768,768]{1,0:T(8,128)(2,1)}, bf16[768,768]{1,0:T(8,128)(2,1)}, u32[]{:S(2)}, u32[]{:S(2)}) collective-permute-start(bf16[768,768]{1,0:T(8,128)(2,1)} %bitcast.53), channel_id=1, source_target_pairs={{0,32},{32,0},{64,96},{96,64},{1,33},{33,1},{65,97},{97,65},{2,34}... | collective-permute-start | bytes 3538952 | tf_op jit(solution)/shard_map/ppermute | solution.py:1242
  105.3 24.2 %all-to-all-start.3 = ((bf16[64,16,512]{2,1,0:T(8,128)(2,1)}), bf16[64,16,512]{2,1,0:T(8,128)(2,1)S(1)}, u32[]{:S(2)}, u32[]{:S(2)}) async-start(bf16[64,16,512]{2,1,0:T(8,128)(2,1)} %bitcast.56), calls=%async_computation.3 | async-start | bytes 2097152 | tf_op jit(solution)/shard_map/all_to_all | solution.py:1236
  111.6 17.9 %copy-start.20 = (bf16[768,768]{1,0:T(8,128)(2,1)}, bf16[768,768]{1,0:T(8,128)(2,1)S(1)}, u32[]{:S(2)}) copy-start(bf16[768,768]{1,0:T(8,128)(2,1)S(1)} %collective-permute-done.5.refs_4_) | copy-start | bytes 3538948
  111.6 17.8 %copy-start.21 = (bf16[768,768]{1,0:T(8,128)(2,1)}, bf16[768,768]{1,0:T(8,128)(2,1)S(1)}, u32[]{:S(2)}) copy-start(bf16[768,768]{1,0:T(8,128)(2,1)S(1)} %collective-permute-done.6.refs_5_) | copy-start | bytes 3538948
  142.1 6.7 %collective-permute-start.8 = (bf16[1600,768]{1,0:T(8,128)(2,1)}, bf16[1600,768]{1,0:T(8,128)(2,1)}, u32[]{:S(2)}, u32[]{:S(2)}) collective-permute-start(bf16[1600,768]{1,0:T(8,128)(2,1)} %get-tuple-element.141), channel_id=1, source_target_pairs={{0,32},{32,0},{64,96},{96,64},{1,33},{33,1},{65,97},{97,65},{2,34}... | collective-permute-start | bytes 7372808 | tf_op jit(solution)/shard_map/ppermute | solution.py:1242
  143.8 23.0 %all-to-all-start.4 = ((bf16[64,16,512]{2,1,0:T(8,128)(2,1)}), bf16[64,16,512]{2,1,0:T(8,128)(2,1)S(1)}, u32[]{:S(2)}, u32[]{:S(2)}) async-start(bf16[64,16,512]{2,1,0:T(8,128)(2,1)} %bitcast.55), calls=%async_computation.4 | async-start | bytes 2097152 | tf_op jit(solution)/shard_map/all_to_all | solution.py:1236
  148.5 90.3 %all-gather.8.cloned.1.call-start = ((), (), s32[]{:S(2)}) async-start(), calls=%async_computation.11 | async-start | bytes 3342336 | tf_op jit(solution)/shard_map/all_gather | solution.py:1228
  150.8 2.2 copy-start.16
  166.8 1.0 copy-start.14
  167.8 19.1 %copy-start.3 = (f32[24,1536]{1,0:T(8,128)S(1)}, f32[24,1536]{1,0:T(8,128)}, u32[]{:S(2)}) copy-start(f32[24,1536]{1,0:T(8,128)} %get-tuple-element.125.par.refs_4_.refs_3_) | copy-start | bytes 442372
  187.0 11.8 %copy-start.5 = (bf16[4,16,2176]{2,1,0:T(8,128)(2,1)}, bf16[4,16,2176]{2,1,0:T(8,128)(2,1)S(1)}, u32[]{:S(2)}) copy-start(bf16[4,16,2176]{2,1,0:T(8,128)(2,1)S(1)} %all_to_all.45) | copy-start | bytes 835588
  187.9 12.2 %all-to-all-start.6 = ((bf16[8,16,2176]{2,1,0:T(8,128)(2,1)}), bf16[8,16,2176]{2,1,0:T(8,128)(2,1)S(1)}, u32[]{:S(2)}, u32[]{:S(2)}) async-start(bf16[8,16,2176]{2,1,0:T(8,128)(2,1)} %bitcast.25), calls=%async_computation.6 | async-start | bytes 1114112 | tf_op jit(solution)/shard_map/all_to_all | solution.py:1199
  200.0 7.6 %copy-start.17 = (bf16[8,16,2176]{2,1,0:T(8,128)(2,1)}, bf16[8,16,2176]{2,1,0:T(8,128)(2,1)S(1)}, u32[]{:S(2)}) copy-start(bf16[8,16,2176]{2,1,0:T(8,128)(2,1)S(1)} %all-to-all-done.6) | copy-start | bytes 1671172
  200.0 30.9 %all-to-all-start.8 = ((bf16[32,144,128]{2,1,0:T(8,128)(2,1)}), bf16[32,144,128]{2,1,0:T(8,128)(2,1)S(1)}, u32[]{:S(2)}, u32[]{:S(2)}) async-start(bf16[32,144,128]{2,1,0:T(8,128)(2,1)} %bitcast.48), calls=%async_computation.8 | async-start | bytes 2359296 | tf_op jit(solution)/shard_map/all_to_all | solution.py:1210
  230.9 24.8 %all-to-all-start.7 = ((bf16[32,48,384]{2,1,0:T(8,128)(2,1)}), bf16[32,48,384]{2,1,0:T(8,128)(2,1)S(1)}, u32[]{:S(2)}, u32[]{:S(2)}) async-start(bf16[32,48,384]{2,1,0:T(8,128)(2,1)} %bitcast.47), calls=%async_computation.7 | async-start | bytes 2359296 | tf_op jit(solution)/shard_map/all_to_all | solution.py:1210
  238.8 2.8 copy-start
  241.6 1.9 copy-start.4
  243.5 3.1 %copy-start.23 = (f32[8,768]{1,0:T(8,128)S(1)}, f32[8,768]{1,0:T(8,128)}, u32[]{:S(2)}) copy-start(f32[8,768]{1,0:T(8,128)} %get-tuple-element.173) | copy-start | bytes 73732
  245.6 10.2 %collective-permute-start.9 = (bf16[48,768]{1,0:T(8,128)(2,1)S(1)}, bf16[48,768]{1,0:T(8,128)(2,1)S(1)}, u32[]{:S(2)}, u32[]{:S(2)}) collective-permute-start(bf16[48,768]{1,0:T(8,128)(2,1)S(1)} %get-tuple-element.172), channel_id=1, source_target_pairs={{0,4},{1,5},{2,6},{3,7},{4,0},{5,1},{6,2},{7,3},{8,12},{9,13},{10,... | collective-permute-start | bytes 221192 | tf_op jit(solution)/shard_map/ppermute | solution.py:1216
  246.6 6.5 %collective-permute-start.10 = (f32[8,768]{1,0:T(8,128)S(1)}, f32[8,768]{1,0:T(8,128)S(1)}, u32[]{:S(2)}, u32[]{:S(2)}) collective-permute-start(f32[8,768]{1,0:T(8,128)S(1)} %copy-done.23), channel_id=1, source_target_pairs={{1,0},{2,1},{3,2},{4,3},{5,4},{6,5},{7,6},{8,7},{9,8},{10,9},{11,1... | collective-permute-start | bytes 73736 | tf_op jit(solution)/shard_map/ppermute | solution.py:1508
  255.7 2.8 copy-start.1
  258.5 10.1 %copy-start.7 = (bf16[128,768]{1,0:T(8,128)(2,1)S(1)}, bf16[128,768]{1,0:T(8,128)(2,1)}, u32[]{:S(2)}) copy-start(bf16[128,768]{1,0:T(8,128)(2,1)} %get-tuple-element.134.refs_14_.refs_25_.hid) | copy-start | bytes 589828
  258.5 10.1 %copy-start.8 = (f32[128,768]{1,0:T(8,128)S(1)}, f32[128,768]{1,0:T(8,128)}, u32[]{:S(2)}) copy-start(f32[128,768]{1,0:T(8,128)} %get-tuple-element.175.mgrad) | copy-start | bytes 1179652
  258.5 10.1 %copy-start.9 = (f32[128,768]{1,0:T(8,128)S(1)}, f32[128,768]{1,0:T(8,128)}, u32[]{:S(2)}) copy-start(f32[128,768]{1,0:T(8,128)} %get-tuple-element.165.ngrad_in) | copy-start | bytes 1179652
  258.5 10.1 %copy-start.10 = (f32[768]{0:T(1024)S(1)}, f32[768]{0:T(1024)}, u32[]{:S(2)}) copy-start(f32[768]{0:T(1024)} %gain.3) | copy-start | bytes 9220
  259.8 4.9 %collective-permute-start.11 = (bf16[96,768]{1,0:T(8,128)(2,1)S(1)}, bf16[96,768]{1,0:T(8,128)(2,1)S(1)}, u32[]{:S(2)}, u32[]{:S(2)}) collective-permute-start(bf16[96,768]{1,0:T(8,128)(2,1)S(1)} %shard_map.345), channel_id=1, source_target_pairs={{0,32},{32,0},{64,96},{96,64},{1,33},{33,1},{65,97},{97,65},{2,34}... | collective-permute-start | bytes 442376 | tf_op jit(solution)/shard_map/ppermute | solution.py:1242
  263.8 4.3 %collective-permute-start.13 = (bf16[96,768]{1,0:T(8,128)(2,1)S(1)}, bf16[96,768]{1,0:T(8,128)(2,1)S(1)}, u32[]{:S(2)}, u32[]{:S(2)}) collective-permute-start(bf16[96,768]{1,0:T(8,128)(2,1)S(1)} %pad_maximum_fusion.2), channel_id=1, source_target_pairs={{0,32},{32,0},{64,96},{96,64},{1,33},{33,1},{65,97},{97,65},{2,34}... | collective-permute-start | bytes 442376 | tf_op jit(solution)/shard_map/ppermute | solution.py:1242
  264.8 7.2 %collective-permute-start.12 = (bf16[96,768]{1,0:T(8,128)(2,1)S(1)}, bf16[96,768]{1,0:T(8,128)(2,1)S(1)}, u32[]{:S(2)}, u32[]{:S(2)}) collective-permute-start(bf16[96,768]{1,0:T(8,128)(2,1)S(1)} %add_convert_fusion.1.ours), channel_id=1, source_target_pairs={{0,64},{64,0},{32,96},{96,32},{1,65},{65,1},{33,97},{97,33},{2,66}... | collective-permute-start | bytes 442376 | tf_op jit(solution)/shard_map/ppermute | solution.py:1246
  268.2 6.5 %collective-permute-start.14 = (bf16[96,768]{1,0:T(8,128)(2,1)S(1)}, bf16[96,768]{1,0:T(8,128)(2,1)S(1)}, u32[]{:S(2)}, u32[]{:S(2)}) collective-permute-start(bf16[96,768]{1,0:T(8,128)(2,1)S(1)} %add_convert_fusion.ours_two), channel_id=1, source_target_pairs={{0,64},{64,0},{32,96},{96,32},{1,65},{65,1},{33,97},{97,33},{2,66}... | collective-permute-start | bytes 442376 | tf_op jit(solution)/shard_map/ppermute | solution.py:1246
  (2 other events, 1.9 us)
Sparse Core Ops, SparseCore 0:
  15.0 58.6 all-gather.3
  92.0 79.7 all-gather.5
  178.0 60.0 all-gather.7

commit v2 on v1

--- a/solution.py
+++ b/solution.py
@@ -260,11 +260,11 @@
 
 
 def front_kernel(
-    moves, core, nrm_in, halo_in, wm, wo, aux, ext_o, pre_o, steps_o, sig_o, small_o, x_o, tpre_o, tsuf_o,
+    moves, core, nrm_in, halo_in, wm, wo, rest_m, rest_o, aux, ext_o, pre_o, steps_o, sig_o, small_o, x_o, tpre_o, tsuf_o,
     state_o, par_o, xd_o, sd_s, q_s, bw_s, nrm_s, sum_s, *, rank, count
 ):
     rows, di = pre_o.shape
-    half = wo.shape[1] - 128
+    half = wo.shape[1]
     steps_in = rows // SUB
     gs = group_of(di)
     low = core[0] == 0
@@ -273,14 +273,14 @@
     nrm_s[0, rows:] = jnp.where(low, halo_in[:, :half], halo_in[:, half:])
     nrm_s[1, rows:] = jnp.where(low, halo_in[:, half:], halo_in[:, :half])
     small_o[...] = jnp.zeros_like(small_o)
-    moves.need(wm, wo)
+    moves.need(rest_m, rest_o)
     par = par_o
     total_rows = par_o.shape[0]
 
     def unpack(g, _):
         lanes = pl.ds(pl.multiple_of(g * 128, 128), 128)
-        mine = wm[lanes, half:]
-        other = wo[lanes, half:]
+        mine = rest_m[lanes, :]
+        other = rest_o[lanes, :]
         xd_o[lanes, :] = jnp.where(low, mine, other)
         turned = jnp.where(low, other, mine).astype(f32).T
         par_o[:, lanes] = (
@@ -291,6 +291,7 @@
         return 0
 
     lax.fori_loop(0, di // 128, unpack, 0)
+    moves.need(wm, wo)
 
     def project(g, _):
         lanes = pl.ds(pl.multiple_of(g * gs, gs), gs)
@@ -349,7 +350,7 @@
             return (states, total + sd)
 
         zero = jnp.zeros((SUB, 128), f32)
-        states, total = lax.fori_loop(0, steps_in, step, ((zero,) * count, zero), unroll=8)
+        states, total = lax.fori_loop(0, steps_in, step, ((zero,) * count, zero), unroll=16)
         row = sublane_iota(128)
         ahead = prefix_sum(total)
         behind = suffix_sum(total)
@@ -506,7 +507,7 @@
             scan_o[at, lanes] = total
             return tuple(fresh)
 
-        lax.fori_loop(0, steps_in, step, first, unroll=8)
+        lax.fori_loop(0, steps_in, step, first, unroll=16)
         return 0
 
     lax.fori_loop(0, di // 128, scan, 0)
@@ -660,7 +661,7 @@
             return (grads, total + sd_here)
 
         zero = jnp.zeros((SUB, 128), f32)
-        grads, total = lax.fori_loop(0, steps_in, step, ((zero,) * count, zero), unroll=8)
+        grads, total = lax.fori_loop(0, steps_in, step, ((zero,) * count, zero), unroll=16)
         row = sublane_iota(128)
         last = []
         for n in range(count):
@@ -855,7 +856,7 @@
                 fresh.append(decay * states[n] + q_here * bw_s[j * count + n])
             return tuple(fresh)
 
-        last = lax.fori_loop(0, steps_in, forward, first, unroll=8)
+        last = lax.fori_loop(0, steps_in, forward, first, unroll=16)
         for n in range(count):
             st_s[steps_in * count + n] = last[n]
         zero = jnp.zeros((SUB, 128), f32)
@@ -1328,10 +1329,11 @@
             pltpu.VMEM((2, rows + 16, half), bf16),
             pltpu.VMEM((16, 128), f32),
         ],
-        (core, nrm, halo, wm, wo, aux),
+        (core, nrm, halo, wm, wo, wm, wo, aux),
         smem=1,
-        late=(3, 4),
+        late=(5, 6, 3, 4),
         early=(0, 1, 2, 3, 9, 10, 11, 12),
+        lanes={3: pl.ds(0, half), 4: pl.ds(0, half), 5: pl.ds(half, 128), 6: pl.ds(half, 128)},
     )
 
     near = exchange_near(states, members)
@@ -1403,6 +1405,7 @@
         (arrived, w_gate[0], w_up[0], w_down[0], w_gate_two, w_up_two, w_down_two),
         late=(1, 2, 3, 4, 5, 6),
         early=(0, 1, 2),
+        limit=44 * 1024 * 1024,
     )
     back = exchange_sides(back.reshape(2 * experts, stride, -1)).reshape(send.shape)
     given = other_core(sent)

time: 285 us -> 284 us (level)
  Pallas kernels: 97.2 us -> 94 us
    pallas_call x16, Pallas kernels: 97.2 us -> 94 us  [call(): pl.pallas_call(staged if moving else kernel, out_shape=out_shapes, in_spe...]
  transfers between devices with their start and end apart: 26 -> 26, of which waited for: 13 -> 13; matrix products, arithmetic and copies ran while one was open for 5% -> 5% of each run, Pallas kernels for 32% -> 31%
where the time goes in v2:
time: 284 us; the launch traced here: 283 us
  Pallas kernels  94 us (33%)
  starting transfers between devices  72.3 us (25%)
  waiting for transfers between devices  64.9 us (23%)
  between operations  14.1 us (5%)
  local copies, waits for them, and re-layouts  12.9 us (5%)
  matrix products  12.8 us (5%)
  blocking collectives  9.15 us (3%)
    pallas_call x16, Pallas kernels, call(): pl.pallas_call(staged if moving else kernel, out_shape=out_shapes, in_spe...  94 us
    all_to_all x3, starting transfers between devices, exchange_channels(): lax.all_to_all(values, 'wide', split_axis=0, concat_axis=0, tiled=True, a...  24 us
    all_to_all x2, waiting for transfers between devices, exchange_sides(): lax.all_to_all(values, ('dp', 'wide'), split_axis=0, concat_axis=0, tiled...  22.8 us
    unnamed x48, local copies, waits for them, and re-layouts  12.9 us
    dot_general x6, matrix products, dot_tn(): lax.dot_general(left, right, (((0,), (0,)), ((), ())), preferred_element_...  12.8 us
    ppermute x1, waiting for transfers between devices, body(): halo = lax.ppermute(tail, 'wide', [(i, i + 1) for i in range(places - 1)])  12.3 us
    all_to_all x2, starting transfers between devices, exchange_sides(): lax.all_to_all(values, ('dp', 'wide'), split_axis=0, concat_axis=0, tiled...  11.8 us
    ppermute x8, starting transfers between devices, other_core(): return lax.ppermute(values, 'dp', [(0, 1), (1, 0), (2, 3), (3, 2)])  11.7 us
  transfers between devices with their start and end apart: 26, of which 13 were waited for; matrix products, arithmetic and copies ran while one was open for 5% of the time, Pallas kernels for 31%

profile of v2, /device:TPU:1, one launch (start us, length us, event | category | flops | bytes accessed | tf_op | source)
XLA Modules:
  0.0 282.7 jit_solution(2804599503582183506)
XLA Ops:
  7.2 1.6 shard_map.331
  8.8 2.0 collective-permute-start
  10.8 2.4 shard_map.332
  14.9 8.8 %all-to-all-start = ((bf16[32,48,512]{2,1,0:T(8,128)(2,1)}), bf16[32,48,512]{2,1,0:T(8,128)(2,1)S(1)}, u32[]{:S(2)}, u32[]{:S(2)}) async-start(bf16[32,48,512]{2,1,0:T(8,128)(2,1)} %bitcast.51), calls=%async_computation | async-start | bytes 3145728 | tf_op jit(solution)/shard_map/all_to_all | solution.py:1211
  23.7 2.4 shard_map.333
  26.1 3.1 %collective-permute-start.2 = (bf16[16,768]{1,0:T(8,128)(2,1)}, bf16[16,768]{1,0:T(8,128)(2,1)S(1)}, u32[]{:S(2)}, u32[]{:S(2)}) collective-permute-start(bf16[16,768]{1,0:T(8,128)(2,1)} %get-tuple-element.117), channel_id=1, source_target_pairs={{0,1},{1,2},{2,3},{3,4},{4,5},{5,6},{6,7},{7,8},{8,9},{9,10},{10,1... | collective-permute-start | bytes 73736 | tf_op jit(solution)/shard_map/ppermute | solution.py:1306
  29.2 12.3 %collective-permute-done.2.refs_2_.refs_18_ = bf16[16,768]{1,0:T(8,128)(2,1)S(1)} collective-permute-done((bf16[16,768]{1,0:T(8,128)(2,1)}, bf16[16,768]{1,0:T(8,128)(2,1)S(1)}, u32[]{:S(2)}, u32[]{:S(2)}) %collective-permute-start.2) | collective-permute-done | bytes 24608 | tf_op jit(solution)/shard_map/ppermute | solution.py:1306
  41.5 4.0 %all-to-all-done = bf16[32,48,512]{2,1,0:T(8,128)(2,1)S(1)} async-done(((bf16[32,48,512]{2,1,0:T(8,128)(2,1)}), bf16[32,48,512]{2,1,0:T(8,128)(2,1)S(1)}, u32[]{:S(2)}, u32[]{:S(2)}) %all-to-all-start) | async-done | bytes 1572896 | tf_op jit(solution)/shard_map/all_to_all | solution.py:1211
  45.6 3.1 %collective-permute-start.3 = (bf16[1536,512]{1,0:T(8,128)(2,1)S(1)}, bf16[1536,512]{1,0:T(8,128)(2,1)S(1)}, u32[]{:S(2)}, u32[]{:S(2)}) collective-permute-start(bf16[1536,512]{1,0:T(8,128)(2,1)S(1)} %bitcast.47), channel_id=1, source_target_pairs={{0,32},{32,0},{64,96},{96,64},{1,33},{33,1},{65,97},{97,65},{2,34}... | collective-permute-start | bytes 4718600 | tf_op jit(solution)/shard_map/ppermute | solution.py:1243
  48.7 1.8 collective-permute-start.1
  52.9 12.6 %shard_map.334 = (f32[152,1536]{1,0:T(8,128)}, f32[128,1536]{1,0:T(8,128)}, f32[128,1536]{1,0:T(8,128)}, f32[128,1536]{1,0:T(8,128)}, f32[128,128]{1,0:T(8,128)}...) custom-call(s32[1]{0:T(128)} %bitcast.core.refs_0_.refs_1_, ...), custom_call_target="tpu_custom_call" | custom-call | tf_op jit(solution)/shard_map/pallas_call | solution.py:92
  65.5 3.4 %all-to-all-start.1 = ((bf16[4,16,1792]{2,1,0:T(8,128)(2,1)}), bf16[4,16,1792]{2,1,0:T(8,128)(2,1)S(1)}, u32[]{:S(2)}, u32[]{:S(2)}) async-start(bf16[4,16,1792]{2,1,0:T(8,128)(2,1)} %bitcast.59), calls=%async_computation.1 | async-start | bytes 458752 | tf_op jit(solution)/shard_map/all_to_all | solution.py:1192
  68.9 7.0 %all-to-all-done.1 = bf16[4,16,1792]{2,1,0:T(8,128)(2,1)S(1)} async-done(((bf16[4,16,1792]{2,1,0:T(8,128)(2,1)}), bf16[4,16,1792]{2,1,0:T(8,128)(2,1)S(1)}, u32[]{:S(2)}, u32[]{:S(2)}) %all-to-all-start.1) | async-done | bytes 229408 | tf_op jit(solution)/shard_map/all_to_all | solution.py:1192
  78.4 4.0 %all-to-all-start.2 = ((bf16[8,16,1792]{2,1,0:T(8,128)(2,1)}), bf16[8,16,1792]{2,1,0:T(8,128)(2,1)S(1)}, u32[]{:S(2)}, u32[]{:S(2)}) async-start(bf16[8,16,1792]{2,1,0:T(8,128)(2,1)} %bitcast.10), calls=%async_computation.2 | async-start | bytes 917504 | tf_op jit(solution)/shard_map/all_to_all | solution.py:1200
  83.3 5.3 %shard_map.336.refs_19_.refs_8_.refs_6_ = f32[128,1536]{1,0:T(8,128)} custom-call(s32[1]{0:T(128)} %bitcast.core.refs_0_.refs_1_, bf16[128,768]{1,0:T(8,128)(2,1)} %get-tuple-element.115.refs_1_, bf16[1536,768]{1,0:T(8,128)(2,1)} %all-gather.4.cloned.1.call-done.refs_2_, bf16[1536,768]{1,0:T(8,128)(2,1)} %collective-permute-done.4.refs_3_), custom_call_target="tpu_custom_call" | custom-call | tf_op jit(solution)/shard_map/pallas_call | solution.py:92
  88.6 2.7 all-to-all-done.2
  91.3 1.6 collective-permute-start.5
  93.4 11.1 %shard_map.337 = (f32[128,1536]{1,0:T(8,128)}, bf16[1024,512]{1,0:T(8,128)(2,1)}, f32[128,768]{1,0:T(8,128)}, bf16[128,768]{1,0:T(8,128)(2,1)}, f32[128,32]{1,0:...) custom-call(s32[1]{0:T(128)} %bitcast.core.refs_0_.refs_1_, ...), custom_call_target="tpu_custom_call" | custom-call | tf_op jit(solution)/shard_map/pallas_call | solution.py:92
  104.4 7.0 %all-to-all-start.3 = ((bf16[64,16,512]{2,1,0:T(8,128)(2,1)}), bf16[64,16,512]{2,1,0:T(8,128)(2,1)S(1)}, u32[]{:S(2)}, u32[]{:S(2)}) async-start(bf16[64,16,512]{2,1,0:T(8,128)(2,1)} %bitcast.57), calls=%async_computation.3 | async-start | bytes 2097152 | tf_op jit(solution)/shard_map/all_to_all | solution.py:1237
  111.5 17.8 %all-to-all-done.3 = bf16[64,16,512]{2,1,0:T(8,128)(2,1)S(1)} async-done(((bf16[64,16,512]{2,1,0:T(8,128)(2,1)}), bf16[64,16,512]{2,1,0:T(8,128)(2,1)S(1)}, u32[]{:S(2)}, u32[]{:S(2)}) %all-to-all-start.3) | async-done | bytes 1048608 | tf_op jit(solution)/shard_map/all_to_all | solution.py:1237
  130.6 9.4 %shard_map.338 = (bf16[1600,768]{1,0:T(8,128)(2,1)}, bf16[1600,768]{1,0:T(8,128)(2,1)}, bf16[1024,512]{1,0:T(8,128)(2,1)S(1)}) custom-call(bf16[1024,512]{1,0:T(8,128)(2,1)S(1)} %bitcast.35, bf16[768,768]{1,0:T(8,128)(2,1)S(1)} %bitcast.41, bf16[768,768]{1,0:T(8,128)(2,1)S(1)} %bitcast.43, bf16[768,768]{1,0:T(8,128)(2,1)S(1)} %bitcast.45, ...), custom_call_target="tpu_custom_call" | custom-call | tf_op jit(solution)/shard_map/pallas_call | solution.py:92
  141.0 1.7 collective-permute-start.8
  142.7 4.8 %all-to-all-start.4 = ((bf16[64,16,512]{2,1,0:T(8,128)(2,1)}), bf16[64,16,512]{2,1,0:T(8,128)(2,1)S(1)}, u32[]{:S(2)}, u32[]{:S(2)}) async-start(bf16[64,16,512]{2,1,0:T(8,128)(2,1)} %bitcast.46), calls=%async_computation.4 | async-start | bytes 2097152 | tf_op jit(solution)/shard_map/all_to_all | solution.py:1237
  147.8 2.0 fusion.4
  149.9 2.2 fusion.2
  152.1 2.2 add_bitcast_fusion.2
  154.3 2.2 add_bitcast_fusion.1
  156.5 2.0 fusion
  158.5 2.2 add_bitcast_fusion
  160.7 5.0 %all-to-all-done.4 = bf16[64,16,512]{2,1,0:T(8,128)(2,1)S(1)} async-done(((bf16[64,16,512]{2,1,0:T(8,128)(2,1)}), bf16[64,16,512]{2,1,0:T(8,128)(2,1)S(1)}, u32[]{:S(2)}, u32[]{:S(2)}) %all-to-all-start.4) | async-done | bytes 1048608 | tf_op jit(solution)/shard_map/all_to_all | solution.py:1237
  166.7 10.1 %shard_map.339 = (f32[128,768]{1,0:T(8,128)}, bf16[128,768]{1,0:T(8,128)(2,1)}, f32[128,768]{1,0:T(8,128)}, f32[128,1536]{1,0:T(8,128)}, f32[128,1536]{1,0:T(8,1...) custom-call(s32[1]{0:T(128)} %bitcast.core.refs_0_.refs_1_, bf16[1024,512]{1,0:T(8,128)(2,1)} %bitcast.52, ...), custom_call_target="tpu_custom_call" | custom-call | tf_op jit(solution)/shard_map/pallas_call | solution.py:92
  176.9 9.1 %all_to_all.45 = bf16[4,16,2176]{2,1,0:T(8,128)(2,1)S(1)} all-to-all(bf16[4,16,2176]{2,1,0:T(8,128)(2,1)} %bitcast.58), channel_id=1, replica_groups={{0,1,2,3},{4,5,6,7},{8,9,10,11},{12,13,14,15},{16,17,18,19},{20,21,22,2..., dimensions={0} | all-to-all | bytes 557056 | tf_op jit(solution)/shard_map/all_to_all | solution.py:1192
  187.0 3.7 %all-to-all-start.6 = ((bf16[8,16,2176]{2,1,0:T(8,128)(2,1)}), bf16[8,16,2176]{2,1,0:T(8,128)(2,1)S(1)}, u32[]{:S(2)}, u32[]{:S(2)}) async-start(bf16[8,16,2176]{2,1,0:T(8,128)(2,1)} %bitcast.25), calls=%async_computation.6 | async-start | bytes 1114112 | tf_op jit(solution)/shard_map/all_to_all | solution.py:1200
  190.7 7.2 %shard_map.340 = (bf16[128,768]{1,0:T(8,128)(2,1)}, bf16[4608,128]{1,0:T(8,128)(2,1)}, f32[1,1536]{1,0:T(1,128)}, f32[2,128,384]{2,1,0:T(8,128)}) custom-call(s32[1]{0:T(128)} %bitcast.core.refs_0_.refs_1_, s32[1]{0:T(128)} %bitcast.1.refs_1_.refs_0_, bf16[1536,768]{1,0:T(8,128)(2,1)} %all-gather.4.cloned.1.call-done.refs_2_, ...), custom_call_target="tpu_custom_call" | custom-call | tf_op jit(solution)/shard_map/pallas_call | solution.py:92
  199.3 7.4 %all-to-all-start.8 = ((bf16[32,144,128]{2,1,0:T(8,128)(2,1)}), bf16[32,144,128]{2,1,0:T(8,128)(2,1)S(1)}, u32[]{:S(2)}, u32[]{:S(2)}) async-start(bf16[32,144,128]{2,1,0:T(8,128)(2,1)} %bitcast.56), calls=%async_computation.8 | async-start | bytes 2359296 | tf_op jit(solution)/shard_map/all_to_all | solution.py:1211
  206.8 22.9 %shard_map.342 = (bf16[1536,384]{1,0:T(8,128)(2,1)}, f32[128,768]{1,0:T(8,128)}, f32[8,768]{1,0:T(8,128)}) custom-call(s32[1]{0:T(128)} %bitcast.4.refs_1_.refs_0_, s32[1]{0:T(128)} %bitcast.core.refs_0_.refs_1_, bf16[1536,128]{1,0:T(8,128)(2,1)} %get-tuple-element.151.refs_2_, f32[24,1536]{1,0:T(8,128)} %get-tuple-element.125.par.refs_4_.refs_3_, ...), custom_call_target="tpu_custom_call" | custom-call | tf_op jit(solution)/shard_map/pallas_call | solution.py:92
  229.7 7.8 %all-to-all-start.7 = ((bf16[32,48,384]{2,1,0:T(8,128)(2,1)}), bf16[32,48,384]{2,1,0:T(8,128)(2,1)S(1)}, u32[]{:S(2)}, u32[]{:S(2)}) async-start(bf16[32,48,384]{2,1,0:T(8,128)(2,1)} %bitcast.55), calls=%async_computation.7 | async-start | bytes 2359296 | tf_op jit(solution)/shard_map/all_to_all | solution.py:1211
  237.6 2.8 copy-done
  240.3 1.9 copy-done.4
  242.2 2.0 shard_map.343
  246.6 5.2 %collective-permute-done.10.beyond = f32[8,768]{1,0:T(8,128)S(1)} collective-permute-done((f32[8,768]{1,0:T(8,128)S(1)}, f32[8,768]{1,0:T(8,128)S(1)}, u32[]{:S(2)}, u32[]{:S(2)}) %collective-permute-start.10) | collective-permute-done | bytes 24608 | tf_op jit(solution)/shard_map/ppermute | solution.py:1511
  251.8 2.6 all-to-all-done.7.got
  254.4 2.8 copy-done.1
  258.5 4.0 %collective-permute-start.11 = (bf16[96,768]{1,0:T(8,128)(2,1)S(1)}, bf16[96,768]{1,0:T(8,128)(2,1)S(1)}, u32[]{:S(2)}, u32[]{:S(2)}) collective-permute-start(bf16[96,768]{1,0:T(8,128)(2,1)S(1)} %shard_map.345), channel_id=1, source_target_pairs={{0,32},{32,0},{64,96},{96,64},{1,33},{33,1},{65,97},{97,65},{2,34}... | collective-permute-start | bytes 442376 | tf_op jit(solution)/shard_map/ppermute | solution.py:1243
  263.5 3.5 %collective-permute-start.12 = (bf16[96,768]{1,0:T(8,128)(2,1)S(1)}, bf16[96,768]{1,0:T(8,128)(2,1)S(1)}, u32[]{:S(2)}, u32[]{:S(2)}) collective-permute-start(bf16[96,768]{1,0:T(8,128)(2,1)S(1)} %add_convert_fusion.1.ours), channel_id=1, source_target_pairs={{0,64},{64,0},{32,96},{96,32},{1,65},{65,1},{33,97},{97,33},{2,66}... | collective-permute-start | bytes 442376 | tf_op jit(solution)/shard_map/ppermute | solution.py:1247
  268.8 2.2 collective-permute-done.12.theirs
  271.0 2.6 collective-permute-done.14.theirs_two
  273.6 2.6 shard_map.346
  (86 shorter events, 20.3 us)
Async XLA Ops:
  7.2 68.7 %all-gather.4.cloned.1.call-start = ((), (), s32[]{:S(2)}) async-start(), calls=%async_computation.9 | async-start | bytes 2506752 | tf_op jit(solution)/shard_map/all_gather | solution.py:1229
  8.8 4.5 %collective-permute-start = (bf16[48,768]{1,0:T(8,128)(2,1)}, bf16[48,768]{1,0:T(8,128)(2,1)S(1)}, u32[]{:S(2)}, u32[]{:S(2)}) collective-permute-start(bf16[48,768]{1,0:T(8,128)(2,1)} %shard_map.331), channel_id=1, source_target_pairs={{0,4},{1,5},{2,6},{3,7},{4,0},{5,1},{6,2},{7,3},{8,12},{9,13},{10,... | collective-permute-start | bytes 221192 | tf_op jit(solution)/shard_map/ppermute | solution.py:1217
  14.9 30.7 %all-to-all-start = ((bf16[32,48,512]{2,1,0:T(8,128)(2,1)}), bf16[32,48,512]{2,1,0:T(8,128)(2,1)S(1)}, u32[]{:S(2)}, u32[]{:S(2)}) async-start(bf16[32,48,512]{2,1,0:T(8,128)(2,1)} %bitcast.51), calls=%async_computation | async-start | bytes 3145728 | tf_op jit(solution)/shard_map/all_to_all | solution.py:1211
  26.1 15.5 %collective-permute-start.2 = (bf16[16,768]{1,0:T(8,128)(2,1)}, bf16[16,768]{1,0:T(8,128)(2,1)S(1)}, u32[]{:S(2)}, u32[]{:S(2)}) collective-permute-start(bf16[16,768]{1,0:T(8,128)(2,1)} %get-tuple-element.117), channel_id=1, source_target_pairs={{0,1},{1,2},{2,3},{3,4},{4,5},{5,6},{6,7},{7,8},{8,9},{9,10},{10,1... | collective-permute-start | bytes 73736 | tf_op jit(solution)/shard_map/ppermute | solution.py:1306
  41.5 10.2 %copy-start.22 = (bf16[16,768]{1,0:T(8,128)(2,1)}, bf16[16,768]{1,0:T(8,128)(2,1)S(1)}, u32[]{:S(2)}) copy-start(bf16[16,768]{1,0:T(8,128)(2,1)S(1)} %collective-permute-done.2.refs_2_.refs_18_) | copy-start | bytes 73732
  45.6 6.1 %copy-start.15 = (bf16[32,48,512]{2,1,0:T(8,128)(2,1)}, bf16[32,48,512]{2,1,0:T(8,128)(2,1)S(1)}, u32[]{:S(2)}) copy-start(bf16[32,48,512]{2,1,0:T(8,128)(2,1)S(1)} %all-to-all-done) | copy-start | bytes 4718596
  45.6 6.1 %collective-permute-start.3 = (bf16[1536,512]{1,0:T(8,128)(2,1)S(1)}, bf16[1536,512]{1,0:T(8,128)(2,1)S(1)}, u32[]{:S(2)}, u32[]{:S(2)}) collective-permute-start(bf16[1536,512]{1,0:T(8,128)(2,1)S(1)} %bitcast.47), channel_id=1, source_target_pairs={{0,32},{32,0},{64,96},{96,64},{1,33},{33,1},{65,97},{97,65},{2,34}... | collective-permute-start | bytes 4718600 | tf_op jit(solution)/shard_map/ppermute | solution.py:1243
  48.7 20.2 %collective-permute-start.1 = (bf16[128,768]{1,0:T(8,128)(2,1)}, bf16[128,768]{1,0:T(8,128)(2,1)S(1)}, u32[]{:S(2)}, u32[]{:S(2)}) collective-permute-start(bf16[128,768]{1,0:T(8,128)(2,1)} %get-tuple-element.115.refs_1_), channel_id=1, source_target_pairs={{0,4},{1,5},{2,6},{3,7},{4,0},{5,1},{6,2},{7,3},{8,12},{9,13},{10,... | collective-permute-start | bytes 589832 | tf_op jit(solution)/shard_map/ppermute | solution.py:1217
  51.7 1.2 copy-start.16
  52.9 29.6 %copy-start.21 = (bf16[128,768]{1,0:T(8,128)(2,1)S(1)}, bf16[128,768]{1,0:T(8,128)(2,1)}, u32[]{:S(2)}) copy-start(bf16[128,768]{1,0:T(8,128)(2,1)} %get-tuple-element.115.refs_1_) | copy-start | bytes 589828
  65.5 10.4 %all-to-all-start.1 = ((bf16[4,16,1792]{2,1,0:T(8,128)(2,1)}), bf16[4,16,1792]{2,1,0:T(8,128)(2,1)S(1)}, u32[]{:S(2)}, u32[]{:S(2)}) async-start(bf16[4,16,1792]{2,1,0:T(8,128)(2,1)} %bitcast.59), calls=%async_computation.1 | async-start | bytes 458752 | tf_op jit(solution)/shard_map/all_to_all | solution.py:1192
  75.9 12.7 %copy-start.6 = (bf16[4,16,1792]{2,1,0:T(8,128)(2,1)}, bf16[4,16,1792]{2,1,0:T(8,128)(2,1)S(1)}, u32[]{:S(2)}) copy-start(bf16[4,16,1792]{2,1,0:T(8,128)(2,1)S(1)} %all-to-all-done.1) | copy-start | bytes 688132
  75.9 7.4 %collective-permute-start.4 = (bf16[1536,768]{1,0:T(8,128)(2,1)}, bf16[1536,768]{1,0:T(8,128)(2,1)}, u32[]{:S(2)}, u32[]{:S(2)}) collective-permute-start(bf16[1536,768]{1,0:T(8,128)(2,1)} %all-gather.4.cloned.1.call-done.refs_2_), channel_id=1, source_target_pairs={{0,32},{32,0},{64,96},{96,64},{1,33},{33,1},{65,97},{97,65},{2,34}... | collective-permute-start | bytes 7077896 | tf_op jit(solution)/shard_map/ppermute | solution.py:1243
  78.4 12.8 %all-to-all-start.2 = ((bf16[8,16,1792]{2,1,0:T(8,128)(2,1)}), bf16[8,16,1792]{2,1,0:T(8,128)(2,1)S(1)}, u32[]{:S(2)}, u32[]{:S(2)}) async-start(bf16[8,16,1792]{2,1,0:T(8,128)(2,1)} %bitcast.10), calls=%async_computation.2 | async-start | bytes 917504 | tf_op jit(solution)/shard_map/all_to_all | solution.py:1200
  82.4 94.5 %all-gather.6.cloned.1.call-start = ((), (), s32[]{:S(2)}) async-start(), calls=%async_computation.10 | async-start | bytes 6684672 | tf_op jit(solution)/shard_map/all_gather | solution.py:1229
  83.3 8.0 %copy-start.8 = (bf16[1,768,768]{2,1,0:T(8,128)(2,1)S(1)}, bf16[1,768,768]{2,1,0:T(8,128)(2,1)}, u32[]{:S(2)}) copy-start(bf16[1,768,768]{2,1,0:T(8,128)(2,1)} %param.37) | copy-start | bytes 3538948
  83.3 9.6 %copy-start.9 = (bf16[1,768,768]{2,1,0:T(8,128)(2,1)S(1)}, bf16[1,768,768]{2,1,0:T(8,128)(2,1)}, u32[]{:S(2)}) copy-start(bf16[1,768,768]{2,1,0:T(8,128)(2,1)} %param.38) | copy-start | bytes 3538948
  91.2 2.1 copy-start.20
  91.3 20.2 %collective-permute-start.5 = (bf16[768,768]{1,0:T(8,128)(2,1)S(1)}, bf16[768,768]{1,0:T(8,128)(2,1)}, u32[]{:S(2)}, u32[]{:S(2)}) collective-permute-start(bf16[768,768]{1,0:T(8,128)(2,1)S(1)} %bitcast.40), channel_id=1, source_target_pairs={{0,32},{32,0},{64,96},{96,64},{1,33},{33,1},{65,97},{97,65},{2,34}... | collective-permute-start | bytes 3538952 | tf_op jit(solution)/shard_map/ppermute | solution.py:1243
  92.8 18.6 %collective-permute-start.6 = (bf16[768,768]{1,0:T(8,128)(2,1)S(1)}, bf16[768,768]{1,0:T(8,128)(2,1)}, u32[]{:S(2)}, u32[]{:S(2)}) collective-permute-start(bf16[768,768]{1,0:T(8,128)(2,1)S(1)} %bitcast.42), channel_id=1, source_target_pairs={{0,32},{32,0},{64,96},{96,64},{1,33},{33,1},{65,97},{97,65},{2,34}... | collective-permute-start | bytes 3538952 | tf_op jit(solution)/shard_map/ppermute | solution.py:1243
  92.9 18.5 %collective-permute-start.7 = (bf16[768,768]{1,0:T(8,128)(2,1)}, bf16[768,768]{1,0:T(8,128)(2,1)}, u32[]{:S(2)}, u32[]{:S(2)}) collective-permute-start(bf16[768,768]{1,0:T(8,128)(2,1)} %bitcast.44), channel_id=1, source_target_pairs={{0,32},{32,0},{64,96},{96,64},{1,33},{33,1},{65,97},{97,65},{2,34}... | collective-permute-start | bytes 3538952 | tf_op jit(solution)/shard_map/ppermute | solution.py:1243
  104.4 24.9 %all-to-all-start.3 = ((bf16[64,16,512]{2,1,0:T(8,128)(2,1)}), bf16[64,16,512]{2,1,0:T(8,128)(2,1)S(1)}, u32[]{:S(2)}, u32[]{:S(2)}) async-start(bf16[64,16,512]{2,1,0:T(8,128)(2,1)} %bitcast.57), calls=%async_computation.3 | async-start | bytes 2097152 | tf_op jit(solution)/shard_map/all_to_all | solution.py:1237
  129.3 1.3 copy-start.10
  141.0 6.8 %collective-permute-start.8 = (bf16[1600,768]{1,0:T(8,128)(2,1)}, bf16[1600,768]{1,0:T(8,128)(2,1)}, u32[]{:S(2)}, u32[]{:S(2)}) collective-permute-start(bf16[1600,768]{1,0:T(8,128)(2,1)} %get-tuple-element.141), channel_id=1, source_target_pairs={{0,32},{32,0},{64,96},{96,64},{1,33},{33,1},{65,97},{97,65},{2,34}... | collective-permute-start | bytes 7372808 | tf_op jit(solution)/shard_map/ppermute | solution.py:1243
  142.7 23.0 %all-to-all-start.4 = ((bf16[64,16,512]{2,1,0:T(8,128)(2,1)}), bf16[64,16,512]{2,1,0:T(8,128)(2,1)S(1)}, u32[]{:S(2)}, u32[]{:S(2)}) async-start(bf16[64,16,512]{2,1,0:T(8,128)(2,1)} %bitcast.46), calls=%async_computation.4 | async-start | bytes 2097152 | tf_op jit(solution)/shard_map/all_to_all | solution.py:1237
  147.6 90.0 %all-gather.8.cloned.1.call-start = ((), (), s32[]{:S(2)}) async-start(), calls=%async_computation.11 | async-start | bytes 3342336 | tf_op jit(solution)/shard_map/all_gather | solution.py:1229
  149.9 2.2 copy-start.18
  165.7 1.0 copy-start.17
  166.7 19.4 %copy-start.3 = (f32[24,1536]{1,0:T(8,128)S(1)}, f32[24,1536]{1,0:T(8,128)}, u32[]{:S(2)}) copy-start(f32[24,1536]{1,0:T(8,128)} %get-tuple-element.125.par.refs_4_.refs_3_) | copy-start | bytes 442372
  186.1 11.9 %copy-start.5 = (bf16[4,16,2176]{2,1,0:T(8,128)(2,1)}, bf16[4,16,2176]{2,1,0:T(8,128)(2,1)S(1)}, u32[]{:S(2)}) copy-start(bf16[4,16,2176]{2,1,0:T(8,128)(2,1)S(1)} %all_to_all.45) | copy-start | bytes 835588
  187.0 12.3 %all-to-all-start.6 = ((bf16[8,16,2176]{2,1,0:T(8,128)(2,1)}), bf16[8,16,2176]{2,1,0:T(8,128)(2,1)S(1)}, u32[]{:S(2)}, u32[]{:S(2)}) async-start(bf16[8,16,2176]{2,1,0:T(8,128)(2,1)} %bitcast.25), calls=%async_computation.6 | async-start | bytes 1114112 | tf_op jit(solution)/shard_map/all_to_all | solution.py:1200
  199.3 7.4 %copy-start.19 = (bf16[8,16,2176]{2,1,0:T(8,128)(2,1)}, bf16[8,16,2176]{2,1,0:T(8,128)(2,1)S(1)}, u32[]{:S(2)}) copy-start(bf16[8,16,2176]{2,1,0:T(8,128)(2,1)S(1)} %all-to-all-done.6) | copy-start | bytes 1671172
  199.3 30.4 %all-to-all-start.8 = ((bf16[32,144,128]{2,1,0:T(8,128)(2,1)}), bf16[32,144,128]{2,1,0:T(8,128)(2,1)S(1)}, u32[]{:S(2)}, u32[]{:S(2)}) async-start(bf16[32,144,128]{2,1,0:T(8,128)(2,1)} %bitcast.56), calls=%async_computation.8 | async-start | bytes 2359296 | tf_op jit(solution)/shard_map/all_to_all | solution.py:1211
  229.7 24.7 %all-to-all-start.7 = ((bf16[32,48,384]{2,1,0:T(8,128)(2,1)}), bf16[32,48,384]{2,1,0:T(8,128)(2,1)S(1)}, u32[]{:S(2)}, u32[]{:S(2)}) async-start(bf16[32,48,384]{2,1,0:T(8,128)(2,1)} %bitcast.55), calls=%async_computation.7 | async-start | bytes 2359296 | tf_op jit(solution)/shard_map/all_to_all | solution.py:1211
  237.6 2.8 copy-start
  240.3 1.9 copy-start.4
  242.2 3.1 %copy-start.23 = (f32[8,768]{1,0:T(8,128)S(1)}, f32[8,768]{1,0:T(8,128)}, u32[]{:S(2)}) copy-start(f32[8,768]{1,0:T(8,128)} %get-tuple-element.173) | copy-start | bytes 73732
  244.3 10.1 %collective-permute-start.9 = (bf16[48,768]{1,0:T(8,128)(2,1)S(1)}, bf16[48,768]{1,0:T(8,128)(2,1)S(1)}, u32[]{:S(2)}, u32[]{:S(2)}) collective-permute-start(bf16[48,768]{1,0:T(8,128)(2,1)S(1)} %get-tuple-element.172), channel_id=1, source_target_pairs={{0,4},{1,5},{2,6},{3,7},{4,0},{5,1},{6,2},{7,3},{8,12},{9,13},{10,... | collective-permute-start | bytes 221192 | tf_op jit(solution)/shard_map/ppermute | solution.py:1217
  245.4 6.5 %collective-permute-start.10 = (f32[8,768]{1,0:T(8,128)S(1)}, f32[8,768]{1,0:T(8,128)S(1)}, u32[]{:S(2)}, u32[]{:S(2)}) collective-permute-start(f32[8,768]{1,0:T(8,128)S(1)} %copy-done.23), channel_id=1, source_target_pairs={{1,0},{2,1},{3,2},{4,3},{5,4},{6,5},{7,6},{8,7},{9,8},{10,9},{11,1... | collective-permute-start | bytes 73736 | tf_op jit(solution)/shard_map/ppermute | solution.py:1511
  254.4 2.8 copy-start.1
  257.2 10.4 %copy-start.7 = (bf16[128,768]{1,0:T(8,128)(2,1)S(1)}, bf16[128,768]{1,0:T(8,128)(2,1)}, u32[]{:S(2)}) copy-start(bf16[128,768]{1,0:T(8,128)(2,1)} %get-tuple-element.134.refs_14_.refs_25_.hid) | copy-start | bytes 589828
  257.2 10.4 %copy-start.12 = (f32[128,768]{1,0:T(8,128)S(1)}, f32[128,768]{1,0:T(8,128)}, u32[]{:S(2)}) copy-start(f32[128,768]{1,0:T(8,128)} %get-tuple-element.175.mgrad) | copy-start | bytes 1179652
  257.2 10.4 %copy-start.13 = (f32[128,768]{1,0:T(8,128)S(1)}, f32[128,768]{1,0:T(8,128)}, u32[]{:S(2)}) copy-start(f32[128,768]{1,0:T(8,128)} %get-tuple-element.165.ngrad_in) | copy-start | bytes 1179652
  257.2 10.4 %copy-start.14 = (f32[768]{0:T(1024)S(1)}, f32[768]{0:T(1024)}, u32[]{:S(2)}) copy-start(f32[768]{0:T(1024)} %gain.3) | copy-start | bytes 9220
  258.5 5.0 %collective-permute-start.11 = (bf16[96,768]{1,0:T(8,128)(2,1)S(1)}, bf16[96,768]{1,0:T(8,128)(2,1)S(1)}, u32[]{:S(2)}, u32[]{:S(2)}) collective-permute-start(bf16[96,768]{1,0:T(8,128)(2,1)S(1)} %shard_map.345), channel_id=1, source_target_pairs={{0,32},{32,0},{64,96},{96,64},{1,33},{33,1},{65,97},{97,65},{2,34}... | collective-permute-start | bytes 442376 | tf_op jit(solution)/shard_map/ppermute | solution.py:1243
  262.5 4.5 %collective-permute-start.13 = (bf16[96,768]{1,0:T(8,128)(2,1)S(1)}, bf16[96,768]{1,0:T(8,128)(2,1)S(1)}, u32[]{:S(2)}, u32[]{:S(2)}) collective-permute-start(bf16[96,768]{1,0:T(8,128)(2,1)S(1)} %pad_maximum_fusion.2), channel_id=1, source_target_pairs={{0,32},{32,0},{64,96},{96,64},{1,33},{33,1},{65,97},{97,65},{2,34}... | collective-permute-start | bytes 442376 | tf_op jit(solution)/shard_map/ppermute | solution.py:1243
  263.5 7.5 %collective-permute-start.12 = (bf16[96,768]{1,0:T(8,128)(2,1)S(1)}, bf16[96,768]{1,0:T(8,128)(2,1)S(1)}, u32[]{:S(2)}, u32[]{:S(2)}) collective-permute-start(bf16[96,768]{1,0:T(8,128)(2,1)S(1)} %add_convert_fusion.1.ours), channel_id=1, source_target_pairs={{0,64},{64,0},{32,96},{96,32},{1,65},{65,1},{33,97},{97,33},{2,66}... | collective-permute-start | bytes 442376 | tf_op jit(solution)/shard_map/ppermute | solution.py:1247
  267.1 6.5 %collective-permute-start.14 = (bf16[96,768]{1,0:T(8,128)(2,1)S(1)}, bf16[96,768]{1,0:T(8,128)(2,1)S(1)}, u32[]{:S(2)}, u32[]{:S(2)}) collective-permute-start(bf16[96,768]{1,0:T(8,128)(2,1)S(1)} %add_convert_fusion.ours_two), channel_id=1, source_target_pairs={{0,64},{64,0},{32,96},{96,32},{1,65},{65,1},{33,97},{97,33},{2,66}... | collective-permute-start | bytes 442376 | tf_op jit(solution)/shard_map/ppermute | solution.py:1247
  (2 other events, 1.9 us)
Sparse Core Ops, SparseCore 0:
  15.0 58.6 all-gather.3
  91.4 80.4 all-gather.5
  177.0 60.2 all-gather.7

commit v3 on v2

--- a/solution.py
+++ b/solution.py
@@ -1073,13 +1073,9 @@
     first_o[...] = dot_tn(order, top) + dot_tn(order, mid) + dot_tn(order, low_part)
 
 
-def ready_kernel(
-    moves, side, comb, nrm_all, mix_half, z_o, mine_o, theirs_o, z_s, gated_s
-):
+def ready_kernel(moves, side, comb, mix_half, mine_o, theirs_o, gated_s):
     places = comb.shape[0]
-    width = z_o.shape[0]
-    for place in range(places):
-        z_s[:, place * 128 : (place + 1) * 128] = comb[place, :width, :]
+    width = mine_o.shape[0]
     for k in range(places // 2):
         place = 2 * k + side[0]
         gated_s[:, k * 128 : (k + 1) * 128] = comb[place, width : 3 * width, :]
@@ -1088,11 +1084,9 @@
     first = side[0] == 0
     mine_o[...] = jnp.where(first, grads[:width, :], grads[width:, :])
     theirs_o[...] = jnp.where(first, grads[width:, :], grads[:width, :])
-    moves.need(nrm_all)
-    z_o[...] = dot_nn(z_s[...], nrm_all[...]).astype(bf16)
-
-
-def grads_kernel(got, nrm_all, out_o, left_s, *, base):
+
+
+def grads_kernel(got, comb, nrm_all, out_one, out_two, out_o, left_s, *, base):
     places, width, _ = got.shape
     model = nrm_all.shape[1]
     each = model // width
@@ -1110,7 +1104,8 @@
         if place + 1 < places:
             beyond = dot_nn(got[gathered_place(place + 1), :, 256:384], placed)
             inner = (inner.astype(f32) + beyond).astype(bf16)
-        left_s[:, at * 128 : (at + 1) * 128] = inner
+        left_s[:width, at * 128 : (at + 1) * 128] = inner
+        left_s[width:, at * 128 : (at + 1) * 128] = comb[at, :width, :]
         there = got[at, :, 128:].astype(f32)
         rest = rest + there
         k = place * each // 128
@@ -1119,9 +1114,10 @@
         for part in range(2):
             turn = (inside - base - part * each) % 128
             routers[k] = routers[k] + jnp.where(mine, pltpu.roll(there[:, 128:], turn, 1), 0.0)
-    out_o[width:, :256] = rest.astype(bf16)
-    out_o[width:, 256:] = jnp.concatenate(routers, axis=1).astype(bf16)
-    out_o[:width, :model] = dot_nn(left_s[...], nrm_all[...]).astype(bf16)
+    out_o[3 * width :, :model] = (out_one[...].astype(f32) + out_two[...].astype(f32)).astype(bf16)
+    out_o[2 * width : 3 * width, :256] = rest.astype(bf16)
+    out_o[2 * width : 3 * width, 256:] = jnp.concatenate(routers, axis=1).astype(bf16)
+    out_o[: 2 * width, :model] = dot_nn(left_s[...], nrm_all[...]).astype(bf16)
 
 
 def token_order(rows):
@@ -1132,16 +1128,18 @@
 
 
 def final_kernel(
-    ours, theirs, ours_two, theirs_two, x_o, z_o, out_o, conv_o, bias_o, xp_o, dt_o, db_o, al_o, skip_o, router_o, one_o,
+    ours, theirs, x_o, z_o, out_o, conv_o, bias_o, xp_o, dt_o, db_o, al_o, skip_o, router_o, one_o,
     two_o, mine_s, other_s, *, rank, count, experts
 ):
     width = out_o.shape[0]
     model = router_o.shape[1]
     each = model // width
     x_o[...] = ours[:width, :model].astype(f32) + theirs[:width, :model].astype(f32)
-    z_o[...] = ours_two[:width, :].astype(f32) + theirs_two[:width, :].astype(f32)
-    out_o[...] = ours_two[width:, :].astype(f32) + theirs_two[width:, :].astype(f32)
-    rest = slice(width, 2 * width)
+    middle = slice(width, 2 * width)
+    z_o[...] = ours[middle, :model].astype(f32) + theirs[middle, :model].astype(f32)
+    last = slice(3 * width, 4 * width)
+    out_o[...] = ours[last, :model].astype(f32) + theirs[last, :model].astype(f32)
+    rest = slice(2 * width, 3 * width)
     xd = ours[rest, :128].astype(f32) + theirs[rest, :128].astype(f32)
     xp_o[...] = xd[:, : rank + 2 * count]
     gap = jnp.zeros((128 - width, 128), f32)
@@ -1509,16 +1507,13 @@
     )
     got_pay = exchange_channels(pay.reshape(places, width, 384))
     beyond = lax.ppermute(beyond, "wide", [(i + 1, i) for i in range(places - 1)])
-    z_ready, out_ready, out_theirs = call(
+    out_ready, out_theirs = call(
         ready_kernel,
-        [shape((width, model), bf16)] * 3,
-        [
-            pltpu.VMEM((width, places * rows), bf16),
-            pltpu.VMEM((2 * width, places // 2 * rows), bf16),
-        ],
-        (side, comb_got, normed_all, mix_half),
+        [shape((width, model), bf16)] * 2,
+        [pltpu.VMEM((2 * width, places // 2 * rows), bf16)],
+        (side, comb_got, mix_half),
         smem=1,
-        late=(3,),
+        late=(2,),
         limit=24 * 1024 * 1024,
     )
     out_other = other_chip(out_theirs)
@@ -1526,16 +1521,12 @@
     first_grad = call(
         hidden_kernel, [shape((rows, model))], [], (ngrad, beyond, hid, mgrad, gain_mix), limit=12 * 1024 * 1024
     )[0]
-    out_ready = (out_ready.astype(f32) + out_other.astype(f32)).astype(bf16)
-    ready = jnp.concatenate([z_ready, out_ready], axis=0)
-    ready = (ready.astype(f32) + other_core(ready).astype(f32)).astype(bf16)
-    ready_side = other_side(ready)
     per_place = model // width
     mats = call(
         partial(grads_kernel, base=8 + count + 2 * per_place),
-        [shape((2 * width, 256 + places * per_place), bf16)],
-        [pltpu.VMEM((width, places * rows), bf16)],
-        (got_pay, normed_all),
+        [shape((4 * width, 256 + places * per_place), bf16)],
+        [pltpu.VMEM((2 * width, places * rows), bf16)],
+        (got_pay, comb_got, normed_all, out_ready, out_other),
         limit=24 * 1024 * 1024,
     )[0]
     mats = (mats.astype(f32) + other_core(mats).astype(f32)).astype(bf16)
@@ -1557,7 +1548,7 @@
             shape((model,)),
         ],
         [pltpu.VMEM(((experts + 8) * per_place, 128), f32)] * 2,
-        (mats, other_side(mats), ready, ready_side),
+        (mats, other_side(mats)),
         limit=12 * 1024 * 1024,
     )
     return (

time: 284 us -> 285 us (level)
  waiting for transfers between devices: 64.9 us -> 70.2 us
    all_to_all x3, waiting for transfers between devices: 6.61 us -> 11.2 us  [exchange_channels(): lax.all_to_all(values, 'wide', split_axis=0, concat_axis=0, tiled=True, a...]
    unnamed x48 -> x46, local copies, waits for them, and re-layouts: 12.9 us -> 10.1 us
    ppermute x2 -> x1, waiting for transfers between devices: 4.75 us -> 5.82 us  [other_side(): return lax.ppermute(values, 'dp', [(0, 2), (2, 0), (1, 3), (3, 1)])]
    ppermute x8 -> x7, starting transfers between devices: 11.7 us -> 11.6 us  [other_core(): return lax.ppermute(values, 'dp', [(0, 1), (1, 0), (2, 3), (3, 2)])]
  transfers between devices with their start and end apart: 26 -> 24, of which waited for: 13 -> 12; matrix products, arithmetic and copies ran while one was open for 5% -> 5% of each run, Pallas kernels for 31% -> 31%
where the time goes in v3:
time: 285 us; the launch traced here: 284 us
  Pallas kernels  92.9 us (33%)
  starting transfers between devices  71.8 us (25%)
  waiting for transfers between devices  70.2 us (25%)
  between operations  14.1 us (5%)
  matrix products  12.8 us (4%)
  local copies, waits for them, and re-layouts  10.1 us (4%)
  blocking collectives  9.15 us (3%)
    pallas_call x16, Pallas kernels, call(): pl.pallas_call(staged if moving else kernel, out_shape=out_shapes, in_spe...  92.9 us
    all_to_all x3, starting transfers between devices, exchange_channels(): lax.all_to_all(values, 'wide', split_axis=0, concat_axis=0, tiled=True, a...  24 us
    all_to_all x2, waiting for transfers between devices, exchange_sides(): lax.all_to_all(values, ('dp', 'wide'), split_axis=0, concat_axis=0, tiled...  22.8 us
    dot_general x6, matrix products, dot_tn(): lax.dot_general(left, right, (((0,), (0,)), ((), ())), preferred_element_...  12.8 us
    ppermute x1, waiting for transfers between devices, body(): halo = lax.ppermute(tail, 'wide', [(i, i + 1) for i in range(places - 1)])  12.3 us
    all_to_all x2, starting transfers between devices, exchange_sides(): lax.all_to_all(values, ('dp', 'wide'), split_axis=0, concat_axis=0, tiled...  11.9 us
    ppermute x7, starting transfers between devices, other_core(): return lax.ppermute(values, 'dp', [(0, 1), (1, 0), (2, 3), (3, 2)])  11.6 us
    all_to_all x3, waiting for transfers between devices, exchange_channels(): lax.all_to_all(values, 'wide', split_axis=0, concat_axis=0, tiled=True, a...  11.2 us
  transfers between devices with their start and end apart: 24, of which 12 were waited for; matrix products, arithmetic and copies ran while one was open for 5% of the time, Pallas kernels for 31%

profile of v3, /device:TPU:1, one launch (start us, length us, event | category | flops | bytes accessed | tf_op | source)
XLA Modules:
  0.0 283.5 jit_solution(1027286856701153724)
XLA Ops:
  7.2 1.6 shard_map.331
  8.8 2.0 collective-permute-start
  10.8 2.4 shard_map.332
  14.9 8.8 %all-to-all-start = ((bf16[32,48,512]{2,1,0:T(8,128)(2,1)}), bf16[32,48,512]{2,1,0:T(8,128)(2,1)S(1)}, u32[]{:S(2)}, u32[]{:S(2)}) async-start(bf16[32,48,512]{2,1,0:T(8,128)(2,1)} %bitcast.51), calls=%async_computation | async-start | bytes 3145728 | tf_op jit(solution)/shard_map/all_to_all | solution.py:1209
  23.7 2.4 shard_map.333
  26.1 3.1 %collective-permute-start.2 = (bf16[16,768]{1,0:T(8,128)(2,1)}, bf16[16,768]{1,0:T(8,128)(2,1)S(1)}, u32[]{:S(2)}, u32[]{:S(2)}) collective-permute-start(bf16[16,768]{1,0:T(8,128)(2,1)} %get-tuple-element.116), channel_id=1, source_target_pairs={{0,1},{1,2},{2,3},{3,4},{4,5},{5,6},{6,7},{7,8},{8,9},{9,10},{10,1... | collective-permute-start | bytes 73736 | tf_op jit(solution)/shard_map/ppermute | solution.py:1304
  29.2 12.3 %collective-permute-done.2.refs_2_.refs_18_ = bf16[16,768]{1,0:T(8,128)(2,1)S(1)} collective-permute-done((bf16[16,768]{1,0:T(8,128)(2,1)}, bf16[16,768]{1,0:T(8,128)(2,1)S(1)}, u32[]{:S(2)}, u32[]{:S(2)}) %collective-permute-start.2) | collective-permute-done | bytes 24608 | tf_op jit(solution)/shard_map/ppermute | solution.py:1304
  41.5 4.0 %all-to-all-done = bf16[32,48,512]{2,1,0:T(8,128)(2,1)S(1)} async-done(((bf16[32,48,512]{2,1,0:T(8,128)(2,1)}), bf16[32,48,512]{2,1,0:T(8,128)(2,1)S(1)}, u32[]{:S(2)}, u32[]{:S(2)}) %all-to-all-start) | async-done | bytes 1572896 | tf_op jit(solution)/shard_map/all_to_all | solution.py:1209
  45.6 3.1 %collective-permute-start.3 = (bf16[1536,512]{1,0:T(8,128)(2,1)S(1)}, bf16[1536,512]{1,0:T(8,128)(2,1)S(1)}, u32[]{:S(2)}, u32[]{:S(2)}) collective-permute-start(bf16[1536,512]{1,0:T(8,128)(2,1)S(1)} %bitcast.47), channel_id=1, source_target_pairs={{0,32},{32,0},{64,96},{96,64},{1,33},{33,1},{65,97},{97,65},{2,34}... | collective-permute-start | bytes 4718600 | tf_op jit(solution)/shard_map/ppermute | solution.py:1241
  48.7 1.8 collective-permute-start.1
  52.9 12.6 %shard_map.334 = (f32[152,1536]{1,0:T(8,128)}, f32[128,1536]{1,0:T(8,128)}, f32[128,1536]{1,0:T(8,128)}, f32[128,1536]{1,0:T(8,128)}, f32[128,128]{1,0:T(8,128)}...) custom-call(s32[1]{0:T(128)} %bitcast.core.refs_0_.refs_1_, ...), custom_call_target="tpu_custom_call" | custom-call | tf_op jit(solution)/shard_map/pallas_call | solution.py:92
  65.5 3.4 %all-to-all-start.1 = ((bf16[4,16,1792]{2,1,0:T(8,128)(2,1)}), bf16[4,16,1792]{2,1,0:T(8,128)(2,1)S(1)}, u32[]{:S(2)}, u32[]{:S(2)}) async-start(bf16[4,16,1792]{2,1,0:T(8,128)(2,1)} %bitcast.59), calls=%async_computation.1 | async-start | bytes 458752 | tf_op jit(solution)/shard_map/all_to_all | solution.py:1190
  68.9 7.0 %all-to-all-done.1 = bf16[4,16,1792]{2,1,0:T(8,128)(2,1)S(1)} async-done(((bf16[4,16,1792]{2,1,0:T(8,128)(2,1)}), bf16[4,16,1792]{2,1,0:T(8,128)(2,1)S(1)}, u32[]{:S(2)}, u32[]{:S(2)}) %all-to-all-start.1) | async-done | bytes 229408 | tf_op jit(solution)/shard_map/all_to_all | solution.py:1190
  78.4 4.0 %all-to-all-start.2 = ((bf16[8,16,1792]{2,1,0:T(8,128)(2,1)}), bf16[8,16,1792]{2,1,0:T(8,128)(2,1)S(1)}, u32[]{:S(2)}, u32[]{:S(2)}) async-start(bf16[8,16,1792]{2,1,0:T(8,128)(2,1)} %bitcast.10), calls=%async_computation.2 | async-start | bytes 917504 | tf_op jit(solution)/shard_map/all_to_all | solution.py:1198
  83.3 5.2 %shard_map.336.refs_19_.refs_8_.refs_6_ = f32[128,1536]{1,0:T(8,128)} custom-call(s32[1]{0:T(128)} %bitcast.core.refs_0_.refs_1_, bf16[128,768]{1,0:T(8,128)(2,1)} %get-tuple-element.114.refs_1_, bf16[1536,768]{1,0:T(8,128)(2,1)} %all-gather.4.cloned.1.call-done.refs_2_, bf16[1536,768]{1,0:T(8,128)(2,1)} %collective-permute-done.4.refs_3_), custom_call_target="tpu_custom_call" | custom-call | tf_op jit(solution)/shard_map/pallas_call | solution.py:92
  88.5 2.7 all-to-all-done.2
  91.3 1.6 collective-permute-start.5
  93.4 11.1 %shard_map.337 = (f32[128,1536]{1,0:T(8,128)}, bf16[1024,512]{1,0:T(8,128)(2,1)}, f32[128,768]{1,0:T(8,128)}, bf16[128,768]{1,0:T(8,128)(2,1)}, f32[128,32]{1,0:...) custom-call(s32[1]{0:T(128)} %bitcast.core.refs_0_.refs_1_, ...), custom_call_target="tpu_custom_call" | custom-call | tf_op jit(solution)/shard_map/pallas_call | solution.py:92
  104.4 7.0 %all-to-all-start.3 = ((bf16[64,16,512]{2,1,0:T(8,128)(2,1)}), bf16[64,16,512]{2,1,0:T(8,128)(2,1)S(1)}, u32[]{:S(2)}, u32[]{:S(2)}) async-start(bf16[64,16,512]{2,1,0:T(8,128)(2,1)} %bitcast.57), calls=%async_computation.3 | async-start | bytes 2097152 | tf_op jit(solution)/shard_map/all_to_all | solution.py:1235
  111.5 17.9 %all-to-all-done.3 = bf16[64,16,512]{2,1,0:T(8,128)(2,1)S(1)} async-done(((bf16[64,16,512]{2,1,0:T(8,128)(2,1)}), bf16[64,16,512]{2,1,0:T(8,128)(2,1)S(1)}, u32[]{:S(2)}, u32[]{:S(2)}) %all-to-all-start.3) | async-done | bytes 1048608 | tf_op jit(solution)/shard_map/all_to_all | solution.py:1235
  130.6 9.4 %shard_map.338 = (bf16[1600,768]{1,0:T(8,128)(2,1)}, bf16[1600,768]{1,0:T(8,128)(2,1)}, bf16[1024,512]{1,0:T(8,128)(2,1)S(1)}) custom-call(bf16[1024,512]{1,0:T(8,128)(2,1)S(1)} %bitcast.35, bf16[768,768]{1,0:T(8,128)(2,1)S(1)} %bitcast.41, bf16[768,768]{1,0:T(8,128)(2,1)S(1)} %bitcast.43, bf16[768,768]{1,0:T(8,128)(2,1)S(1)} %bitcast.45, ...), custom_call_target="tpu_custom_call" | custom-call | tf_op jit(solution)/shard_map/pallas_call | solution.py:92
  141.1 1.7 collective-permute-start.8
  142.7 4.8 %all-to-all-start.4 = ((bf16[64,16,512]{2,1,0:T(8,128)(2,1)}), bf16[64,16,512]{2,1,0:T(8,128)(2,1)S(1)}, u32[]{:S(2)}, u32[]{:S(2)}) async-start(bf16[64,16,512]{2,1,0:T(8,128)(2,1)} %bitcast.46), calls=%async_computation.4 | async-start | bytes 2097152 | tf_op jit(solution)/shard_map/all_to_all | solution.py:1235
  147.9 2.0 fusion.4
  149.9 2.2 fusion.2
  152.1 2.2 add_bitcast_fusion.2
  154.3 2.2 add_bitcast_fusion.1
  156.5 2.0 fusion
  158.5 2.2 add_bitcast_fusion
  160.7 5.0 %all-to-all-done.4 = bf16[64,16,512]{2,1,0:T(8,128)(2,1)S(1)} async-done(((bf16[64,16,512]{2,1,0:T(8,128)(2,1)}), bf16[64,16,512]{2,1,0:T(8,128)(2,1)S(1)}, u32[]{:S(2)}, u32[]{:S(2)}) %all-to-all-start.4) | async-done | bytes 1048608 | tf_op jit(solution)/shard_map/all_to_all | solution.py:1235
  166.7 10.1 %shard_map.339 = (f32[128,768]{1,0:T(8,128)}, bf16[128,768]{1,0:T(8,128)(2,1)}, f32[128,768]{1,0:T(8,128)}, f32[128,1536]{1,0:T(8,128)}, f32[128,1536]{1,0:T(8,1...) custom-call(s32[1]{0:T(128)} %bitcast.core.refs_0_.refs_1_, bf16[1024,512]{1,0:T(8,128)(2,1)} %bitcast.52, ...), custom_call_target="tpu_custom_call" | custom-call | tf_op jit(solution)/shard_map/pallas_call | solution.py:92
  176.9 9.1 %all_to_all.45 = bf16[4,16,2176]{2,1,0:T(8,128)(2,1)S(1)} all-to-all(bf16[4,16,2176]{2,1,0:T(8,128)(2,1)} %bitcast.58), channel_id=1, replica_groups={{0,1,2,3},{4,5,6,7},{8,9,10,11},{12,13,14,15},{16,17,18,19},{20,21,22,2..., dimensions={0} | all-to-all | bytes 557056 | tf_op jit(solution)/shard_map/all_to_all | solution.py:1190
  187.0 3.7 %all-to-all-start.6 = ((bf16[8,16,2176]{2,1,0:T(8,128)(2,1)}), bf16[8,16,2176]{2,1,0:T(8,128)(2,1)S(1)}, u32[]{:S(2)}, u32[]{:S(2)}) async-start(bf16[8,16,2176]{2,1,0:T(8,128)(2,1)} %bitcast.25), calls=%async_computation.6 | async-start | bytes 1114112 | tf_op jit(solution)/shard_map/all_to_all | solution.py:1198
  190.7 7.2 %shard_map.340 = (bf16[128,768]{1,0:T(8,128)(2,1)}, bf16[4608,128]{1,0:T(8,128)(2,1)}, f32[1,1536]{1,0:T(1,128)}, f32[2,128,384]{2,1,0:T(8,128)}) custom-call(s32[1]{0:T(128)} %bitcast.core.refs_0_.refs_1_, s32[1]{0:T(128)} %bitcast.1.refs_1_.refs_0_, bf16[1536,768]{1,0:T(8,128)(2,1)} %all-gather.4.cloned.1.call-done.refs_2_, ...), custom_call_target="tpu_custom_call" | custom-call | tf_op jit(solution)/shard_map/pallas_call | solution.py:92
  197.9 1.4 all-to-all-done.6
  199.3 7.5 %all-to-all-start.8 = ((bf16[32,144,128]{2,1,0:T(8,128)(2,1)}), bf16[32,144,128]{2,1,0:T(8,128)(2,1)S(1)}, u32[]{:S(2)}, u32[]{:S(2)}) async-start(bf16[32,144,128]{2,1,0:T(8,128)(2,1)} %bitcast.56), calls=%async_computation.8 | async-start | bytes 2359296 | tf_op jit(solution)/shard_map/all_to_all | solution.py:1209
  206.7 22.9 %shard_map.342 = (bf16[1536,384]{1,0:T(8,128)(2,1)}, f32[128,768]{1,0:T(8,128)}, f32[8,768]{1,0:T(8,128)}) custom-call(s32[1]{0:T(128)} %bitcast.4.refs_1_.refs_0_, s32[1]{0:T(128)} %bitcast.core.refs_0_.refs_1_, bf16[1536,128]{1,0:T(8,128)(2,1)} %get-tuple-element.150.refs_2_, f32[24,1536]{1,0:T(8,128)} %get-tuple-element.124.par.refs_4_.refs_3_, ...), custom_call_target="tpu_custom_call" | custom-call | tf_op jit(solution)/shard_map/pallas_call | solution.py:92
  229.7 7.7 %all-to-all-start.7 = ((bf16[32,48,384]{2,1,0:T(8,128)(2,1)}), bf16[32,48,384]{2,1,0:T(8,128)(2,1)S(1)}, u32[]{:S(2)}, u32[]{:S(2)}) async-start(bf16[32,48,384]{2,1,0:T(8,128)(2,1)} %bitcast.55), calls=%async_computation.7 | async-start | bytes 2359296 | tf_op jit(solution)/shard_map/all_to_all | solution.py:1209
  237.5 1.9 copy-done.3
  241.4 1.3 collective-permute-start.10
  242.7 4.5 %collective-permute-done.10.beyond = f32[8,768]{1,0:T(8,128)S(1)} collective-permute-done((f32[8,768]{1,0:T(8,128)S(1)}, f32[8,768]{1,0:T(8,128)S(1)}, u32[]{:S(2)}, u32[]{:S(2)}) %collective-permute-start.10) | collective-permute-done | bytes 24608 | tf_op jit(solution)/shard_map/ppermute | solution.py:1509
  247.2 7.1 %all-to-all-done.7.got = bf16[32,48,384]{2,1,0:T(8,128)(2,1)S(1)} async-done(((bf16[32,48,384]{2,1,0:T(8,128)(2,1)}), bf16[32,48,384]{2,1,0:T(8,128)(2,1)S(1)}, u32[]{:S(2)}, u32[]{:S(2)}) %all-to-all-start.7) | async-done | bytes 1179680 | tf_op jit(solution)/shard_map/all_to_all | solution.py:1209
  254.3 2.8 copy-done
  257.1 1.3 shard_map.345
  258.4 4.0 %collective-permute-start.11 = (bf16[192,768]{1,0:T(8,128)(2,1)S(1)}, bf16[192,768]{1,0:T(8,128)(2,1)S(1)}, u32[]{:S(2)}, u32[]{:S(2)}) collective-permute-start(bf16[192,768]{1,0:T(8,128)(2,1)S(1)} %shard_map.345), channel_id=1, source_target_pairs={{0,32},{32,0},{64,96},{96,64},{1,33},{33,1},{65,97},{97,65},{2,34}... | collective-permute-start | bytes 884744 | tf_op jit(solution)/shard_map/ppermute | solution.py:1241
  263.7 3.6 %collective-permute-start.12 = (bf16[192,768]{1,0:T(8,128)(2,1)S(1)}, bf16[192,768]{1,0:T(8,128)(2,1)S(1)}, u32[]{:S(2)}, u32[]{:S(2)}) collective-permute-start(bf16[192,768]{1,0:T(8,128)(2,1)S(1)} %add_convert_fusion.ours), channel_id=1, source_target_pairs={{0,64},{64,0},{32,96},{96,32},{1,65},{65,1},{33,97},{97,33},{2,66}... | collective-permute-start | bytes 884744 | tf_op jit(solution)/shard_map/ppermute | solution.py:1245
  268.6 5.8 %collective-permute-done.12.theirs = bf16[192,768]{1,0:T(8,128)(2,1)S(1)} collective-permute-done((bf16[192,768]{1,0:T(8,128)(2,1)S(1)}, bf16[192,768]{1,0:T(8,128)(2,1)S(1)}, u32[]{:S(2)}, u32[]{:S(2)}) %collective-permute-start.12) | collective-permute-done | bytes 294944 | tf_op jit(solution)/shard_map/ppermute | solution.py:1245
  274.4 2.6 shard_map.346
  (77 shorter events, 17.1 us)
Async XLA Ops:
  7.2 68.7 %all-gather.4.cloned.1.call-start = ((), (), s32[]{:S(2)}) async-start(), calls=%async_computation.9 | async-start | bytes 2506752 | tf_op jit(solution)/shard_map/all_gather | solution.py:1227
  8.8 4.5 %collective-permute-start = (bf16[48,768]{1,0:T(8,128)(2,1)}, bf16[48,768]{1,0:T(8,128)(2,1)S(1)}, u32[]{:S(2)}, u32[]{:S(2)}) collective-permute-start(bf16[48,768]{1,0:T(8,128)(2,1)} %shard_map.331), channel_id=1, source_target_pairs={{0,4},{1,5},{2,6},{3,7},{4,0},{5,1},{6,2},{7,3},{8,12},{9,13},{10,... | collective-permute-start | bytes 221192 | tf_op jit(solution)/shard_map/ppermute | solution.py:1215
  14.9 30.7 %all-to-all-start = ((bf16[32,48,512]{2,1,0:T(8,128)(2,1)}), bf16[32,48,512]{2,1,0:T(8,128)(2,1)S(1)}, u32[]{:S(2)}, u32[]{:S(2)}) async-start(bf16[32,48,512]{2,1,0:T(8,128)(2,1)} %bitcast.51), calls=%async_computation | async-start | bytes 3145728 | tf_op jit(solution)/shard_map/all_to_all | solution.py:1209
  26.1 15.5 %collective-permute-start.2 = (bf16[16,768]{1,0:T(8,128)(2,1)}, bf16[16,768]{1,0:T(8,128)(2,1)S(1)}, u32[]{:S(2)}, u32[]{:S(2)}) collective-permute-start(bf16[16,768]{1,0:T(8,128)(2,1)} %get-tuple-element.116), channel_id=1, source_target_pairs={{0,1},{1,2},{2,3},{3,4},{4,5},{5,6},{6,7},{7,8},{8,9},{9,10},{10,1... | collective-permute-start | bytes 73736 | tf_op jit(solution)/shard_map/ppermute | solution.py:1304
  41.5 10.2 %copy-start.21 = (bf16[16,768]{1,0:T(8,128)(2,1)}, bf16[16,768]{1,0:T(8,128)(2,1)S(1)}, u32[]{:S(2)}) copy-start(bf16[16,768]{1,0:T(8,128)(2,1)S(1)} %collective-permute-done.2.refs_2_.refs_18_) | copy-start | bytes 73732
  45.6 6.1 %copy-start.14 = (bf16[32,48,512]{2,1,0:T(8,128)(2,1)}, bf16[32,48,512]{2,1,0:T(8,128)(2,1)S(1)}, u32[]{:S(2)}) copy-start(bf16[32,48,512]{2,1,0:T(8,128)(2,1)S(1)} %all-to-all-done) | copy-start | bytes 4718596
  45.6 6.1 %collective-permute-start.3 = (bf16[1536,512]{1,0:T(8,128)(2,1)S(1)}, bf16[1536,512]{1,0:T(8,128)(2,1)S(1)}, u32[]{:S(2)}, u32[]{:S(2)}) collective-permute-start(bf16[1536,512]{1,0:T(8,128)(2,1)S(1)} %bitcast.47), channel_id=1, source_target_pairs={{0,32},{32,0},{64,96},{96,64},{1,33},{33,1},{65,97},{97,65},{2,34}... | collective-permute-start | bytes 4718600 | tf_op jit(solution)/shard_map/ppermute | solution.py:1241
  48.7 20.2 %collective-permute-start.1 = (bf16[128,768]{1,0:T(8,128)(2,1)}, bf16[128,768]{1,0:T(8,128)(2,1)S(1)}, u32[]{:S(2)}, u32[]{:S(2)}) collective-permute-start(bf16[128,768]{1,0:T(8,128)(2,1)} %get-tuple-element.114.refs_1_), channel_id=1, source_target_pairs={{0,4},{1,5},{2,6},{3,7},{4,0},{5,1},{6,2},{7,3},{8,12},{9,13},{10,... | collective-permute-start | bytes 589832 | tf_op jit(solution)/shard_map/ppermute | solution.py:1215
  51.7 1.2 copy-start.15
  52.9 29.5 %copy-start.20 = (bf16[128,768]{1,0:T(8,128)(2,1)S(1)}, bf16[128,768]{1,0:T(8,128)(2,1)}, u32[]{:S(2)}) copy-start(bf16[128,768]{1,0:T(8,128)(2,1)} %get-tuple-element.114.refs_1_) | copy-start | bytes 589828
  65.5 10.4 %all-to-all-start.1 = ((bf16[4,16,1792]{2,1,0:T(8,128)(2,1)}), bf16[4,16,1792]{2,1,0:T(8,128)(2,1)S(1)}, u32[]{:S(2)}, u32[]{:S(2)}) async-start(bf16[4,16,1792]{2,1,0:T(8,128)(2,1)} %bitcast.59), calls=%async_computation.1 | async-start | bytes 458752 | tf_op jit(solution)/shard_map/all_to_all | solution.py:1190
  75.9 12.6 %copy-start.5 = (bf16[4,16,1792]{2,1,0:T(8,128)(2,1)}, bf16[4,16,1792]{2,1,0:T(8,128)(2,1)S(1)}, u32[]{:S(2)}) copy-start(bf16[4,16,1792]{2,1,0:T(8,128)(2,1)S(1)} %all-to-all-done.1) | copy-start | bytes 688132
  75.9 7.4 %collective-permute-start.4 = (bf16[1536,768]{1,0:T(8,128)(2,1)}, bf16[1536,768]{1,0:T(8,128)(2,1)}, u32[]{:S(2)}, u32[]{:S(2)}) collective-permute-start(bf16[1536,768]{1,0:T(8,128)(2,1)} %all-gather.4.cloned.1.call-done.refs_2_), channel_id=1, source_target_pairs={{0,32},{32,0},{64,96},{96,64},{1,33},{33,1},{65,97},{97,65},{2,34}... | collective-permute-start | bytes 7077896 | tf_op jit(solution)/shard_map/ppermute | solution.py:1241
  76.6 0.9 copy-start.1
  78.4 12.8 %all-to-all-start.2 = ((bf16[8,16,1792]{2,1,0:T(8,128)(2,1)}), bf16[8,16,1792]{2,1,0:T(8,128)(2,1)S(1)}, u32[]{:S(2)}, u32[]{:S(2)}) async-start(bf16[8,16,1792]{2,1,0:T(8,128)(2,1)} %bitcast.10), calls=%async_computation.2 | async-start | bytes 917504 | tf_op jit(solution)/shard_map/all_to_all | solution.py:1198
  82.4 94.5 %all-gather.6.cloned.1.call-start = ((), (), s32[]{:S(2)}) async-start(), calls=%async_computation.10 | async-start | bytes 6684672 | tf_op jit(solution)/shard_map/all_gather | solution.py:1227
  83.3 8.0 %copy-start.7 = (bf16[1,768,768]{2,1,0:T(8,128)(2,1)S(1)}, bf16[1,768,768]{2,1,0:T(8,128)(2,1)}, u32[]{:S(2)}) copy-start(bf16[1,768,768]{2,1,0:T(8,128)(2,1)} %param.37) | copy-start | bytes 3538948
  83.3 9.6 %copy-start.8 = (bf16[1,768,768]{2,1,0:T(8,128)(2,1)S(1)}, bf16[1,768,768]{2,1,0:T(8,128)(2,1)}, u32[]{:S(2)}) copy-start(bf16[1,768,768]{2,1,0:T(8,128)(2,1)} %param.38) | copy-start | bytes 3538948
  91.2 2.1 copy-start.19
  91.3 20.2 %collective-permute-start.5 = (bf16[768,768]{1,0:T(8,128)(2,1)S(1)}, bf16[768,768]{1,0:T(8,128)(2,1)}, u32[]{:S(2)}, u32[]{:S(2)}) collective-permute-start(bf16[768,768]{1,0:T(8,128)(2,1)S(1)} %bitcast.40), channel_id=1, source_target_pairs={{0,32},{32,0},{64,96},{96,64},{1,33},{33,1},{65,97},{97,65},{2,34}... | collective-permute-start | bytes 3538952 | tf_op jit(solution)/shard_map/ppermute | solution.py:1241
  92.8 18.6 %collective-permute-start.6 = (bf16[768,768]{1,0:T(8,128)(2,1)S(1)}, bf16[768,768]{1,0:T(8,128)(2,1)}, u32[]{:S(2)}, u32[]{:S(2)}) collective-permute-start(bf16[768,768]{1,0:T(8,128)(2,1)S(1)} %bitcast.42), channel_id=1, source_target_pairs={{0,32},{32,0},{64,96},{96,64},{1,33},{33,1},{65,97},{97,65},{2,34}... | collective-permute-start | bytes 3538952 | tf_op jit(solution)/shard_map/ppermute | solution.py:1241
  92.9 18.5 %collective-permute-start.7 = (bf16[768,768]{1,0:T(8,128)(2,1)}, bf16[768,768]{1,0:T(8,128)(2,1)}, u32[]{:S(2)}, u32[]{:S(2)}) collective-permute-start(bf16[768,768]{1,0:T(8,128)(2,1)} %bitcast.44), channel_id=1, source_target_pairs={{0,32},{32,0},{64,96},{96,64},{1,33},{33,1},{65,97},{97,65},{2,34}... | collective-permute-start | bytes 3538952 | tf_op jit(solution)/shard_map/ppermute | solution.py:1241
  104.4 24.9 %all-to-all-start.3 = ((bf16[64,16,512]{2,1,0:T(8,128)(2,1)}), bf16[64,16,512]{2,1,0:T(8,128)(2,1)S(1)}, u32[]{:S(2)}, u32[]{:S(2)}) async-start(bf16[64,16,512]{2,1,0:T(8,128)(2,1)} %bitcast.57), calls=%async_computation.3 | async-start | bytes 2097152 | tf_op jit(solution)/shard_map/all_to_all | solution.py:1235
  129.3 1.3 copy-start.9
  140.1 1.0 copy-start.10
  141.1 6.8 %collective-permute-start.8 = (bf16[1600,768]{1,0:T(8,128)(2,1)}, bf16[1600,768]{1,0:T(8,128)(2,1)}, u32[]{:S(2)}, u32[]{:S(2)}) collective-permute-start(bf16[1600,768]{1,0:T(8,128)(2,1)} %get-tuple-element.140), channel_id=1, source_target_pairs={{0,32},{32,0},{64,96},{96,64},{1,33},{33,1},{65,97},{97,65},{2,34}... | collective-permute-start | bytes 7372808 | tf_op jit(solution)/shard_map/ppermute | solution.py:1241
  142.7 23.0 %all-to-all-start.4 = ((bf16[64,16,512]{2,1,0:T(8,128)(2,1)}), bf16[64,16,512]{2,1,0:T(8,128)(2,1)S(1)}, u32[]{:S(2)}, u32[]{:S(2)}) async-start(bf16[64,16,512]{2,1,0:T(8,128)(2,1)} %bitcast.46), calls=%async_computation.4 | async-start | bytes 2097152 | tf_op jit(solution)/shard_map/all_to_all | solution.py:1235
  147.6 89.9 %all-gather.8.cloned.1.call-start = ((), (), s32[]{:S(2)}) async-start(), calls=%async_computation.11 | async-start | bytes 3342336 | tf_op jit(solution)/shard_map/all_gather | solution.py:1227
  149.9 2.2 copy-start.17
  165.7 1.0 copy-start.16
  166.7 19.3 %copy-start.2 = (f32[24,1536]{1,0:T(8,128)S(1)}, f32[24,1536]{1,0:T(8,128)}, u32[]{:S(2)}) copy-start(f32[24,1536]{1,0:T(8,128)} %get-tuple-element.124.par.refs_4_.refs_3_) | copy-start | bytes 442372
  186.0 11.9 %copy-start.4 = (bf16[4,16,2176]{2,1,0:T(8,128)(2,1)}, bf16[4,16,2176]{2,1,0:T(8,128)(2,1)S(1)}, u32[]{:S(2)}) copy-start(bf16[4,16,2176]{2,1,0:T(8,128)(2,1)S(1)} %all_to_all.45) | copy-start | bytes 835588
  187.0 12.3 %all-to-all-start.6 = ((bf16[8,16,2176]{2,1,0:T(8,128)(2,1)}), bf16[8,16,2176]{2,1,0:T(8,128)(2,1)S(1)}, u32[]{:S(2)}, u32[]{:S(2)}) async-start(bf16[8,16,2176]{2,1,0:T(8,128)(2,1)} %bitcast.25), calls=%async_computation.6 | async-start | bytes 1114112 | tf_op jit(solution)/shard_map/all_to_all | solution.py:1198
  199.3 7.5 %copy-start.18 = (bf16[8,16,2176]{2,1,0:T(8,128)(2,1)}, bf16[8,16,2176]{2,1,0:T(8,128)(2,1)S(1)}, u32[]{:S(2)}) copy-start(bf16[8,16,2176]{2,1,0:T(8,128)(2,1)S(1)} %all-to-all-done.6) | copy-start | bytes 1671172
  199.3 30.4 %all-to-all-start.8 = ((bf16[32,144,128]{2,1,0:T(8,128)(2,1)}), bf16[32,144,128]{2,1,0:T(8,128)(2,1)S(1)}, u32[]{:S(2)}, u32[]{:S(2)}) async-start(bf16[32,144,128]{2,1,0:T(8,128)(2,1)} %bitcast.56), calls=%async_computation.8 | async-start | bytes 2359296 | tf_op jit(solution)/shard_map/all_to_all | solution.py:1209
  229.7 24.6 %all-to-all-start.7 = ((bf16[32,48,384]{2,1,0:T(8,128)(2,1)}), bf16[32,48,384]{2,1,0:T(8,128)(2,1)S(1)}, u32[]{:S(2)}, u32[]{:S(2)}) async-start(bf16[32,48,384]{2,1,0:T(8,128)(2,1)} %bitcast.55), calls=%async_computation.7 | async-start | bytes 2359296 | tf_op jit(solution)/shard_map/all_to_all | solution.py:1209
  237.5 1.9 copy-start.3
  239.4 2.0 copy-start.22
  240.3 14.0 %collective-permute-start.9 = (bf16[48,768]{1,0:T(8,128)(2,1)S(1)}, bf16[48,768]{1,0:T(8,128)(2,1)S(1)}, u32[]{:S(2)}, u32[]{:S(2)}) collective-permute-start(bf16[48,768]{1,0:T(8,128)(2,1)S(1)} %get-tuple-element.170), channel_id=1, source_target_pairs={{0,4},{1,5},{2,6},{3,7},{4,0},{5,1},{6,2},{7,3},{8,12},{9,13},{10,... | collective-permute-start | bytes 221192 | tf_op jit(solution)/shard_map/ppermute | solution.py:1215
  241.4 5.8 %collective-permute-start.10 = (f32[8,768]{1,0:T(8,128)S(1)}, f32[8,768]{1,0:T(8,128)S(1)}, u32[]{:S(2)}, u32[]{:S(2)}) collective-permute-start(f32[8,768]{1,0:T(8,128)S(1)} %copy-done.22), channel_id=1, source_target_pairs={{1,0},{2,1},{3,2},{4,3},{5,4},{6,5},{7,6},{8,7},{9,8},{10,9},{11,1... | collective-permute-start | bytes 73736 | tf_op jit(solution)/shard_map/ppermute | solution.py:1509
  254.3 2.8 copy-start
  257.1 10.2 %copy-start.6 = (bf16[128,768]{1,0:T(8,128)(2,1)S(1)}, bf16[128,768]{1,0:T(8,128)(2,1)}, u32[]{:S(2)}) copy-start(bf16[128,768]{1,0:T(8,128)(2,1)} %get-tuple-element.133.refs_14_.refs_25_.hid) | copy-start | bytes 589828
  257.1 10.2 %copy-start.11 = (f32[128,768]{1,0:T(8,128)S(1)}, f32[128,768]{1,0:T(8,128)}, u32[]{:S(2)}) copy-start(f32[128,768]{1,0:T(8,128)} %get-tuple-element.173.mgrad) | copy-start | bytes 1179652
  257.1 10.2 %copy-start.12 = (f32[128,768]{1,0:T(8,128)S(1)}, f32[128,768]{1,0:T(8,128)}, u32[]{:S(2)}) copy-start(f32[128,768]{1,0:T(8,128)} %get-tuple-element.164.ngrad_in) | copy-start | bytes 1179652
  257.1 10.2 %copy-start.13 = (f32[768]{0:T(1024)S(1)}, f32[768]{0:T(1024)}, u32[]{:S(2)}) copy-start(f32[768]{0:T(1024)} %gain.3) | copy-start | bytes 9220
  258.4 5.2 %collective-permute-start.11 = (bf16[192,768]{1,0:T(8,128)(2,1)S(1)}, bf16[192,768]{1,0:T(8,128)(2,1)S(1)}, u32[]{:S(2)}, u32[]{:S(2)}) collective-permute-start(bf16[192,768]{1,0:T(8,128)(2,1)S(1)} %shard_map.345), channel_id=1, source_target_pairs={{0,32},{32,0},{64,96},{96,64},{1,33},{33,1},{65,97},{97,65},{2,34}... | collective-permute-start | bytes 884744 | tf_op jit(solution)/shard_map/ppermute | solution.py:1241
  263.7 10.7 %collective-permute-start.12 = (bf16[192,768]{1,0:T(8,128)(2,1)S(1)}, bf16[192,768]{1,0:T(8,128)(2,1)S(1)}, u32[]{:S(2)}, u32[]{:S(2)}) collective-permute-start(bf16[192,768]{1,0:T(8,128)(2,1)S(1)} %add_convert_fusion.ours), channel_id=1, source_target_pairs={{0,64},{64,0},{32,96},{96,32},{1,65},{65,1},{33,97},{97,33},{2,66}... | collective-permute-start | bytes 884744 | tf_op jit(solution)/shard_map/ppermute | solution.py:1245
Sparse Core Ops, SparseCore 0:
  15.0 58.6 all-gather.3
  91.4 80.4 all-gather.5
  177.0 60.3 all-gather.7
